TPU v7x, 256 devices: a whole 4x4x8 slice. The times are simulated.
256 devices in a mesh: grp: 128 (over z, y, x), sub: 2 (over core).
Axes of the slice: x: 4, y: 4, z: 8, core: 2. Of those that a mesh axis runs over, the one named last changes fastest.
Arguments:
- fine_rows: bfloat16 [131072, 192], P(('grp', 'sub')), may hold values from -6 to 6
- qkv_weight: bfloat16 [192, 576], replicated, may hold values from -0.4375 to 0.4375
- out_weight: bfloat16 [192, 192], replicated, may hold values from -0.4375 to 0.4375
- pool_weight: bfloat16 [1536, 384], replicated, may hold values from -0.15625 to 0.15625
- coarse_qkv_weight: bfloat16 [3, 384, 384], P(None, None, 'sub'), may hold values from -0.3125 to 0.3125
- coarse_out_weight: bfloat16 [384, 384], P('sub'), may hold values from -0.3125 to 0.3125
- parent_index: int32 [131072], P(('grp', 'sub')), may hold values from 0 to 32767, as said below
- child_slot: int32 [131072], P(('grp', 'sub')), may hold values from 0 to 7
- out_grad: bfloat16 [32768, 384], P(('grp', 'sub')), may hold values from -6 to 6
Outputs:
- coarse_rows: bfloat16 [32768, 384], P(('grp', 'sub'))
- row_grad: bfloat16 [131072, 192], P(('grp', 'sub'))
- grad_qkv: float32 [192, 576], replicated
- grad_out: float32 [192, 192], replicated
- grad_pool: float32 [1536, 384], replicated
- grad_coarse_qkv: float32 [3, 384, 384], P(None, None, 'sub')
- grad_coarse_out: float32 [384, 384], P('sub')
Inputs may be any that keep to these rules, and one draw needn't show every extreme that they name: parent_index never falls, the octants of one parent are consecutive, and every parent has 1 to 7 children with distinct, rising child_slot values. Parent p belongs to the device holding rows p // 128 * 512 onward: each device's rows belong to its own 128 parents, except its first 1 to 3 rows (none on the first device), which belong to the last parent of the device before it.
All inputs are finite; a program needn't handle non-finite values.
Results may differ from a plain program's by a relative error of at most 0.024.
Values may be sent and summed in bfloat16 or wider, within the bound.
No kernel may reach another device: no remote copies, remote signals or barrier semaphores. Data moves between devices by JAX's collectives and lax.ppermute only.
A program may use at most 64 MiB of HBM per device.

v0:
```python
import jax
import jax.numpy as jnp
from jax import lax
from jax.sharding import PartitionSpec as P

HD = 16
WINDOW_OCTANTS = 32
DILATION_STRIDE = 4


EPSILON = 1e-05


def passed_along(shard, axis, by):
    count = lax.axis_size(axis)
    pairs = [(i, i + by) for i in range(count) if 0 <= i + by < count]
    return lax.ppermute(shard, axis, pairs)


def bround(value):
    return value.astype(jnp.bfloat16)


def multiply(form, left, right):
    return jnp.einsum(form, left, right, preferred_element_type=jnp.float32)


def layer_norm(value):
    center = value - jnp.mean(value, -1, keepdims=True)
    inverse = lax.rsqrt(jnp.mean(center * center, -1, keepdims=True) + EPSILON)
    return (center * inverse, inverse)


def layer_norm_back(normed, inverse, upstream):
    return inverse * (
        upstream
        - jnp.mean(upstream, -1, keepdims=True)
        - normed * jnp.mean(upstream * normed, -1, keepdims=True)
    )


def split_heads(input_tensor, head_count):
    return input_tensor.reshape(
        input_tensor.shape[0],
        input_tensor.shape[1],
        head_count,
        input_tensor.shape[2] // head_count,
    )


def to_windows(input_tensor):
    block_list = input_tensor.shape[0] // (WINDOW_OCTANTS * DILATION_STRIDE)
    channel_width = input_tensor.shape[-1]
    return (
        input_tensor.reshape(block_list, WINDOW_OCTANTS, DILATION_STRIDE, channel_width)
        .transpose(0, 2, 1, 3)
        .reshape(block_list * DILATION_STRIDE, WINDOW_OCTANTS, channel_width)
    )


def from_windows(input_tensor):
    channel_width = input_tensor.shape[-1]
    block_list = input_tensor.shape[0] // DILATION_STRIDE
    return (
        input_tensor.reshape(block_list, DILATION_STRIDE, WINDOW_OCTANTS, channel_width)
        .transpose(0, 2, 1, 3)
        .reshape(block_list * WINDOW_OCTANTS * DILATION_STRIDE, channel_width)
    )


def attention_probs(query_heads, key_heads, query_form, key_form):
    scaling = query_heads.shape[-1] ** (-0.5)
    exponent = jnp.exp(
        multiply(query_form + "," + key_form + "->whjk", query_heads, key_heads) * scaling
    )
    return exponent / jnp.sum(exponent, -1, keepdims=True)


def attend(queries, key_rows, values, head_count, layout):
    query_form = layout + "hd"
    key_form = query_form.replace("j", "k")
    query_heads = split_heads(queries, head_count)
    key_heads = split_heads(key_rows, head_count)
    value_heads = split_heads(values, head_count)
    attn_prob = attention_probs(query_heads, key_heads, query_form, key_form)
    mixed = multiply("whjk," + key_form + "->" + query_form, bround(attn_prob), value_heads)
    return bround(mixed).reshape(queries.shape)


def attend_back(queries, key_rows, values, upstream, head_count, layout):
    query_form = layout + "hd"
    key_form = query_form.replace("j", "k")
    query_heads = split_heads(queries, head_count)
    key_heads = split_heads(key_rows, head_count)
    value_heads = split_heads(values, head_count)
    scaling = query_heads.shape[-1] ** (-0.5)
    attn_prob = attention_probs(query_heads, key_heads, query_form, key_form)
    up_heads = split_heads(upstream, head_count)
    grad_values = multiply("whjk," + query_form + "->" + key_form, bround(attn_prob), up_heads)
    grad_prob = multiply(query_form + "," + key_form + "->whjk", up_heads, value_heads)
    grad_score = bround(
        attn_prob * (grad_prob - jnp.sum(attn_prob * grad_prob, -1, keepdims=True)) * scaling
    )
    grad_query = multiply("whjk," + key_form + "->" + query_form, grad_score, key_heads)
    grad_keys = multiply("whjk," + query_form + "->" + key_form, grad_score, query_heads)
    row_dimensions = queries.shape
    return (
        bround(grad_query).reshape(row_dimensions),
        bround(grad_keys).reshape(row_dimensions),
        bround(grad_values).reshape(row_dimensions),
    )


def pair_rows(padded, owned_count, row_count):
    first_rows = padded[:row_count].reshape((owned_count, 4) + padded.shape[1:])
    later_rows = padded[4 : row_count + 4].reshape((owned_count, 4) + padded.shape[1:])
    return jnp.concatenate([first_rows, later_rows], 1)


def coarse_window(input_tensor, channel_width):
    return input_tensor.reshape(-1, WINDOW_OCTANTS, channel_width)


def on_device(
    fine_rows,
    qkv_weight,
    out_weight,
    pool_weight,
    coarse_qkv_weight,
    coarse_out_weight,
    parent_index,
    child_slot,
    out_grad,
):
    sub_count = lax.axis_size("sub")
    grp_count = lax.axis_size("grp")
    row_count = fine_rows.shape[0]
    channels = fine_rows.shape[1]
    fine_heads = channels // HD
    owned_count = out_grad.shape[0]
    coarse_part = coarse_out_weight.shape[0]
    device = lax.axis_index("grp") * sub_count + lax.axis_index("sub")
    first_parent = device * owned_count
    fine_scale = (row_count * grp_count * sub_count) ** (-0.5)
    coarse_scale = (owned_count * grp_count * sub_count) ** (-0.5)
    rows_float = fine_rows.astype(jnp.float32)
    normed, inverse = layer_norm(rows_float)
    attn_input = bround(normed)
    qkv = bround(jnp.dot(attn_input, qkv_weight, preferred_element_type=jnp.float32))
    qkv_window = to_windows(qkv)
    mixed = from_windows(
        attend(
            qkv_window[..., :channels],
            qkv_window[..., channels : 2 * channels],
            qkv_window[..., 2 * channels :],
            fine_heads,
            "wj",
        )
    )
    hidden = bround(rows_float + jnp.dot(mixed, out_weight, preferred_element_type=jnp.float32))
    padded_hidden = jnp.concatenate([hidden, jnp.zeros((4, channels), jnp.bfloat16)], 0)
    padded_parent = jnp.concatenate([parent_index, jnp.full((4,), -1, jnp.int32)], 0)
    padded_slot = jnp.concatenate([child_slot, jnp.zeros((4,), jnp.int32)], 0)
    paired_hidden = pair_rows(padded_hidden, owned_count, row_count)
    paired_parent = pair_rows(padded_parent, owned_count, row_count)
    paired_slot = pair_rows(padded_slot, owned_count, row_count)
    own_parent = first_parent + jnp.arange(owned_count, dtype=jnp.int32)
    slot_range = jnp.arange(8, dtype=jnp.int32)
    match_mask = (
        (paired_parent == own_parent[:, None])[:, :, None] & (paired_slot[:, :, None] == slot_range)
    ).astype(jnp.bfloat16)
    local_pooled = bround(
        jnp.einsum("kjs,kjc->ksc", match_mask, paired_hidden, preferred_element_type=jnp.float32)
    )
    head_match = (
        (parent_index[:4] == first_parent - 1)[:, None] & (child_slot[:4, None] == slot_range)
    ).astype(jnp.bfloat16)
    spill_row = bround(
        jnp.einsum("js,jc->sc", head_match, hidden[:4], preferred_element_type=jnp.float32)
    )
    spill_in = passed_along(spill_row, ("grp", "sub"), -1)
    pooled = jnp.concatenate(
        [local_pooled[: owned_count - 1], local_pooled[owned_count - 1 :] + spill_in[None]], 0
    )
    pooled_flat = pooled.reshape(owned_count, 8 * channels)
    parents = bround(jnp.dot(pooled_flat, pool_weight, preferred_element_type=jnp.float32))
    part_heads = coarse_part // HD
    group_rows = lax.all_gather(parents, "sub", axis=0, tiled=True)
    coarse_normed, coarse_inverse = layer_norm(group_rows.astype(jnp.float32))
    coarse_input = bround(coarse_normed)
    coarse_qkv = bround(
        jnp.einsum(
            "pc,icd->ipd", coarse_input, coarse_qkv_weight, preferred_element_type=jnp.float32
        )
    )
    coarse_mixed = attend(
        coarse_window(coarse_qkv[0], coarse_part),
        coarse_window(coarse_qkv[1], coarse_part),
        coarse_window(coarse_qkv[2], coarse_part),
        part_heads,
        "wj",
    ).reshape(-1, coarse_part)
    summed = lax.psum_scatter(
        jnp.dot(coarse_mixed, coarse_out_weight, preferred_element_type=jnp.float32).astype(
            jnp.bfloat16
        ),
        "sub",
        scatter_dimension=0,
        tiled=True,
    ).astype(jnp.float32)
    coarse_rows = bround(parents.astype(jnp.float32) + summed)
    group_grad = lax.all_gather(out_grad, "sub", axis=0, tiled=True)
    grad_cout_part = jnp.dot(coarse_mixed.T, group_grad, preferred_element_type=jnp.float32)
    grad_cmixed = bround(
        jnp.dot(group_grad, coarse_out_weight.T, preferred_element_type=jnp.float32)
    )
    grad_cq, grad_ck, grad_cv = attend_back(
        coarse_window(coarse_qkv[0], coarse_part),
        coarse_window(coarse_qkv[1], coarse_part),
        coarse_window(coarse_qkv[2], coarse_part),
        coarse_window(grad_cmixed, coarse_part),
        part_heads,
        "wj",
    )
    grad_cqkv = jnp.stack(
        [
            grad_cq.reshape(-1, coarse_part),
            grad_ck.reshape(-1, coarse_part),
            grad_cv.reshape(-1, coarse_part),
        ],
        0,
    )
    grad_cqkv_part = jnp.einsum(
        "pc,ipd->icd", coarse_input, grad_cqkv, preferred_element_type=jnp.float32
    )
    grad_cnormed = jnp.einsum(
        "ipd,icd->pc", grad_cqkv, coarse_qkv_weight, preferred_element_type=jnp.float32
    )
    norm_grad = lax.psum_scatter(
        layer_norm_back(coarse_normed, coarse_inverse, grad_cnormed).astype(jnp.bfloat16),
        "sub",
        scatter_dimension=0,
        tiled=True,
    ).astype(jnp.float32)
    parent_gradient = bround(out_grad.astype(jnp.float32) + norm_grad)
    grad_pool_part = jnp.dot(pooled_flat.T, parent_gradient, preferred_element_type=jnp.float32)
    grad_pooled = bround(
        jnp.dot(parent_gradient, pool_weight.T, preferred_element_type=jnp.float32)
    )
    grad_pooled = grad_pooled.reshape(owned_count, 8, channels)
    spill_grad = passed_along(grad_pooled[owned_count - 1], ("grp", "sub"), 1)
    grad_paired = jnp.einsum(
        "kjs,ksc->kjc", match_mask, grad_pooled, preferred_element_type=jnp.float32
    )
    first_half = grad_paired[:, :4].reshape(row_count, channels)
    second_half = grad_paired[:, 4:].reshape(row_count, channels)
    straddle_rows = jnp.einsum(
        "js,sc->jc", head_match, spill_grad, preferred_element_type=jnp.float32
    )
    lead_rows = jnp.concatenate(
        [straddle_rows, jnp.zeros((row_count - 4, channels), jnp.float32)], 0
    )
    later_rows = jnp.concatenate(
        [jnp.zeros((4, channels), jnp.float32), second_half[: row_count - 4]], 0
    )
    grad_hidden = bround(first_half + lead_rows + later_rows)
    grad_out_part = jnp.dot(mixed.T, grad_hidden, preferred_element_type=jnp.float32)
    grad_mixed = bround(jnp.dot(grad_hidden, out_weight.T, preferred_element_type=jnp.float32))
    grad_query, grad_keys, grad_values = attend_back(
        qkv_window[..., :channels],
        qkv_window[..., channels : 2 * channels],
        qkv_window[..., 2 * channels :],
        to_windows(grad_mixed),
        fine_heads,
        "wj",
    )
    grad_qkv_rows = from_windows(jnp.concatenate([grad_query, grad_keys, grad_values], -1))
    grad_qkv_part = jnp.dot(attn_input.T, grad_qkv_rows, preferred_element_type=jnp.float32)
    grad_normed = jnp.dot(grad_qkv_rows, qkv_weight.T, preferred_element_type=jnp.float32)
    row_grad = bround(
        grad_hidden.astype(jnp.float32) + layer_norm_back(normed, inverse, grad_normed)
    )
    grad_qkv, grad_out, grad_pool = lax.psum(
        (grad_qkv_part, grad_out_part, grad_pool_part), ("grp", "sub")
    )
    grad_coarse_qkv, grad_coarse_out = lax.psum((grad_cqkv_part, grad_cout_part), "grp")
    return (
        coarse_rows,
        row_grad,
        grad_qkv * fine_scale,
        grad_out * fine_scale,
        grad_pool * coarse_scale,
        grad_coarse_qkv * coarse_scale,
        grad_coarse_out * coarse_scale,
    )


def solution(mesh):
    in_specs = (
        P(("grp", "sub"), None),
        P(),
        P(),
        P(),
        P(None, None, "sub"),
        P("sub", None),
        P(("grp", "sub")),
        P(("grp", "sub")),
        P(("grp", "sub"), None),
    )
    out_specs = (
        P(("grp", "sub"), None),
        P(("grp", "sub"), None),
        P(),
        P(),
        P(),
        P(None, None, "sub"),
        P("sub", None),
    )
    return jax.shard_map(
        on_device, mesh=mesh, in_specs=in_specs, out_specs=out_specs, check_vma=False
    )
```

profile of v0, /device:TPU:1, one launch (start us, length us, event | category | flops | bytes accessed | tf_op | source)
XLA Modules:
  0.0 580.2 jit_solution(16776484635085999424)
XLA Ops:
  8.1 1.1 convert_reduce_fusion
  9.1 1.0 fusion.73
  10.1 1.4 convolution_convert_fusion.3
  12.3 1.2 copy.169
  14.3 1.0 fusion.4
  18.1 5.2 collective-permute-start
  24.9 1.9 all_gather.7
  28.2 1.0 reshape_reshape.14
  30.9 2.1 all_gather.6
  35.9 1.8 fusion.46
  37.7 2.6 fusion.82
  40.3 3.3 fusion.39
  43.6 3.3 fusion.36
  46.9 2.3 fusion.43
  49.2 1.0 copy.187
  50.2 1.9 stack_reshape_reshape.9
  52.2 1.5 constant_dynamic-update-slice_fusion.2
  53.7 2.0 copy.190
  55.7 1.9 stack_reshape_reshape.10
  57.6 2.0 copy.193
  59.6 1.9 stack_reshape_reshape.11
  61.6 1.5 constant_dynamic-update-slice_fusion.1
  63.1 1.5 constant_dynamic-update-slice_fusion
  64.7 1.6 fusion.128
  68.2 1.8 convolution_convert_fusion.8
  70.1 1.8 fusion.137
  72.0 1.3 convolution_bitcast_fusion
  73.4 8.6 %reduce-scatter.5.cloned.1.call-done = bf16[128,384]{1,0:T(8,128)(2,1)} async-done(((bf16[256,384]{1,0:T(8,128)(2,1)}), bf16[128,384]{1,0:T(8,128)(2,1)}) %reduce-scatter.5.cloned.1.call-update) | async-done | bytes 98320 | tf_op jit(solution)/shard_map/reduce_scatter | solution.py:239
  82.0 1.5 convolution_convert_fusion
  84.3 3.1 collective-permute-start.1
  87.4 1.9 fusion.99
  92.2 4.0 convolution_convert_fusion.1
  96.2 2.4 fusion.135
  98.6 1.5 copy.206
  100.1 7.5 %fusion.27 = bf16[16,12,16,32]{3,2,1,0:T(8,128)(2,1)} fusion(bf16[16,32,12,16]{1,3,2,0:T(8,128)(2,1)S(1)} %bitcast.111, f32[16,12,32,32]{2,3,1,0:T(8,128)} %fusion.135, f32[16,12,32,32]{2,3,1,0:T(8,128)} %copy-done.4, f32[16,12,32]{2,1,0:T(8,128)S(1)} %copy-done.27), kind=kOutput, calls=%fused_computation.20 | convolution fusion | flops 8165407 | bytes 1990656 | tf_op jit(solution)/shard_map/whjk,wjhd->wkhd/dot_general | solution.py:25
  107.6 2.2 copy.205
  109.8 7.3 %fusion.24 = bf16[16,12,16,32]{3,2,1,0:T(8,128)(2,1)} fusion(bf16[16,32,12,16]{1,3,2,0:T(8,128)(2,1)S(1)} %bitcast.109, f32[16,12,32,32]{2,3,1,0:T(8,128)} %fusion.135, f32[16,12,32,32]{2,3,1,0:T(8,128)} %copy-done.4, f32[16,12,32]{2,1,0:T(8,128)S(1)} %copy-done.27), kind=kOutput, calls=%fused_computation.19 | convolution fusion | flops 8165407 | bytes 1990656 | tf_op jit(solution)/shard_map/whjk,wkhd->wjhd/dot_general | solution.py:25
  117.1 1.5 copy.204
  118.6 1.5 maximum_bitcast_fusion
  121.4 1.1 fusion.95
  122.6 1.6 add_convert_fusion.2
  125.4 168.8 %all-reduce.12.cloned.1.call-done = (f32[3,384,192]{1,2,0:T(8,128)}, f32[192,384]{1,0:T(8,128)}) async-done(((f32[3,384,192]{1,2,0:T(8,128)}, f32[192,384]{1,0:T(8,128)}), (f32[3,384,192]{1,2,0:T(8,128)}, f32[192,384]{1,0:T(8,128)})) %all-reduce.12.cloned.1.call-update) | async-done | bytes 1179664 | tf_op jit(solution)/shard_map/psum | solution.py:286
  294.1 1.7 broadcast_multiply_fusion.3
  295.8 2.2 broadcast_multiply_fusion.1
  298.0 268.0 %all-reduce.10.cloned.1.call-done = (f32[192,576]{1,0:T(8,128)}, f32[192,192]{1,0:T(8,128)}, f32[1536,384]{1,0:T(8,128)}) async-done(((f32[192,576]{1,0:T(8,128)}, f32[192,192]{1,0:T(8,128)}, f32[1536,384]{1,0:T(8,128)}), (f32[192,576]{1,0:T(8,128)}, f32[192,192]{1,0:T(8,128)}, f32[1536,384]{1,0:T(8,128)})) %all-reduce.10.cloned.1.call-update) | async-done | bytes 2949136 | tf_op jit(solution)/shard_map/psum | solution.py:283
  566.0 1.9 broadcast_multiply_fusion.2
  567.9 1.6 broadcast_multiply_fusion.4
  569.5 3.3 broadcast_multiply_fusion
  (164 shorter events, 19.6 us)
Async XLA Ops:
  8.0 22.5 %copy-start = (bf16[1536,384]{1,0:T(8,128)(2,1)S(1)}, bf16[1536,384]{1,0:T(8,128)(2,1)}, u32[]{:S(2)}) copy-start(bf16[1536,384]{1,0:T(8,128)(2,1)} %param.12) | copy-start | bytes 3538948
  8.0 74.0 %reduce-scatter.5.cloned.1.call-start = ((), (), s32[]{:S(2)}) async-start(), calls=%async_computation.3 | async-start | bytes 294912 | tf_op jit(solution)/shard_map/reduce_scatter | solution.py:239
  13.8 1.5 copy-start.7
  14.2 1.1 copy-start.5
  14.2 1.4 copy-start.9
  15.3 1.7 copy-start.4
  15.3 1.7 copy-start.26
  15.7 1.9 copy-start.32
  15.7 1.9 copy-start.1
  15.7 1.9 copy-start.23
  15.7 2.2 copy-start.33
  17.4 7.5 %copy-start.14 = (bf16[128,384]{1,0:T(8,128)(2,1)S(1)}, bf16[128,384]{1,0:T(8,128)(2,1)}, u32[]{:S(2)}) copy-start(bf16[128,384]{1,0:T(8,128)(2,1)} %param.17) | copy-start | bytes 294916
  17.6 10.3 %copy-start.11 = (bf16[512,192]{1,0:T(8,128)(2,1)}, bf16[512,192]{1,0:T(8,128)(2,1)S(1)}, u32[]{:S(2)}) copy-start(bf16[512,192]{1,0:T(8,128)(2,1)S(1)} %reshape.183) | copy-start | bytes 589828
  17.6 5.7 copy-start.36
  17.9 10.0 %copy-start.34 = (pred[4]{0:T(512)(128)(4,1)}, pred[4]{0:T(512)(128)(4,1)S(1)}, u32[]{:S(2)}) copy-start(pred[4]{0:T(512)(128)(4,1)S(1)} %slice_compare_fusion) | copy-start | bytes 16
  18.1 11.0 %collective-permute-start = (bf16[8,192]{1,0:T(8,128)(2,1)S(1)}, bf16[8,192]{1,0:T(8,128)(2,1)S(1)}, u32[]{:S(2)}, u32[]{:S(2)}) collective-permute-start(bf16[8,192]{1,0:T(8,128)(2,1)S(1)} %convolution_convert_fusion.11), channel_id=1, source_target_pairs={{1,0},{2,1},{3,2},{4,3},{5,4},{6,5},{7,6},{8,7},{9,8},{10,9},{11,1... | collective-permute-start | bytes 9224 | tf_op jit(solution)/shard_map/ppermute | solution.py:17
  23.5 4.4 copy-start.18
  24.9 3.3 copy-start.30
  26.8 1.3 copy-start.13
  26.9 1.3 copy-start.28
  28.2 5.2 copy-start.20
  29.7 0.7 copy-start.2
  30.9 2.5 copy-start.16
  46.9 2.3 copy-start.22
  67.2 55.3 %reduce-scatter.3.cloned.1.call-start = ((), (), s32[]{:S(2)}) async-start(), calls=%async_computation.2 | async-start | bytes 294912 | tf_op jit(solution)/shard_map/reduce_scatter | solution.py:203
  67.6 4.3 copy-start.19
  67.6 14.4 %copy-start.15 = (bf16[128,384]{1,0:T(8,128)(2,1)S(1)}, bf16[128,384]{1,0:T(8,128)(2,1)}, u32[]{:S(2)}) copy-start(bf16[128,384]{1,0:T(8,128)(2,1)} %param.17) | copy-start | bytes 294916
  70.0 224.1 %all-reduce.12.cloned.1.call-start = ((), (), s32[]{:S(2)}) async-start(), calls=%async_computation.5 | async-start | bytes 2359296 | tf_op jit(solution)/shard_map/psum | solution.py:286
  73.3 14.1 %copy-start.3 = (bf16[128,8,192]{0,2,1:T(8,128)(2,1)S(1)}, bf16[128,8,192]{0,2,1:T(8,128)(2,1)}, u32[]{:S(2)}) copy-start(bf16[128,8,192]{0,2,1:T(8,128)(2,1)} %copy-done.2) | copy-start | bytes 1179652
  73.3 492.7 %all-reduce.10.cloned.1.call-start = ((), (), s32[]{:S(2)}) async-start(), calls=%async_computation.4 | async-start | bytes 6094848 | tf_op jit(solution)/shard_map/psum | solution.py:283
  82.0 5.4 copy-start.21
  83.5 5.8 copy-start.29
  83.5 5.8 copy-start.31
  84.3 6.7 %collective-permute-start.1 = (bf16[8,192]{1,0:T(8,128)(2,1)S(1)}, bf16[8,192]{1,0:T(8,128)(2,1)S(1)}, u32[]{:S(2)}, u32[]{:S(2)}) collective-permute-start(bf16[8,192]{1,0:T(8,128)(2,1)S(1)} %squeeze.3), channel_id=1, source_target_pairs={{0,1},{1,2},{2,3},{3,4},{4,5},{5,6},{6,7},{7,8},{8,9},{9,10},{10,1... | collective-permute-start | bytes 9224 | tf_op jit(solution)/shard_map/ppermute | solution.py:17
  90.1 0.9 copy-start.35
  90.1 0.9 copy-start.37
  90.1 1.2 copy-start.24
  92.2 4.0 copy-start.10
  96.2 3.9 copy-start.8
  96.2 3.9 copy-start.27
  100.1 9.7 %copy-start.6 = (bf16[16,32,192]{1,2,0:T(8,128)(2,1)S(1)}, bf16[16,32,192]{1,2,0:T(8,128)(2,1)}, u32[]{:S(2)}) copy-start(bf16[16,32,192]{1,2,0:T(8,128)(2,1)} %copy-done.5) | copy-start | bytes 589828
  117.1 3.4 copy-start.12
  121.4 1.2 copy-start.17
  121.4 2.7 copy-start.25
Sparse Core Ops, SparseCore 0:
  67.3 14.6 reduce-scatter.4
  85.1 14.1 reduce-scatter.2
Sparse Core Ops, SparseCore 1:
  76.6 217.4 all-reduce.11
  300.5 265.5 all-reduce.9
where the time goes:
time: 582 us; the launch traced here: 580 us
  waiting for transfers between devices  446 us (77%)
  matrix products  53.8 us (9%)
  local copies, waits for them, and re-layouts  33.7 us (6%)
  other arithmetic  18.2 us (3%)
  between operations  16.4 us (3%)
  starting transfers between devices  8.45 us (1%)
    psum x1, waiting for transfers between devices, on_device(): lax.psum((grad_qkv_part, grad_out_part, grad_pool_part), ('grp', 'sub'))  268 us
    psum x1, waiting for transfers between devices, on_device(): lax.psum((grad_cqkv_part, grad_cout_part), 'grp')  169 us
    dot_general x11, matrix products, multiply(): return jnp.einsum(form, left, right, preferred_element_type=jnp.float32)  34.7 us
  transfers between devices with their start and end apart: 6, of which 3 were waited for; matrix products, arithmetic and copies ran while one was open for 9% of the time, Pallas kernels for 0%

commit v1 on v0

v1 whole, which is shorter than its diff:
```python
import functools

import jax
import jax.numpy as jnp
from jax import lax
from jax.experimental import pallas as pl
from jax.experimental.pallas import tpu as pltpu
from jax.sharding import Mesh, PartitionSpec as P

HD = 16
WINDOW_OCTANTS = 32
DILATION_STRIDE = 4
SLOTS = 8
LANES = 128
SPILL = 16
EPSILON = 1e-05
AXES = ("z", "y", "x", "sub")
VMEM_BYTES = 48 * 1024 * 1024
FAR = -1e30


def passed_along(shard, by):
    count = 1
    for name in AXES:
        count *= lax.axis_size(name)
    pairs = [(i, i + by) for i in range(count) if 0 <= i + by < count]
    return lax.ppermute(shard, AXES, pairs)


def swap_cores(shard):
    return lax.ppermute(shard, "sub", [(0, 1), (1, 0)])


def bround(value):
    return value.astype(jnp.bfloat16)


def product(left, right, left_dim, right_dim):
    return lax.dot_general(
        left, right, (((left_dim,), (right_dim,)), ((), ())), preferred_element_type=jnp.float32
    )


def nn(left, right):
    return product(left, right, 1, 0)


def nt(left, right):
    return product(left, right, 1, 1)


def tn(left, right):
    return product(left, right, 0, 0)


def indicator(condition):
    return bround(jnp.where(condition, 1.0, 0.0))


def layer_norm(value):
    center = value - jnp.mean(value, 0, keepdims=True)
    inverse = lax.rsqrt(jnp.mean(center * center, 0, keepdims=True) + EPSILON)
    return (center * inverse, inverse)


def layer_norm_back(normed, inverse, upstream):
    return inverse * (
        upstream
        - jnp.mean(upstream, 0, keepdims=True)
        - normed * jnp.mean(upstream * normed, 0, keepdims=True)
    )


def window_bias(same_window):
    key = lax.broadcasted_iota(jnp.int32, (LANES, LANES), 0)
    query = lax.broadcasted_iota(jnp.int32, (LANES, LANES), 1)
    return jnp.where(same_window(key) == same_window(query), 0.0, FAR)


def attention_probs(query, key, bias):
    score = tn(key, query * jnp.bfloat16(HD**-0.5)) + bias
    exponent = jnp.exp(score - jnp.max(score, 0, keepdims=True))
    return exponent * (1.0 / jnp.sum(exponent, 0, keepdims=True))


def attend_back(query, key, value, prob, upstream):
    grad_prob = tn(value, upstream * jnp.bfloat16(HD**-0.5))
    grad_score = bround(prob * (grad_prob - jnp.sum(prob * grad_prob, 0, keepdims=True)))
    grad_value = nt(upstream, bround(prob))
    grad_query = nn(key, grad_score)
    grad_key = nt(query, grad_score)
    return (bround(grad_query), bround(grad_key), bround(grad_value))


def fine_forward(
    rows, qkv_weight, out_weight, codes, hidden, mixed, qkv, probs, spill
):
    channels = rows.shape[1]
    rows_float = rows[...].astype(jnp.float32).T
    normed, _ = layer_norm(rows_float)
    qkv[...] = bround(tn(qkv_weight[...], bround(normed)))
    bias = window_bias(lambda at: at % DILATION_STRIDE)
    heads = channels // HD
    for block in range(rows.shape[0] // LANES):
        lanes = slice(block * LANES, (block + 1) * LANES)
        for head in range(heads):
            at = head * HD
            query = qkv[at : at + HD, lanes]
            key = qkv[channels + at : channels + at + HD, lanes]
            value = qkv[2 * channels + at : 2 * channels + at + HD, lanes]
            prob = bround(attention_probs(query, key, bias))
            probs[block * heads + head] = prob
            mixed[at : at + HD, lanes] = bround(nn(value, prob))
    total = bround(rows_float + tn(out_weight[...], mixed[...]))
    hidden[...] = total
    slot = lax.broadcasted_iota(jnp.int32, (SPILL, LANES), 0)
    leading = indicator(codes[:, :LANES] == slot - SLOTS)
    spill[...] = bround(nt(leading, total[:, :LANES]))


def coarse_both(
    core_ref,
    hidden,
    codes,
    spill,
    pool_weight,
    own_qkv,
    other_qkv,
    own_out,
    other_out,
    out_grad,
    coarse_rows,
    grad_hidden,
    spill_grad,
    keep,
    give,
    pooled,
    mixed,
    grads,
):
    core = core_ref[0]
    owned, wide = out_grad.shape
    channels, row_count = hidden.shape
    part = own_out.shape[0]
    parent = lax.broadcasted_iota(jnp.int32, (owned, row_count), 0)
    slot_of = codes[...] - parent * SLOTS
    spill_slot = lax.broadcasted_iota(jnp.int32, (SPILL, owned), 0)
    last = lax.broadcasted_iota(jnp.int32, (SPILL, owned), 1) == owned - 1
    total = jnp.zeros((owned, wide), jnp.float32)
    for slot in range(SLOTS):
        edge = indicator(last & (spill_slot == slot))
        children = nt(hidden[...], indicator(slot_of == slot)) + tn(spill[...], edge)
        pooled[slot] = bround(children)
        total += tn(bround(children), pool_weight[slot * channels : (slot + 1) * channels])
    parents = bround(total).astype(jnp.float32)
    normed, inverse = layer_norm(parents.T)
    coarse_input = bround(normed)
    upstream = out_grad[...]
    bias = window_bias(lambda at: at // WINDOW_OCTANTS)
    weights = ((own_qkv, own_out), (other_qkv, other_out))
    grad_normed = jnp.zeros((wide, owned), jnp.float32)
    summed = jnp.zeros((owned, wide), jnp.float32)
    for half, (qkv_weight, out_weight) in enumerate(weights):
        queries, keys, values = (
            bround(tn(qkv_weight[which], coarse_input)) for which in range(3)
        )
        grad_mixed = bround(nt(out_weight[...], upstream))
        for head in range(part // HD):
            at = slice(head * HD, (head + 1) * HD)
            prob = attention_probs(queries[at], keys[at], bias)
            mixed[at] = bround(nn(values[at], bround(prob)))
            back = attend_back(queries[at], keys[at], values[at], prob, grad_mixed[at])
            for which in range(3):
                start = which * part + head * HD
                grads[start : start + HD] = back[which]
        summed += tn(mixed[...], out_weight[...])
        for which in range(3):
            grad_normed += nn(qkv_weight[which], grads[which * part : (which + 1) * part])
        target = give if half else keep
        grad_qkv = bround(nt(coarse_input, grads[...]))
        whole = 3 * part // LANES
        for panel in range(whole):
            target[panel * wide : (panel + 1) * wide] = grad_qkv[
                :, panel * LANES : (panel + 1) * LANES
            ]
        tail = grad_qkv[:, whole * LANES :]
        base = whole * wide
        target[base : base + part] = jnp.concatenate([tail[:part], tail[part:]], 1)
        base += part
        grad_out = bround(nn(mixed[...], upstream))
        for panel in range(wide // LANES):
            target[base + panel * part : base + (panel + 1) * part] = grad_out[
                :, panel * LANES : (panel + 1) * LANES
            ]
    coarse_rows[...] = bround(parents + summed)
    grad_parents = bround(
        upstream.astype(jnp.float32).T + layer_norm_back(normed, inverse, grad_normed)
    )
    base = 4 * part * wide // LANES
    panels = wide // LANES
    for target, first in ((keep, core), (give, 1 - core)):
        for step in range(SLOTS // 2):
            grad_pool = bround(nt(pooled[first * (SLOTS // 2) + step], grad_parents))
            for panel in range(panels):
                start = base + (step * panels + panel) * channels
                target[start : start + channels] = grad_pool[
                    :, panel * LANES : (panel + 1) * LANES
                ]
    grad_total = jnp.zeros((channels, row_count), jnp.float32)
    edge_total = jnp.zeros((SPILL, channels), jnp.float32)
    for slot in range(SLOTS):
        weight = pool_weight[slot * channels : (slot + 1) * channels]
        grad_pooled = bround(nn(weight, grad_parents))
        grad_total += nn(grad_pooled, indicator(slot_of == slot))
        edge_total += nt(indicator(last & (spill_slot == slot)), grad_pooled)
    grad_hidden[...] = bround(grad_total)
    spill_grad[...] = bround(edge_total)


def fine_back(
    core_ref,
    rows,
    grad_hidden,
    spill_grad,
    codes,
    probs,
    qkv,
    mixed,
    qkv_weight,
    out_weight,
    row_grad,
    keep,
    give,
    upstream,
    grads,
):
    core = core_ref[0]
    row_count, channels = rows.shape
    normed, inverse = layer_norm(rows[...].astype(jnp.float32).T)
    slot = lax.broadcasted_iota(jnp.int32, (SPILL, LANES), 0)
    leading = indicator(codes[:, :LANES] == slot - SLOTS)
    upstream[...] = grad_hidden[...]
    upstream[:, :LANES] = bround(
        grad_hidden[:, :LANES].astype(jnp.float32) + tn(spill_grad[...], leading)
    )
    grad_mixed = bround(nn(out_weight[...], upstream[...]))
    heads = channels // HD
    for block in range(row_count // LANES):
        lanes = slice(block * LANES, (block + 1) * LANES)
        for head in range(heads):
            at = [which * channels + head * HD for which in range(3)]
            query, key, value = (qkv[start : start + HD, lanes] for start in at)
            prob = probs[block * heads + head].astype(jnp.float32)
            back = attend_back(
                query, key, value, prob, grad_mixed[head * HD : (head + 1) * HD, lanes]
            )
            for which in range(3):
                grads[at[which] : at[which] + HD, lanes] = back[which]
    grad_normed = nn(qkv_weight[...], grads[...])
    total = upstream[...].astype(jnp.float32) + layer_norm_back(normed, inverse, grad_normed)
    row_grad[...] = bround(total.T)
    grad_qkv = bround(nt(bround(normed), grads[...]))
    grad_out = bround(nt(mixed[...], upstream[...]))
    whole = 3 * channels // LANES
    panels = [grad_qkv[:, i * LANES : (i + 1) * LANES] for i in range(whole)]
    panels.append(jnp.concatenate([grad_qkv[:, whole * LANES :], grad_out[:, LANES:]], 1))
    panels.append(grad_out[:, :LANES])
    half = len(panels) // 2
    for i in range(half):
        at = slice(i * channels, (i + 1) * channels)
        keep[at] = jnp.where(core == 0, panels[i], panels[half + i])
        give[at] = jnp.where(core == 0, panels[half + i], panels[i])


def assemble(
    fine_scale,
    coarse_scale,
    core_ref,
    mine,
    other,
    grad_qkv,
    grad_out,
    grad_pool,
    grad_coarse_qkv,
    grad_coarse_out,
):
    core = core_ref[0]
    channels = grad_out.shape[0]
    part, wide = grad_coarse_out.shape
    edge = part % LANES

    def coarse(start, count):
        return mine[start : start + count].astype(jnp.float32) * coarse_scale

    panels = [coarse(i * wide, wide) for i in range(4)]
    base = 4 * wide
    tail = coarse(base, part)
    grad_coarse_qkv[0, :, :LANES] = panels[0]
    grad_coarse_qkv[0, :, LANES:] = panels[1][:, :edge]
    grad_coarse_qkv[1] = jnp.concatenate([panels[1][:, edge:], panels[2]], 1)
    grad_coarse_qkv[2, :, :LANES] = panels[3]
    grad_coarse_qkv[2, :part, LANES:] = tail[:, :edge]
    grad_coarse_qkv[2, part:, LANES:] = tail[:, edge:]
    base += part
    for panel in range(wide // LANES):
        grad_coarse_out[:, panel * LANES : (panel + 1) * LANES] = coarse(base, part)
        base += part
    first = base
    pool_panels = wide // LANES
    half_rows = SLOTS // 2 * channels
    for source, start, half in ((mine, first, core), (other, 0, 1 - core)):
        for step in range(SLOTS // 2):
            row = pl.multiple_of(half * half_rows + step * channels, 8)
            for panel in range(pool_panels):
                at = start + (step * pool_panels + panel) * channels
                grad_pool[pl.ds(row, channels), panel * LANES : (panel + 1) * LANES] = (
                    source[at : at + channels].astype(jnp.float32) * coarse_scale
                )
    skip = half_rows * pool_panels
    fine = []
    for half in range(2):
        for i in range(3):
            at = skip + i * channels
            near = mine[first + at : first + at + channels].astype(jnp.float32)
            far = other[at : at + channels].astype(jnp.float32)
            fine.append(jnp.where(core == half, near, far) * fine_scale)
    for i in range(4):
        grad_qkv[:, i * LANES : (i + 1) * LANES] = fine[i]
    grad_qkv[:, 4 * LANES :] = fine[4][:, :edge]
    grad_out[:, :LANES] = fine[5]
    grad_out[:, LANES:] = fine[4][:, edge:]


def call(kernel, outs, scratch, *operands, scalars=1, cost=0):
    specs = [pl.BlockSpec(memory_space=pltpu.SMEM)] * scalars
    specs += [pl.BlockSpec(memory_space=pltpu.VMEM)] * (len(operands) - scalars)
    return pl.pallas_call(
        kernel,
        out_shape=[jax.ShapeDtypeStruct(shape, dtype) for shape, dtype in outs],
        in_specs=specs,
        out_specs=[pl.BlockSpec(memory_space=pltpu.VMEM)] * len(outs),
        scratch_shapes=[pltpu.VMEM(shape, jnp.bfloat16) for shape in scratch],
        compiler_params=pltpu.CompilerParams(vmem_limit_bytes=VMEM_BYTES),
        cost_estimate=pl.CostEstimate(
            flops=cost, bytes_accessed=4 * 1024 * 1024, transcendentals=0
        ),
    )(*operands)


def float_sum(stacked):
    return bround(jnp.sum(stacked.astype(jnp.float32), 0))


def sum_over_chips(parts):
    plane = lax.all_to_all(parts, ("y", "x"), 0, 0, tiled=True)
    slab = float_sum(plane)
    copies = jnp.broadcast_to(slab, (lax.axis_size("z"),) + slab.shape)
    slab = float_sum(lax.all_to_all(copies, "z", 0, 0, tiled=True))
    copies = jnp.broadcast_to(slab, parts.shape)
    return lax.all_to_all(copies, ("y", "x"), 0, 0, tiled=True)


def on_device(
    fine_rows,
    qkv_weight,
    out_weight,
    pool_weight,
    coarse_qkv_weight,
    coarse_out_weight,
    parent_index,
    child_slot,
    out_grad,
):
    bf16, f32 = jnp.bfloat16, jnp.float32
    devices = 1
    for name in AXES:
        devices *= lax.axis_size(name)
    row_count, channels = fine_rows.shape
    owned, wide = out_grad.shape
    part = coarse_out_weight.shape[0]
    blocks = row_count // LANES
    heads = channels // HD
    core = lax.axis_index("sub").astype(jnp.int32).reshape(1)
    other_qkv = swap_cores(coarse_qkv_weight)
    other_out = swap_cores(coarse_out_weight)
    first_parent = lax.axis_index(AXES) * owned
    codes = ((parent_index - first_parent) * SLOTS + child_slot).reshape(1, row_count)
    coarse_count = 4 * part * wide // LANES
    pool_count = SLOTS // 2 * channels * wide // LANES
    fine_count = 2 * channels * channels // LANES

    hidden, mixed, qkv, probs, spill = call(
        fine_forward,
        [
            ((channels, row_count), bf16),
            ((channels, row_count), bf16),
            ((3 * channels, row_count), bf16),
            ((blocks * heads, LANES, LANES), bf16),
            ((SPILL, channels), bf16),
        ],
        [],
        fine_rows,
        qkv_weight,
        out_weight,
        codes,
        scalars=0,
        cost=10**10,
    )
    spill_in = passed_along(spill, -1)
    coarse_rows, grad_hidden, spill_grad, keep, give = call(
        coarse_both,
        [
            ((owned, wide), bf16),
            ((channels, row_count), bf16),
            ((SPILL, channels), bf16),
            ((coarse_count + pool_count, LANES), bf16),
            ((coarse_count + pool_count, LANES), bf16),
        ],
        [(SLOTS, channels, owned), (part, owned), (3 * part, owned)],
        core,
        hidden,
        codes,
        spill_in,
        pool_weight,
        coarse_qkv_weight,
        other_qkv,
        coarse_out_weight,
        other_out,
        out_grad,
        cost=10**10,
    )
    spill_back = passed_along(spill_grad, 1)
    got = swap_cores(give)
    row_grad, fine_keep, fine_give = call(
        fine_back,
        [
            ((row_count, channels), bf16),
            ((fine_count, LANES), bf16),
            ((fine_count, LANES), bf16),
        ],
        [(channels, row_count), (3 * channels, row_count)],
        core,
        fine_rows,
        grad_hidden,
        spill_back,
        codes,
        probs,
        qkv,
        mixed,
        qkv_weight,
        out_weight,
        cost=10**10,
    )
    fine_got = swap_cores(fine_give)
    plane = lax.axis_size("y") * lax.axis_size("x")
    count = coarse_count + pool_count + fine_count
    unit = plane * 8
    padded = -(-count // unit) * unit
    rows = jnp.concatenate(
        [
            bround(keep.astype(f32) + got.astype(f32)),
            bround(fine_keep.astype(f32) + fine_got.astype(f32)),
            jnp.zeros((padded - count, LANES), bf16),
        ],
        0,
    )
    total = sum_over_chips(rows.reshape(plane, padded // plane, LANES)).reshape(padded, LANES)
    other = swap_cores(total[coarse_count:count])
    grad_qkv, grad_out, grad_pool, grad_coarse_qkv, grad_coarse_out = call(
        functools.partial(
            assemble, (row_count * devices) ** (-0.5), (owned * devices) ** (-0.5)
        ),
        [
            ((channels, 3 * channels), f32),
            ((channels, channels), f32),
            ((SLOTS * channels, wide), f32),
            ((3, wide, part), f32),
            ((part, wide), f32),
        ],
        [],
        core,
        total,
        other,
    )
    return (
        coarse_rows,
        row_grad,
        grad_qkv,
        grad_out,
        grad_pool,
        grad_coarse_qkv,
        grad_coarse_out,
    )


def solution(mesh):
    torus = Mesh(mesh.devices.reshape(-1, 4, 4, mesh.shape["sub"]), AXES)
    in_specs = (
        P(AXES, None),
        P(),
        P(),
        P(),
        P(None, None, "sub"),
        P("sub", None),
        P(AXES),
        P(AXES),
        P(AXES, None),
    )
    out_specs = (
        P(AXES, None),
        P(AXES, None),
        P(),
        P(),
        P(),
        P(None, None, "sub"),
        P("sub", None),
    )
    return jax.shard_map(
        on_device, mesh=torus, in_specs=in_specs, out_specs=out_specs, check_vma=False
    )
```

time: 582 us -> 147 us (0.25)
  waiting for transfers between devices: 446 us -> 3.77 us
  blocking collectives: 4.08 us -> 79.5 us
  matrix products: 53.8 us -> 0 us
  Pallas kernels: 0 us -> 33.6 us
  local copies, waits for them, and re-layouts: 33.7 us -> 8.83 us
  between operations: 16.4 us -> 0.83 us
  other arithmetic: 18.2 us -> 7.07 us
    psum x2 -> x0, waiting for transfers between devices: 437 us -> none  [the longest x1 268 us: on_device(): lax.psum((grad_qkv_part, grad_out_part, grad_pool_part), ('grp', 'sub'))]
    all_to_all x0 -> x3, blocking collectives: none -> 79.5 us  [the longest x1 29.4 us: sum_over_chips(): slab = float_sum(lax.all_to_all(copies, 'z', 0, 0, tiled=True))]
    dot_general x29 -> x0, matrix products: 51.6 us -> none  [the longest x11 34.7 us: multiply(): return jnp.einsum(form, left, right, preferred_element_type=jnp.float32)]
    pallas_call x0 -> x4, Pallas kernels: none -> 33.6 us  [call(): pl.pallas_call(kernel, out_shape=[jax.ShapeDtypeStruct(shape, dtype) for...]
    another operation x10 -> x0, local copies, waits for them, and re-layouts: 11 us -> none  [the longest x4 7.38 us: on_device(): jnp.stack([grad_cq.reshape(-1, coarse_part), grad_ck.reshape(-1, coarse_p...]
    mul x5 -> x0, other arithmetic: 10.6 us -> none  [the longest x1 3.27 us: on_device(): grad_pool * coarse_scale]
    reduce_scatter x2 -> x0, waiting for transfers between devices: 8.67 us -> none  [the longest x1 8.65 us: on_device(): lax.psum_scatter(layer_norm_back(coarse_normed, coarse_inverse, grad_cnor...]
    convert_element_type x8 -> x0, local copies, waits for them, and re-layouts: 6.04 us -> none  [bround(): return value.astype(jnp.bfloat16)]
  transfers between devices with their start and end apart: 6 -> 7, of which waited for: 3 -> 4; matrix products, arithmetic and copies ran while one was open for 9% -> 3% of each run, Pallas kernels for 0% -> 13%
where the time goes in v1:
time: 147 us; the launch traced here: 146 us
  blocking collectives  79.5 us (54%)
  Pallas kernels  33.6 us (23%)
  starting transfers between devices  12.5 us (9%)
  local copies, waits for them, and re-layouts  8.83 us (6%)
  other arithmetic  7.07 us (5%)
  waiting for transfers between devices  3.77 us (3%)
    pallas_call x4, Pallas kernels, call(): pl.pallas_call(kernel, out_shape=[jax.ShapeDtypeStruct(shape, dtype) for...  33.6 us
    all_to_all x1, blocking collectives, sum_over_chips(): slab = float_sum(lax.all_to_all(copies, 'z', 0, 0, tiled=True))  29.4 us
    all_to_all x1, blocking collectives, sum_over_chips(): plane = lax.all_to_all(parts, ('y', 'x'), 0, 0, tiled=True)  28.6 us
    all_to_all x1, blocking collectives, sum_over_chips(): return lax.all_to_all(copies, ('y', 'x'), 0, 0, tiled=True)  21.5 us
    ppermute x5, starting transfers between devices, swap_cores(): return lax.ppermute(shard, 'sub', [(0, 1), (1, 0)])  7.54 us
    unnamed x28, local copies, waits for them, and re-layouts  7.19 us
    concatenate x1, other arithmetic, on_device(): jnp.concatenate([bround(keep.astype(f32) + got.astype(f32)), bround(fine_...  5.73 us
    ppermute x2, starting transfers between devices, passed_along(): return lax.ppermute(shard, AXES, pairs)  4.94 us
  transfers between devices with their start and end apart: 7, of which 4 were waited for; matrix products, arithmetic and copies ran while one was open for 3% of the time, Pallas kernels for 13%

profile of v1, /device:TPU:1, one launch (start us, length us, event | category | flops | bytes accessed | tf_op | source)
XLA Modules:
  0.0 146.1 jit_solution(5587691588860977369)
XLA Ops:
  0.6 3.3 %collective-permute-start.2 = (bf16[192,384]{1,0:T(8,128)(2,1)}, bf16[192,384]{1,0:T(8,128)(2,1)S(1)}, u32[]{:S(2)}, u32[]{:S(2)}) collective-permute-start(bf16[192,384]{1,0:T(8,128)(2,1)} %own_out.1), channel_id=1, source_target_pairs={{0,1},{1,0},{2,3},{3,2},{4,5},{5,4},{6,7},{7,6},{8,9},{9,8},{10,11... | collective-permute-start | bytes 442376 | tf_op jit(solution)/shard_map/ppermute | solution.py:31
  4.0 0.1 collective-permute-start.1
  4.1 1.1 copy.28.rows
  5.1 0.7 multiply_add_fusion
  5.9 0.9 copy-done.1
  6.8 0.9 copy-done.5
  7.7 10.3 %shard_map.144 = (bf16[192,512]{1,0:T(8,128)(2,1)S(1)}, bf16[192,512]{1,0:T(8,128)(2,1)S(1)}, bf16[576,512]{1,0:T(8,128)(2,1)S(1)}, bf16[48,128,128]{2,1,0:T(8,128)(2,1)S(1)}, bf16[16,192]{1,0:T(8,128)(2,1)S(1)}) custom-call(bf16[512,192]{1,0:T(8,128)(2,1)S(1)} %copy.28.rows, bf16[192,576]{1,0:T(8,128)(2,1)S(1)} %copy-done.1, ...), custom_call_target="tpu_custom_call" | custom-call | flops 10000000000 | bytes 4194304 | tf_op jit(solution)/shard_map/pallas_call | solution.py:337
  17.9 0.0 copy-start.7
  18.0 1.1 copy-done.7
  19.1 0.8 copy-done.9
  19.9 2.6 %collective-permute-start = (bf16[16,192]{1,0:T(8,128)(2,1)S(1)}, bf16[16,192]{1,0:T(8,128)(2,1)S(1)}, u32[]{:S(2)}, u32[]{:S(2)}) collective-permute-start(bf16[16,192]{1,0:T(8,128)(2,1)S(1)} %get-tuple-element.26), channel_id=1, source_target_pairs={{1,0},{2,1},{3,2},{4,3},{5,4},{6,5},{7,6},{8,7},{9,8},{10,9},{11,1... | collective-permute-start | bytes 18440 | tf_op jit(solution)/shard_map/ppermute | solution.py:27
  22.5 0.0 copy-done.11
  22.6 0.2 copy.29.own_qkv
  22.8 0.0 collective-permute-done.1
  22.8 1.2 copy.30.other_qkv
  24.1 0.9 collective-permute-done.spill
  25.0 0.0 collective-permute-done.2.other_out
  25.0 0.0 copy-done.3
  25.0 0.0 copy-done.4
  25.0 0.0 copy-start.2
  25.0 0.0 copy-start.6
  25.1 0.0 copy-start.8
  25.1 0.0 copy-start.10
  25.1 12.5 %shard_map.145 = (bf16[128,384]{1,0:T(8,128)(2,1)}, bf16[192,512]{1,0:T(8,128)(2,1)S(1)}, bf16[16,192]{1,0:T(8,128)(2,1)S(1)}, bf16[4608,128]{1,0:T(8,128)(2,1)S(1)}, bf16[4608,128]{1,0:T(8,128)(2,1)S(1)}) custom-call(s32[1]{0:T(128)} %bitcast.core_ref, bf16[192,512]{1,0:T(8,128)(2,1)S(1)} %get-tuple-element.25.hidden, s32[1,512]{1,0:T(1,128)S(1)} %bitcast.7, ...), custom_call_target="tpu_custom_call" | custom-call | flops 10000000000 | bytes 4194304 | tf_op jit(solution)/shard_map/pallas_call | solution.py:337
  37.6 2.3 %collective-permute-start.3 = (bf16[16,192]{1,0:T(8,128)(2,1)S(1)}, bf16[16,192]{1,0:T(8,128)(2,1)S(1)}, u32[]{:S(2)}, u32[]{:S(2)}) collective-permute-start(bf16[16,192]{1,0:T(8,128)(2,1)S(1)} %get-tuple-element.29), channel_id=1, source_target_pairs={{0,1},{1,2},{2,3},{3,4},{4,5},{5,6},{6,7},{7,8},{8,9},{9,10},{10,1... | collective-permute-start | bytes 18440 | tf_op jit(solution)/shard_map/ppermute | solution.py:27
  39.9 0.2 collective-permute-start.4
  40.1 0.6 collective-permute-done.3.spill_grad
  40.7 0.0 copy-done.2
  40.7 0.0 copy-done.8
  40.7 8.9 %shard_map.146 = (bf16[512,192]{1,0:T(8,128)(2,1)S(1)}, bf16[576,128]{1,0:T(8,128)(2,1)S(1)}, bf16[576,128]{1,0:T(8,128)(2,1)S(1)}) custom-call(s32[1]{0:T(128)} %bitcast.core_ref, bf16[512,192]{1,0:T(8,128)(2,1)S(1)} %copy.28.rows, bf16[192,512]{1,0:T(8,128)(2,1)S(1)} %get-tuple-element.28.grad_hidden, ...), custom_call_target="tpu_custom_call" | custom-call | flops 10000000000 | bytes 4194304 | tf_op jit(solution)/shard_map/pallas_call | solution.py:337
  49.6 0.4 collective-permute-start.5
  50.1 0.1 pad.2.clone
  50.2 1.2 collective-permute-done.5
  51.4 0.0 collective-permute-done.4
  51.4 0.3 add_convert_fusion
  51.7 5.7 %maximum_maximum_fusion = bf16[5248,128]{1,0:T(8,128)(2,1)S(1)} fusion(bf16[576,128]{1,0:T(8,128)(2,1)S(1)} %add_convert_fusion.1, bf16[4608,128]{1,0:T(8,128)(2,1)S(1)} %add_convert_fusion, bf16[5248]{0:T(1024)(128)(2,1)S(1)} %pad.2.clone), kind=kLoop, calls=%fused_computation.1 | loop fusion | flops 4030464 | bytes 2681088 | tf_op jit(solution)/shard_map/concatenate | solution.py:459
  57.4 28.6 %all_to_all.15 = bf16[16,328,128]{2,1,0:T(8,128)(2,1)S(1)} all-to-all(bf16[16,328,128]{2,1,0:T(8,128)(2,1)S(1)} %bitcast.9), channel_id=1, replica_groups=mesh['z'=8,'y'=4,'x'=4,'sub'=2] {'y','x'}, dimensions={0} | all-to-all | bytes 2686976 | tf_op jit(solution)/shard_map/all_to_all | solution.py:355
  86.0 0.2 reduce_sum.24
  86.2 0.1 broadcast_in_dim.10
  86.3 29.4 %all_to_all.16 = bf16[8,328,128]{2,1,0:T(8,128)(2,1)S(1)} all-to-all(bf16[8,328,128]{2,1,0:T(8,128)(2,1)S(1)} %broadcast_in_dim.10), channel_id=1, replica_groups=mesh['z'=8,'y'=4,'x'=4,'sub'=2] {'z'}, dimensions={0} | all-to-all | bytes 1343488 | tf_op jit(solution)/shard_map/all_to_all | solution.py:358
  115.8 0.1 reduce_sum.25
  115.8 0.2 broadcast_in_dim.11
  116.0 21.5 %all_to_all.17 = bf16[16,328,128]{2,1,0:T(8,128)(2,1)S(1)} all-to-all(bf16[16,328,128]{2,1,0:T(8,128)(2,1)S(1)} %broadcast_in_dim.11), channel_id=1, replica_groups=mesh['z'=8,'y'=4,'x'=4,'sub'=2] {'y','x'}, dimensions={0} | all-to-all | bytes 2686976 | tf_op jit(solution)/shard_map/all_to_all | solution.py:360
  137.5 3.5 %collective-permute-start.6 = (bf16[2880,128]{1,0:T(8,128)(2,1)S(1)}, bf16[2880,128]{1,0:T(8,128)(2,1)S(1)}, u32[]{:S(2)}, u32[]{:S(2)}) collective-permute-start(bf16[2880,128]{1,0:T(8,128)(2,1)S(1)} %slice.4), channel_id=1, source_target_pairs={{0,1},{1,0},{2,3},{3,2},{4,5},{5,4},{6,7},{7,6},{8,9},{9,8},{10,11... | collective-permute-start | bytes 2211848 | tf_op jit(solution)/shard_map/ppermute | solution.py:31
  141.1 0.8 copy.32
  141.9 1.0 collective-permute-done.6.other
  142.9 1.9 %shard_map.147 = (f32[192,576]{1,0:T(8,128)}, f32[192,192]{1,0:T(8,128)}, f32[1536,384]{1,0:T(8,128)}, f32[3,384,192]{2,1,0:T(8,128)S(1)}, f32[192,384]{1,0:T(8,128)}) custom-call(s32[1]{0:T(128)} %bitcast.core_ref, bf16[5248,128]{1,0:T(8,128)(2,1)S(1)} %bitcast.5, bf16[2880,128]{1,0:T(8,128)(2,1)S(1)} %collective-permute-done.6.other), custom_call_target="tpu_custom_call" | custom-call | bytes 4194304 | tf_op jit(solution)/shard_map/pallas_call | solution.py:337
  144.9 1.3 copy.33
  (13 shorter events, 0.1 us)
Async XLA Ops:
  0.6 24.4 %collective-permute-start.2 = (bf16[192,384]{1,0:T(8,128)(2,1)}, bf16[192,384]{1,0:T(8,128)(2,1)S(1)}, u32[]{:S(2)}, u32[]{:S(2)}) collective-permute-start(bf16[192,384]{1,0:T(8,128)(2,1)} %own_out.1), channel_id=1, source_target_pairs={{0,1},{1,0},{2,3},{3,2},{4,5},{5,4},{6,7},{7,6},{8,9},{9,8},{10,11... | collective-permute-start | bytes 442376 | tf_op jit(solution)/shard_map/ppermute | solution.py:31
  4.0 18.8 %collective-permute-start.1 = (bf16[3,384,192]{1,2,0:T(8,128)(2,1)}, bf16[3,384,192]{1,2,0:T(8,128)(2,1)}, u32[]{:S(2)}, u32[]{:S(2)}) collective-permute-start(bf16[3,384,192]{1,2,0:T(8,128)(2,1)} %param.13), channel_id=1, source_target_pairs={{0,1},{1,0},{2,3},{3,2},{4,5},{5,4},{6,7},{7,6},{8,9},{9,8},{10,11... | collective-permute-start | bytes 1327112 | tf_op jit(solution)/shard_map/ppermute | solution.py:31
  5.8 0.9 copy-start.1
  6.8 0.9 copy-start.5
  7.7 14.9 %copy-start.11 = (bf16[3,384,192]{1,2,0:T(8,128)(2,1)S(1)}, bf16[3,384,192]{1,2,0:T(8,128)(2,1)}, u32[]{:S(2)}) copy-start(bf16[3,384,192]{1,2,0:T(8,128)(2,1)} %param.13) | copy-start | bytes 1327108
  17.9 1.1 copy-start.7
  19.1 0.8 copy-start.9
  19.9 5.1 %copy-start = (bf16[1536,384]{1,0:T(8,128)(2,1)S(1)}, bf16[1536,384]{1,0:T(8,128)(2,1)}, u32[]{:S(2)}) copy-start(bf16[1536,384]{1,0:T(8,128)(2,1)} %pool_weight.1) | copy-start | bytes 3538948
  19.9 5.1 %copy-start.3 = (bf16[192,384]{1,0:T(8,128)(2,1)S(1)}, bf16[192,384]{1,0:T(8,128)(2,1)}, u32[]{:S(2)}) copy-start(bf16[192,384]{1,0:T(8,128)(2,1)} %own_out.1) | copy-start | bytes 442372
  19.9 5.1 %copy-start.4 = (bf16[128,384]{1,0:T(8,128)(2,1)S(1)}, bf16[128,384]{1,0:T(8,128)(2,1)}, u32[]{:S(2)}) copy-start(bf16[128,384]{1,0:T(8,128)(2,1)} %out_grad.1) | copy-start | bytes 294916
  19.9 5.1 %collective-permute-start = (bf16[16,192]{1,0:T(8,128)(2,1)S(1)}, bf16[16,192]{1,0:T(8,128)(2,1)S(1)}, u32[]{:S(2)}, u32[]{:S(2)}) collective-permute-start(bf16[16,192]{1,0:T(8,128)(2,1)S(1)} %get-tuple-element.26), channel_id=1, source_target_pairs={{1,0},{2,1},{3,2},{4,3},{5,4},{6,5},{7,6},{8,7},{9,8},{10,9},{11,1... | collective-permute-start | bytes 18440 | tf_op jit(solution)/shard_map/ppermute | solution.py:27
  25.0 15.7 %copy-start.2 = (bf16[192,576]{1,0:T(8,128)(2,1)S(1)}, bf16[192,576]{1,0:T(8,128)(2,1)}, u32[]{:S(2)}) copy-start(bf16[192,576]{1,0:T(8,128)(2,1)} %qkv_weight.3) | copy-start | bytes 663556
  25.0 15.7 %copy-start.6 = (bf16[192,192]{1,0:T(8,128)(2,1)S(1)}, bf16[192,192]{1,0:T(8,128)(2,1)}, u32[]{:S(2)}) copy-start(bf16[192,192]{1,0:T(8,128)(2,1)} %out_weight.3) | copy-start | bytes 221188
  25.1 15.6 %copy-start.8 = (bf16[48,128,128]{2,1,0:T(8,128)(2,1)S(1)}, bf16[48,128,128]{2,1,0:T(8,128)(2,1)}, u32[]{:S(2)}) copy-start(bf16[48,128,128]{2,1,0:T(8,128)(2,1)} %copy-done.7) | copy-start | bytes 4718596
  25.1 15.6 %copy-start.10 = (bf16[576,512]{1,0:T(8,128)(2,1)S(1)}, bf16[576,512]{1,0:T(8,128)(2,1)}, u32[]{:S(2)}) copy-start(bf16[576,512]{1,0:T(8,128)(2,1)} %copy-done.9) | copy-start | bytes 1769476
  37.6 3.1 %collective-permute-start.3 = (bf16[16,192]{1,0:T(8,128)(2,1)S(1)}, bf16[16,192]{1,0:T(8,128)(2,1)S(1)}, u32[]{:S(2)}, u32[]{:S(2)}) collective-permute-start(bf16[16,192]{1,0:T(8,128)(2,1)S(1)} %get-tuple-element.29), channel_id=1, source_target_pairs={{0,1},{1,2},{2,3},{3,4},{4,5},{5,6},{6,7},{7,8},{8,9},{9,10},{10,1... | collective-permute-start | bytes 18440 | tf_op jit(solution)/shard_map/ppermute | solution.py:27
  39.9 11.4 %collective-permute-start.4 = (bf16[4608,128]{1,0:T(8,128)(2,1)S(1)}, bf16[4608,128]{1,0:T(8,128)(2,1)S(1)}, u32[]{:S(2)}, u32[]{:S(2)}) collective-permute-start(bf16[4608,128]{1,0:T(8,128)(2,1)S(1)} %get-tuple-element.35), channel_id=1, source_target_pairs={{0,1},{1,0},{2,3},{3,2},{4,5},{5,4},{6,7},{7,6},{8,9},{9,8},{10,11... | collective-permute-start | bytes 3538952 | tf_op jit(solution)/shard_map/ppermute | solution.py:31
  49.6 1.7 %collective-permute-start.5 = (bf16[576,128]{1,0:T(8,128)(2,1)S(1)}, bf16[576,128]{1,0:T(8,128)(2,1)S(1)}, u32[]{:S(2)}, u32[]{:S(2)}) collective-permute-start(bf16[576,128]{1,0:T(8,128)(2,1)S(1)} %get-tuple-element.37), channel_id=1, source_target_pairs={{0,1},{1,0},{2,3},{3,2},{4,5},{5,4},{6,7},{7,6},{8,9},{9,8},{10,11... | collective-permute-start | bytes 442376 | tf_op jit(solution)/shard_map/ppermute | solution.py:31
  137.5 5.4 %collective-permute-start.6 = (bf16[2880,128]{1,0:T(8,128)(2,1)S(1)}, bf16[2880,128]{1,0:T(8,128)(2,1)S(1)}, u32[]{:S(2)}, u32[]{:S(2)}) collective-permute-start(bf16[2880,128]{1,0:T(8,128)(2,1)S(1)} %slice.4), channel_id=1, source_target_pairs={{0,1},{1,0},{2,3},{3,2},{4,5},{5,4},{6,7},{7,6},{8,9},{9,8},{10,11... | collective-permute-start | bytes 2211848 | tf_op jit(solution)/shard_map/ppermute | solution.py:31

commit v2 on v1

v2 whole, which is shorter than its diff:
```python
import functools

import jax
import jax.numpy as jnp
from jax import lax
from jax.experimental import pallas as pl
from jax.experimental.pallas import tpu as pltpu
from jax.sharding import Mesh, PartitionSpec as P

HD = 16
WINDOW_OCTANTS = 32
DILATION_STRIDE = 4
SLOTS = 8
LANES = 128
SPILL = 16
EPSILON = 1e-05
NEAR = ("zl", "y", "x")
AXES = ("zh",) + NEAR + ("sub",)
VMEM_BYTES = 20 * 1024 * 1024
FAR = -1e30


def passed_along(shard, by):
    count = 1
    for name in AXES:
        count *= lax.axis_size(name)
    pairs = [(i, i + by) for i in range(count) if 0 <= i + by < count]
    return lax.ppermute(shard, AXES, pairs)


def swap_cores(shard):
    return lax.ppermute(shard, "sub", [(0, 1), (1, 0)])


def bround(value):
    return value.astype(jnp.bfloat16)


def product(left, right, left_dim, right_dim):
    return lax.dot_general(
        left, right, (((left_dim,), (right_dim,)), ((), ())), preferred_element_type=jnp.float32
    )


def nn(left, right):
    return product(left, right, 1, 0)


def nt(left, right):
    return product(left, right, 1, 1)


def tn(left, right):
    return product(left, right, 0, 0)


def indicator(condition):
    return bround(jnp.where(condition, 1.0, 0.0))


def layer_norm(value, axis):
    center = value - jnp.mean(value, axis, keepdims=True)
    inverse = lax.rsqrt(jnp.mean(center * center, axis, keepdims=True) + EPSILON)
    return (center * inverse, inverse)


def layer_norm_back(normed, inverse, upstream, axis):
    return inverse * (
        upstream
        - jnp.mean(upstream, axis, keepdims=True)
        - normed * jnp.mean(upstream * normed, axis, keepdims=True)
    )


def window_rows(window_of):
    row = lax.broadcasted_iota(jnp.int32, (SPILL, LANES), 0)
    lane = lax.broadcasted_iota(jnp.int32, (SPILL, LANES), 1)
    return indicator(window_of(lane) == row)


def mask_rows(window_of, heads):
    row = lax.broadcasted_iota(jnp.int32, (SPILL, LANES), 0)
    lane = lax.broadcasted_iota(jnp.int32, (SPILL, LANES), 1)
    other = (window_of(lane) != row) & (row < LANES // WINDOW_OCTANTS)
    return jnp.concatenate([bround(jnp.where(other, FAR, 0.0))] * heads, 1)


def fine_window(at):
    return at % DILATION_STRIDE


def coarse_window(at):
    return at // WINDOW_OCTANTS


def spread(wide, rows, heads):
    for head in range(heads):
        at = slice(head * HD, (head + 1) * HD)
        wide[at, head * LANES : (head + 1) * LANES] = rows[at]


def softmax_parts(score):
    exponent = jnp.exp(score - jnp.max(score, 0, keepdims=True))
    return (bround(exponent), 1.0 / jnp.sum(exponent, 0, keepdims=True))


def attend_back(query, key, upstream, exponent, inverse, grad_prob):
    weighted = exponent.astype(jnp.float32)
    mean = inverse * jnp.sum(weighted * grad_prob, 0, keepdims=True)
    grad_score = bround(weighted * (grad_prob - mean))
    grad_value = nt(bround(upstream.astype(jnp.float32) * inverse), exponent)
    grad_query = nn(key, grad_score)
    grad_key = nt(query, grad_score)
    return (bround(grad_query), bround(grad_key), bround(grad_value))


def scaled(value):
    return value * jnp.bfloat16(HD**-0.5)


def fine_attention(qkv, wide, classes, heads, mixed, store):
    channels = heads * HD
    spread(wide, scaled(qkv[:channels]), heads)
    keys = jnp.concatenate([qkv[channels : 2 * channels], classes], 0)
    scores = tn(keys, wide[...])
    for head in range(heads):
        exponent, inverse = softmax_parts(scores[:, head * LANES : (head + 1) * LANES])
        value = qkv[2 * channels + head * HD : 2 * channels + (head + 1) * HD]
        mixed[head * HD : (head + 1) * HD] = bround(nn(value, exponent) * inverse)
        if store is not None:
            store(head, exponent, inverse)


def clear_wide(wide, heads, window_of):
    wide[...] = jnp.zeros(wide.shape, wide.dtype)
    for slot in range(wide.shape[0]):
        wide[slot, heads * HD :] = mask_rows(window_of, heads)


def fine_forward(
    rows_in,
    qkv_in,
    out_in,
    rows,
    qkv_weight,
    out_weight,
    hidden,
    mixed,
    qkv,
    exponents,
    inverses,
    wide,
    arrived,
):
    pairs = ((rows_in, rows), (qkv_in, qkv_weight), (out_in, out_weight))
    copies = [
        pltpu.make_async_copy(source, target, arrived.at[i])
        for i, (source, target) in enumerate(pairs)
    ]
    for copy in copies:
        copy.start()
    channels, count = hidden.shape
    heads = channels // HD
    clear_wide(wide, heads, fine_window)
    classes = window_rows(fine_window)
    copies[0].wait()
    copies[1].wait()
    rows_float = rows[...].astype(jnp.float32)
    normed, _ = layer_norm(rows_float, 0)
    qkv[...] = bround(tn(qkv_weight[...], bround(normed)))
    for block in range(count // LANES):
        lanes = slice(block * LANES, (block + 1) * LANES)

        def store(head, exponent, inverse):
            exponents[block, :, head * LANES : (head + 1) * LANES] = exponent
            at = block * heads + head
            inverses[at : at + 1] = inverse

        fine_attention(
            qkv[:, lanes],
            wide.at[block % wide.shape[0]],
            classes,
            heads,
            mixed.at[:, lanes],
            store,
        )
    copies[2].wait()
    hidden[...] = bround(rows_float + tn(out_weight[...], mixed[...]))


def leading_slots(parent_index, child_slot, first_parent):
    slot = lax.broadcasted_iota(jnp.int32, (SPILL, LANES), 0)
    before = parent_index[:, :LANES] < first_parent[0]
    return indicator(before & (child_slot[:, :LANES] == slot))


def slot_numbers(parent_index, child_slot, first_parent, owned):
    parent = lax.broadcasted_iota(jnp.int32, (owned, parent_index.shape[1]), 0)
    mine = parent_index - first_parent[0] == parent
    return jnp.where(mine, child_slot, -1)


def coarse_both(
    first_parent,
    own_hidden,
    parent_index,
    child_slot,
    next_rows,
    next_parent,
    next_slot,
    fine_qkv,
    fine_out,
    pool_weight,
    own_qkv,
    other_qkv,
    own_out,
    other_out,
    out_grad,
    coarse_rows,
    spill_grad,
    grad_parents,
    pooled,
    grad_pooled,
    coarse_input,
    mixed,
    grads,
    hidden,
    next_mixed,
    wide_next,
    wide_query,
    wide_grad,
):
    owned, width = out_grad.shape
    channels, row_count = own_hidden.shape
    part = own_out.shape[0]
    heads = part // HD
    fine_heads = channels // HD
    clear_wide(wide_next, fine_heads, fine_window)
    rows_float = next_rows[:, :LANES].astype(jnp.float32)
    normed, _ = layer_norm(rows_float, 0)
    fine_attention(
        bround(tn(fine_qkv[...], bround(normed))),
        wide_next.at[0],
        window_rows(fine_window),
        fine_heads,
        next_mixed,
        None,
    )
    hidden[:, :row_count] = own_hidden[...]
    hidden[:, row_count:] = bround(rows_float + tn(fine_out[...], next_mixed[...]))
    slot_of = slot_numbers(
        jnp.concatenate([parent_index[...], next_parent[:, :LANES]], 1),
        jnp.concatenate([child_slot[...], next_slot[:, :LANES]], 1),
        first_parent,
        owned,
    )
    total = jnp.zeros((owned, width), jnp.float32)
    for slot in range(0, SLOTS, 2):
        both = jnp.concatenate([indicator(slot_of == slot), indicator(slot_of == slot + 1)], 0)
        children = bround(nt(hidden[...], both))
        for i in range(2):
            chosen = children[:, i * owned : (i + 1) * owned]
            pooled[slot + i] = chosen
            at = (slot + i) * channels
            total += tn(chosen, pool_weight[at : at + channels])
    parents = bround(total).astype(jnp.float32)
    normed, inverse = layer_norm(parents, 1)
    coarse_input[...] = bround(normed)
    upstream = out_grad[...]
    classes = window_rows(coarse_window)
    grad_normed = jnp.zeros((owned, width), jnp.float32)
    summed = jnp.zeros((owned, width), jnp.float32)
    for wide in (wide_query, wide_grad):
        wide[...] = jnp.zeros(wide.shape, wide.dtype)
    weights = ((own_qkv, own_out), (other_qkv, other_out))
    for half, (qkv_weight, out_weight) in enumerate(weights):
        qkv = bround(nt(qkv_weight[...], coarse_input[...]))
        upward = bround(nt(out_weight[...], upstream))
        wide_query[half, part:] = mask_rows(coarse_window, heads)
        spread(wide_query.at[half], scaled(qkv[:part]), heads)
        keys = jnp.concatenate([qkv[part : 2 * part], classes], 0)
        scores = tn(keys, wide_query[half])
        parts = []
        for head in range(heads):
            at = slice(head * HD, (head + 1) * HD)
            exponent, scale = softmax_parts(scores[:, head * LANES : (head + 1) * LANES])
            parts.append((exponent, scale))
            value = qkv[2 * part + head * HD : 2 * part + (head + 1) * HD]
            mixed[half, at] = bround(nn(value, exponent) * scale)
            weighted = scaled(upward[at]).astype(jnp.float32) * scale
            wide_grad[half, at, head * LANES : (head + 1) * LANES] = bround(weighted)
        grad_probs = tn(qkv[2 * part :], wide_grad[half])
        for head in range(heads):
            at = [slice(i * part + head * HD, i * part + (head + 1) * HD) for i in range(3)]
            back = attend_back(
                qkv[at[0]],
                qkv[at[1]],
                upward[at[0]],
                *parts[head],
                grad_probs[:, head * LANES : (head + 1) * LANES],
            )
            for which in range(3):
                grads[half, at[which]] = back[which]
        summed += tn(mixed[half], out_weight[...])
        grad_normed += tn(grads[half], qkv_weight[...])
    coarse_rows[...] = bround(parents + summed)
    upstream_total = bround(
        upstream.astype(jnp.float32) + layer_norm_back(normed, inverse, grad_normed, 1)
    )
    grad_parents[...] = upstream_total
    spill_slot = lax.broadcasted_iota(jnp.int32, (SPILL, owned), 0)
    last = lax.broadcasted_iota(jnp.int32, (SPILL, owned), 1) == owned - 1
    edge_total = jnp.zeros((SPILL, channels), jnp.float32)
    for slot in range(SLOTS):
        weight = pool_weight[slot * channels : (slot + 1) * channels]
        grad_slot = bround(nt(weight, upstream_total))
        grad_pooled[slot] = grad_slot
        edge_total += nt(indicator(last & (spill_slot == slot)), grad_slot)
    spill_grad[...] = bround(edge_total)


def coarse_weights(
    core_ref,
    first_parent,
    parent_index,
    child_slot,
    grad_parents,
    pooled,
    grad_pooled,
    coarse_input,
    mixed,
    grads,
    out_grad,
    grad_hidden,
    keep,
    give,
):
    core = core_ref[0]
    owned, width = out_grad.shape
    channels, row_count = grad_hidden.shape
    part = mixed.shape[1]
    panels = width // LANES

    def store(target, start, value):
        for panel in range(panels):
            at = start + panel * value.shape[0]
            target[at : at + value.shape[0]] = bround(
                value[:, panel * LANES : (panel + 1) * LANES]
            )

    for half, target in enumerate((keep, give)):
        store(target, 0, nn(grads[half], coarse_input[...]))
        store(target, 3 * part * panels, nn(mixed[half], out_grad[...]))
    base = 4 * part * panels
    for target, first in ((keep, core), (give, 1 - core)):
        for step in range(SLOTS // 2):
            grad_pool = nn(pooled[first * (SLOTS // 2) + step], grad_parents[...])
            store(target, base + step * panels * channels, grad_pool)
    slot_of = slot_numbers(parent_index[...], child_slot[...], first_parent, owned)
    grad_total = jnp.zeros((channels, row_count), jnp.float32)
    for slot in range(SLOTS):
        grad_total += nn(grad_pooled[slot], indicator(slot_of == slot))
    grad_hidden[...] = bround(grad_total)


def fine_back(
    first_block,
    core_ref,
    first_parent,
    rows,
    grad_hidden,
    exponents,
    inverses,
    qkv,
    mixed,
    qkv_weight,
    out_weight,
    *rest,
):
    if first_block:
        row_grad, qkv_total, out_total, grads, wide = rest
        spill_grad = None
    else:
        spill_grad, parent_index, child_slot, row_rest, qkv_rest, out_rest = rest[:6]
        row_grad, keep, give, grads, wide = rest[6:]
    channels, count = grads.shape[0] // 3, grads.shape[1]
    heads = channels // HD
    span = slice(first_block * LANES, first_block * LANES + count)
    normed, inverse = layer_norm(rows[:, span].astype(jnp.float32), 0)
    upstream = grad_hidden[:, span]
    if spill_grad is not None:
        leading = leading_slots(parent_index, child_slot, first_parent)
        upstream = bround(upstream.astype(jnp.float32) + tn(spill_grad[...], leading))
    upward = bround(nn(out_weight[...], upstream))
    wide[...] = jnp.zeros(wide.shape, wide.dtype)
    for block in range(count // LANES):
        lanes = slice(block * LANES, (block + 1) * LANES)
        whole = first_block + block
        outer = slice(whole * LANES, (whole + 1) * LANES)
        grad_rows = wide.at[block % wide.shape[0]]
        scales = [
            inverses[whole * heads + head : whole * heads + head + 1] for head in range(heads)
        ]
        for head in range(heads):
            at = slice(head * HD, (head + 1) * HD)
            weighted = scaled(upward[at, lanes]).astype(jnp.float32) * scales[head]
            grad_rows[at, head * LANES : (head + 1) * LANES] = bround(weighted)
        grad_probs = tn(qkv[2 * channels :, outer], grad_rows[...])
        for head in range(heads):
            at = [slice(i * channels + head * HD, i * channels + (head + 1) * HD) for i in range(3)]
            out = slice(head * LANES, (head + 1) * LANES)
            back = attend_back(
                qkv[at[0], outer],
                qkv[at[1], outer],
                upward[at[0], lanes],
                exponents[whole, :, out],
                scales[head],
                grad_probs[:, out],
            )
            for which in range(3):
                grads[at[which], lanes] = back[which]
    grad_normed = nn(qkv_weight[...], grads[...])
    total = upstream.astype(jnp.float32) + layer_norm_back(normed, inverse, grad_normed, 0)
    grad_qkv = nt(bround(normed), grads[...])
    grad_out = nt(mixed[:, span], upstream)
    if first_block:
        row_grad[...] = bround(total)
        qkv_total[...] = grad_qkv
        out_total[...] = grad_out
        return
    row_grad[:, span] = bround(total)
    row_grad[:, count:] = row_rest[...]
    grad_qkv = bround(grad_qkv + qkv_rest[...])
    grad_out = bround(grad_out + out_rest[...])
    core = core_ref[0]
    whole = 3 * channels // LANES
    panels = [grad_qkv[:, i * LANES : (i + 1) * LANES] for i in range(whole)]
    panels.append(jnp.concatenate([grad_qkv[:, whole * LANES :], grad_out[:, LANES:]], 1))
    panels.append(grad_out[:, :LANES])
    half = len(panels) // 2
    for i in range(half):
        at = slice(i * channels, (i + 1) * channels)
        keep[at] = jnp.where(core == 0, panels[i], panels[half + i])
        give[at] = jnp.where(core == 0, panels[half + i], panels[i])


def merge(keep, got, fine_keep, fine_got, total):
    first, second = keep.shape[0], fine_keep.shape[0]
    total[:first] = keep[...] + got[...]
    total[first : first + second] = fine_keep[...] + fine_got[...]
    pad = total.shape[0] - first - second
    total[first + second :] = jnp.zeros((pad, LANES), total.dtype)


def assemble(
    fine_scale,
    coarse_scale,
    core_ref,
    mine,
    other,
    grad_qkv,
    grad_out,
    grad_pool,
    grad_coarse_qkv,
    grad_coarse_out,
):
    core = core_ref[0]
    channels = grad_out.shape[0]
    part, width = grad_coarse_out.shape
    panels = width // LANES
    edge = channels % LANES

    def coarse(start, count):
        return mine[start : start + count].astype(jnp.float32) * coarse_scale

    first = 3 * part * panels
    for panel in range(panels):
        lanes = slice(panel * LANES, (panel + 1) * LANES)
        for which in range(3):
            grad_coarse_qkv[which, :, lanes] = coarse((3 * panel + which) * part, part)
        grad_coarse_out[:, lanes] = coarse(first + panel * part, part)
    first += panels * part
    half_rows = SLOTS // 2 * channels
    for source, start, half in ((mine, first, core), (other, 0, 1 - core)):
        for step in range(SLOTS // 2):
            row = pl.multiple_of(half * half_rows + step * channels, 8)
            for panel in range(panels):
                at = start + (step * panels + panel) * channels
                grad_pool[pl.ds(row, channels), panel * LANES : (panel + 1) * LANES] = (
                    source[at : at + channels].astype(jnp.float32) * coarse_scale
                )
    skip = half_rows * panels
    fine = []
    for half in range(2):
        for i in range(3):
            at = skip + i * channels
            near = mine[first + at : first + at + channels].astype(jnp.float32)
            far = other[at : at + channels].astype(jnp.float32)
            fine.append(jnp.where(core == half, near, far) * fine_scale)
    for i in range(4):
        grad_qkv[:, i * LANES : (i + 1) * LANES] = fine[i]
    grad_qkv[:, 4 * LANES :] = fine[4][:, :edge]
    grad_out[:, :LANES] = fine[5]
    grad_out[:, LANES:] = fine[4][:, edge:]


def call(kernel, outs, scratch, *operands, scalars=1, micros=1, hbm=0, copies=0):
    spaces = [pltpu.SMEM] * scalars + [pltpu.HBM] * hbm
    spaces += [pltpu.VMEM] * (len(operands) - len(spaces))
    return pl.pallas_call(
        kernel,
        out_shape=[jax.ShapeDtypeStruct(shape, dtype) for shape, dtype in outs],
        in_specs=[pl.BlockSpec(memory_space=space) for space in spaces],
        out_specs=[pl.BlockSpec(memory_space=pltpu.VMEM)] * len(outs),
        scratch_shapes=[pltpu.VMEM(shape, jnp.bfloat16) for shape in scratch]
        + ([pltpu.SemaphoreType.DMA((copies,))] if copies else []),
        compiler_params=pltpu.CompilerParams(vmem_limit_bytes=VMEM_BYTES),
        cost_estimate=pl.CostEstimate(
            flops=int(micros * 10**9), bytes_accessed=int(micros * 10**6), transcendentals=0
        ),
    )(*operands)


def float_sum(stacked):
    return bround(jnp.sum(stacked.astype(jnp.float32), 0))


def sum_over_chips(parts):
    plane = lax.all_to_all(parts, NEAR, 0, 0, tiled=True)
    slab = float_sum(plane)
    copies = jnp.broadcast_to(slab, (lax.axis_size("zh"),) + slab.shape)
    slab = float_sum(lax.all_to_all(copies, "zh", 0, 0, tiled=True))
    copies = jnp.broadcast_to(slab, parts.shape)
    return lax.all_to_all(copies, NEAR, 0, 0, tiled=True)


def on_device(
    fine_rows,
    qkv_weight,
    out_weight,
    pool_weight,
    coarse_qkv_weight,
    coarse_out_weight,
    parent_index,
    child_slot,
    out_grad,
):
    bf16, f32 = jnp.bfloat16, jnp.float32
    devices = 1
    for name in AXES:
        devices *= lax.axis_size(name)
    row_count, channels = fine_rows.shape
    owned, width = out_grad.shape
    part = coarse_out_weight.shape[0]
    blocks = row_count // LANES
    heads = channels // HD
    coarse_heads = part // HD
    coarse_count = 4 * part * width // LANES
    pool_count = SLOTS // 2 * channels * width // LANES
    fine_count = 2 * channels * channels // LANES
    core = lax.axis_index("sub").astype(jnp.int32).reshape(1)
    first_parent = (lax.axis_index(AXES) * owned).astype(jnp.int32).reshape(1)
    rows = fine_rows.T
    parent_row = parent_index.reshape(1, row_count)
    slot_row = child_slot.reshape(1, row_count)
    own_qkv = coarse_qkv_weight.transpose(0, 2, 1).reshape(3 * part, width)
    other_qkv = swap_cores(own_qkv)
    other_out = swap_cores(coarse_out_weight)
    next_rows = passed_along(rows, -1)
    next_parent = passed_along(parent_row, -1)
    next_slot = passed_along(slot_row, -1)
    wide_rows = heads * LANES
    rows, fine_qkv, fine_out, hidden, mixed_fine, qkv, exponents, inverses = call(
        fine_forward,
        [
            ((channels, row_count), bf16),
            ((channels, 3 * channels), bf16),
            ((channels, channels), bf16),
            ((channels, row_count), bf16),
            ((channels, row_count), bf16),
            ((3 * channels, row_count), bf16),
            ((blocks, LANES, wide_rows), bf16),
            ((blocks * heads, LANES), f32),
        ],
        [(2, channels + SPILL, wide_rows)],
        *(
            pltpu.with_memory_space_constraint(array, pltpu.HBM)
            for array in (rows, qkv_weight, out_weight)
        ),
        scalars=0,
        hbm=3,
        copies=3,
        micros=4,
    )
    coarse_rows, spill_grad, grad_parents, pooled, grad_pooled, coarse_input, mixed, grads = call(
        coarse_both,
        [
            ((owned, width), bf16),
            ((SPILL, channels), bf16),
            ((owned, width), bf16),
            ((SLOTS, channels, owned), bf16),
            ((SLOTS, channels, owned), bf16),
            ((owned, width), bf16),
            ((2, part, owned), bf16),
            ((2, 3 * part, owned), bf16),
        ],
        [
            (channels, row_count + LANES),
            (channels, LANES),
            (1, channels + SPILL, wide_rows),
            (2, part + SPILL, coarse_heads * LANES),
            (2, part, coarse_heads * LANES),
        ],
        first_parent,
        hidden,
        parent_row,
        slot_row,
        next_rows,
        next_parent,
        next_slot,
        fine_qkv,
        fine_out,
        pool_weight,
        own_qkv,
        other_qkv,
        coarse_out_weight,
        other_out,
        out_grad,
        micros=9,
    )
    spill_back = passed_along(spill_grad, 1)
    grad_hidden, keep, give = call(
        coarse_weights,
        [
            ((channels, row_count), bf16),
            ((coarse_count + pool_count, LANES), bf16),
            ((coarse_count + pool_count, LANES), bf16),
        ],
        [],
        core,
        first_parent,
        parent_row,
        slot_row,
        grad_parents,
        pooled,
        grad_pooled,
        coarse_input,
        mixed,
        grads,
        out_grad,
        scalars=2,
        micros=1e-4,
    )
    got = swap_cores(give)
    shared = (
        core,
        first_parent,
        rows,
        grad_hidden,
        exponents,
        inverses,
        qkv,
        mixed_fine,
        fine_qkv,
        fine_out,
    )
    rest_count = row_count - LANES
    row_rest, qkv_rest, out_rest = call(
        functools.partial(fine_back, 1),
        [
            ((channels, rest_count), bf16),
            ((channels, 3 * channels), f32),
            ((channels, channels), f32),
        ],
        [(3 * channels, rest_count), (2, channels, wide_rows)],
        *shared,
        scalars=2,
        micros=1e-4,
    )
    row_grad, fine_keep, fine_give = call(
        functools.partial(fine_back, 0),
        [
            ((channels, row_count), bf16),
            ((fine_count, LANES), bf16),
            ((fine_count, LANES), bf16),
        ],
        [(3 * channels, LANES), (1, channels, wide_rows)],
        *shared,
        spill_back,
        parent_row,
        slot_row,
        row_rest,
        qkv_rest,
        out_rest,
        scalars=2,
        micros=2,
    )
    fine_got = swap_cores(fine_give)
    plane = lax.axis_size("zl") * lax.axis_size("y") * lax.axis_size("x")
    count = coarse_count + pool_count + fine_count
    unit = plane * 8
    padded = -(-count // unit) * unit
    (merged,) = call(
        merge, [((padded, LANES), bf16)], [], keep, got, fine_keep, fine_got, scalars=0, micros=1
    )
    total = sum_over_chips(merged.reshape(plane, padded // plane, LANES)).reshape(padded, LANES)
    other = swap_cores(total[coarse_count:count])
    grad_qkv, grad_out, grad_pool, grad_coarse_qkv, grad_coarse_out = call(
        functools.partial(
            assemble, (row_count * devices) ** (-0.5), (owned * devices) ** (-0.5)
        ),
        [
            ((channels, 3 * channels), f32),
            ((channels, channels), f32),
            ((SLOTS * channels, width), f32),
            ((3, part, width), f32),
            ((part, width), f32),
        ],
        [],
        core,
        total,
        other,
        micros=2,
    )
    return (
        coarse_rows,
        row_grad.T,
        grad_qkv,
        grad_out,
        grad_pool,
        grad_coarse_qkv.transpose(0, 2, 1),
        grad_coarse_out,
    )


def solution(mesh):
    torus = Mesh(mesh.devices.reshape(-1, 2, 4, 4, mesh.shape["sub"]), AXES)
    in_specs = (
        P(AXES, None),
        P(),
        P(),
        P(),
        P(None, None, "sub"),
        P("sub", None),
        P(AXES),
        P(AXES),
        P(AXES, None),
    )
    out_specs = (
        P(AXES, None),
        P(AXES, None),
        P(),
        P(),
        P(),
        P(None, None, "sub"),
        P("sub", None),
    )
    return jax.shard_map(
        on_device, mesh=torus, in_specs=in_specs, out_specs=out_specs, check_vma=False
    )
```

time: 147 us -> 116 us (0.79)
  Pallas kernels: 33.6 us -> 21.1 us
  blocking collectives: 79.5 us -> 67.3 us
  other arithmetic: 7.07 us -> 0.22 us
  starting transfers between devices: 12.5 us -> 17.9 us
  local copies, waits for them, and re-layouts: 8.83 us -> 4.04 us
    pallas_call x4 -> x7, Pallas kernels: 33.6 us -> 21.1 us  [call(): pl.pallas_call(kernel, out_shape=[jax.ShapeDtypeStruct(shape, dtype) for...]
    all_to_all x3, blocking collectives: 79.5 us -> 67.3 us  [the longest x1 30.5 us: sum_over_chips(): plane = lax.all_to_all(parts, NEAR, 0, 0, tiled=True)]
    concatenate x1 -> x0, other arithmetic: 5.73 us -> none  [on_device(): jnp.concatenate([bround(keep.astype(f32) + got.astype(f32)), bround(fine_...]
    ppermute x2 -> x4, starting transfers between devices: 4.94 us -> 10.2 us  [passed_along(): return lax.ppermute(shard, AXES, pairs)]
    unnamed x28 -> x16, local copies, waits for them, and re-layouts: 7.19 us -> 3.79 us
  transfers between devices with their start and end apart: 7 -> 9, of which waited for: 4 -> 3; matrix products, arithmetic and copies ran while one was open for 3% -> 0% of each run, Pallas kernels for 13% -> 8%
where the time goes in v2:
time: 116 us
  blocking collectives  67.3 us (58%)
  Pallas kernels  21.1 us (18%)
  starting transfers between devices  17.9 us (15%)
  waiting for transfers between devices  4.35 us (4%)
  local copies, waits for them, and re-layouts  4.04 us (3%)
    all_to_all x1, blocking collectives, sum_over_chips(): plane = lax.all_to_all(parts, NEAR, 0, 0, tiled=True)  30.5 us
    all_to_all x1, blocking collectives, sum_over_chips(): return lax.all_to_all(copies, NEAR, 0, 0, tiled=True)  21.8 us
    pallas_call x7, Pallas kernels, call(): pl.pallas_call(kernel, out_shape=[jax.ShapeDtypeStruct(shape, dtype) for...  21.1 us
    all_to_all x1, blocking collectives, sum_over_chips(): slab = float_sum(lax.all_to_all(copies, 'zh', 0, 0, tiled=True))  15 us
    ppermute x4, starting transfers between devices, passed_along(): return lax.ppermute(shard, AXES, pairs)  10.2 us
    ppermute x5, starting transfers between devices, swap_cores(): return lax.ppermute(shard, 'sub', [(0, 1), (1, 0)])  7.67 us
    unnamed x16, local copies, waits for them, and re-layouts  3.79 us
    ppermute x5, waiting for transfers between devices, swap_cores(): return lax.ppermute(shard, 'sub', [(0, 1), (1, 0)])  3.22 us
  transfers between devices with their start and end apart: 9, of which 3 were waited for; matrix products, arithmetic and copies ran while one was open for 0% of the time, Pallas kernels for 8%

profile of v2, /device:TPU:1, one launch (start us, length us, event | category | flops | bytes accessed | tf_op | source)
XLA Modules:
  0.0 115.7 jit_solution(16615581623039819470)
XLA Ops:
  0.6 3.3 %collective-permute-start.3 = (bf16[576,384]{1,0:T(8,128)(2,1)}, bf16[576,384]{1,0:T(8,128)(2,1)}, u32[]{:S(2)}, u32[]{:S(2)}) collective-permute-start(bf16[576,384]{1,0:T(8,128)(2,1)} %bitcast.23), channel_id=1, source_target_pairs={{0,1},{1,0},{2,3},{3,2},{4,5},{5,4},{6,7},{7,6},{8,9},{9,8},{10,11... | collective-permute-start | bytes 1327112 | tf_op jit(solution)/shard_map/ppermute | solution.py:32
  4.0 1.9 %collective-permute-start.1 = (s32[1,512]{1,0:T(1,128)}, s32[1,512]{1,0:T(1,128)S(1)}, u32[]{:S(2)}, u32[]{:S(2)}) collective-permute-start(s32[1,512]{1,0:T(1,128)} %bitcast.15), channel_id=1, source_target_pairs={{1,0},{2,1},{3,2},{4,3},{5,4},{6,5},{7,6},{8,7},{9,8},{10,9},{11,1... | collective-permute-start | bytes 6152 | tf_op jit(solution)/shard_map/ppermute | solution.py:28
  5.9 1.9 %collective-permute-start.2 = (s32[1,512]{1,0:T(1,128)}, s32[1,512]{1,0:T(1,128)S(1)}, u32[]{:S(2)}, u32[]{:S(2)}) collective-permute-start(s32[1,512]{1,0:T(1,128)} %bitcast.19), channel_id=1, source_target_pairs={{1,0},{2,1},{3,2},{4,3},{5,4},{6,5},{7,6},{8,7},{9,8},{10,9},{11,1... | collective-permute-start | bytes 6152 | tf_op jit(solution)/shard_map/ppermute | solution.py:28
  7.8 0.1 collective-permute-start.4
  7.9 0.0 copy-start
  7.9 0.0 copy-start.1
  7.9 0.0 copy-start.2
  8.0 0.0 copy-start.4
  8.0 2.5 %collective-permute-start = (bf16[192,512]{1,0:T(8,128)(2,1)}, bf16[192,512]{1,0:T(8,128)(2,1)}, u32[]{:S(2)}, u32[]{:S(2)}) collective-permute-start(bf16[192,512]{1,0:T(8,128)(2,1)} %bitcast.25), channel_id=1, source_target_pairs={{1,0},{2,1},{3,2},{4,3},{5,4},{6,5},{7,6},{8,7},{9,8},{10,9},{11,1... | collective-permute-start | bytes 589832 | tf_op jit(solution)/shard_map/ppermute | solution.py:28
  10.5 3.5 %shard_map.144 = (bf16[192,512]{1,0:T(8,128)(2,1)S(1)}, bf16[192,576]{1,0:T(8,128)(2,1)S(1)}, bf16[192,192]{1,0:T(8,128)(2,1)S(1)}, bf16[192,512]{1,0:T(8,128)(2...) custom-call(bf16[192,512]{1,0:T(8,128)(2,1)} %bitcast.26, ...), custom_call_target="tpu_custom_call" | custom-call | flops 4000000000 | bytes 4000000 | tf_op jit(solution)/shard_map/pallas_call | solution.py:510
  14.0 0.0 copy-start.6
  14.0 0.7 copy-done.6
  14.7 0.0 collective-permute-done.1.next_parent
  14.7 0.0 collective-permute-done.2.next_slot
  14.7 0.0 collective-permute-done.4.other_out
  14.7 1.1 collective-permute-done.next_rows
  15.8 0.0 collective-permute-done.3.other_qkv
  15.8 0.0 copy-done
  15.8 0.0 copy-done.1
  15.9 0.0 copy-done.2
  15.9 0.0 copy-done.4
  15.9 0.0 copy-start.3
  15.9 1.3 %copy-done.3 = bf16[1536,384]{1,0:T(8,128)(2,1)S(1)} copy-done((bf16[1536,384]{1,0:T(8,128)(2,1)S(1)}, bf16[1536,384]{1,0:T(8,128)(2,1)}, u32[]{:S(2)}) %copy-start.3) | copy-done | bytes 1179672
  17.1 0.0 copy-start.5
  17.1 0.9 copy-done.5
  18.1 0.0 copy-start.7
  18.1 0.9 copy-done.7
  19.0 8.6 %shard_map.145 = (bf16[128,384]{1,0:T(8,128)(2,1)}, bf16[16,192]{1,0:T(8,128)(2,1)S(1)}, bf16[128,384]{1,0:T(8,128)(2,1)S(1)}, bf16[8,192,128]{2,1,0:T(8,128)(2,...) custom-call(s32[1]{0:T(128)} %bitcast.first_parent, ...), custom_call_target="tpu_custom_call" | custom-call | flops 8999999488 | bytes 9000000 | tf_op jit(solution)/shard_map/pallas_call | solution.py:510
  27.6 1.2 %shard_map.146 = (bf16[192,512]{1,0:T(8,128)(2,1)S(1)}, bf16[4608,128]{1,0:T(8,128)(2,1)S(1)}, bf16[4608,128]{1,0:T(8,128)(2,1)S(1)}) custom-call(s32[1]{0:T(128)} %bitcast.7.core_ref, s32[1]{0:T(128)} %bitcast.first_parent, s32[1,512]{1,0:T(1,128)S(1)} %bitcast.17, s32[1,512]{1,0:T(1,128)S(1)} %bitcast.21, ...), custom_call_target="tpu_custom_call" | custom-call | flops 100000 | bytes 100 | tf_op jit(solution)/shard_map/pallas_call | solution.py:510
  28.8 0.1 collective-permute-start.6
  28.9 3.8 %collective-permute-start.5 = (bf16[16,192]{1,0:T(8,128)(2,1)S(1)}, bf16[16,192]{1,0:T(8,128)(2,1)S(1)}, u32[]{:S(2)}, u32[]{:S(2)}) collective-permute-start(bf16[16,192]{1,0:T(8,128)(2,1)S(1)} %get-tuple-element.53), channel_id=1, source_target_pairs={{0,1},{1,2},{2,3},{3,4},{4,5},{5,6},{6,7},{7,8},{8,9},{9,10},{10,1... | collective-permute-start | bytes 18440 | tf_op jit(solution)/shard_map/ppermute | solution.py:28
  32.7 3.1 %shard_map.147 = (bf16[192,384]{1,0:T(8,128)(2,1)S(1)}, f32[192,576]{1,0:T(8,128)S(1)}, f32[192,192]{1,0:T(8,128)S(1)}) custom-call(s32[1]{0:T(128)} %bitcast.7.core_ref, s32[1]{0:T(128)} %bitcast.first_parent, bf16[192,512]{1,0:T(8,128)(2,1)S(1)} %get-tuple-element.41.rows, bf16[192,512]{1,0:T(8,128)(2,1)S(1)} %get-tuple-element.48.grad_hidden, ...), custom_call_target="tpu_custom_call" | custom-call | flops 100000 | bytes 100 | tf_op jit(solution)/shard_map/pallas_call | solution.py:510
  35.8 0.0 collective-permute-done.5.rest_0_
  35.8 2.3 %shard_map.148 = (bf16[192,512]{1,0:T(8,128)(2,1)}, bf16[576,128]{1,0:T(8,128)(2,1)S(1)}, bf16[576,128]{1,0:T(8,128)(2,1)S(1)}) custom-call(s32[1]{0:T(128)} %bitcast.7.core_ref, s32[1]{0:T(128)} %bitcast.first_parent, bf16[192,512]{1,0:T(8,128)(2,1)S(1)} %get-tuple-element.41.rows, bf16[192,512]{1,0:T(8,128)(2,1)S(1)} %get-tuple-element.48.grad_hidden, ...), custom_call_target="tpu_custom_call" | custom-call | flops 2000000000 | bytes 2000000 | tf_op jit(solution)/shard_map/pallas_call | solution.py:510
  38.1 0.0 collective-permute-start.7
  38.1 1.4 %collective-permute-done.7.fine_got = bf16[576,128]{1,0:T(8,128)(2,1)S(1)} collective-permute-done((bf16[576,128]{1,0:T(8,128)(2,1)S(1)}, bf16[576,128]{1,0:T(8,128)(2,1)S(1)}, u32[]{:S(2)}, u32[]{:S(2)}) %collective-permute-start.7) | collective-permute-done | bytes 147488 | tf_op jit(solution)/shard_map/ppermute | solution.py:32
  39.5 0.0 collective-permute-done.6.got
  39.5 0.3 shard_map.149
  39.8 30.5 %all_to_all.15 = bf16[32,168,128]{2,1,0:T(8,128)(2,1)S(1)} all-to-all(bf16[32,168,128]{2,1,0:T(8,128)(2,1)S(1)} %bitcast.12), channel_id=1, replica_groups=mesh['zh'=4,'zl'=2,'y'=4,'x'=4,'sub'=2] {'zl','y','x'}, dimensions={0} | all-to-all | bytes 2752512 | tf_op jit(solution)/shard_map/all_to_all | solution.py:529
  70.2 0.2 reduce_sum.24
  70.5 15.0 %all_to_all.16 = bf16[4,168,128]{2,1,0:T(8,128)(2,1)S(1)} all-to-all(bf16[4,168,128]{2,1,0:T(8,128)(2,1)S(1)} %broadcast_in_dim.6), channel_id=1, replica_groups=mesh['zh'=4,'zl'=2,'y'=4,'x'=4,'sub'=2] {'zh'}, dimensions={0} | all-to-all | bytes 344064 | tf_op jit(solution)/shard_map/all_to_all | solution.py:532
  85.5 0.2 broadcast_in_dim.7
  85.7 21.8 %all_to_all.17 = bf16[32,168,128]{2,1,0:T(8,128)(2,1)S(1)} all-to-all(bf16[32,168,128]{2,1,0:T(8,128)(2,1)S(1)} %broadcast_in_dim.7), channel_id=1, replica_groups=mesh['zh'=4,'zl'=2,'y'=4,'x'=4,'sub'=2] {'zl','y','x'}, dimensions={0} | all-to-all | bytes 2752512 | tf_op jit(solution)/shard_map/all_to_all | solution.py:534
  107.6 4.1 %collective-permute-start.8 = (bf16[2880,128]{1,0:T(8,128)(2,1)S(1)}, bf16[2880,128]{1,0:T(8,128)(2,1)S(1)}, u32[]{:S(2)}, u32[]{:S(2)}) collective-permute-start(bf16[2880,128]{1,0:T(8,128)(2,1)S(1)} %slice.4), channel_id=1, source_target_pairs={{0,1},{1,0},{2,3},{3,2},{4,5},{5,4},{6,7},{7,6},{8,9},{9,8},{10,11... | collective-permute-start | bytes 2211848 | tf_op jit(solution)/shard_map/ppermute | solution.py:32
  111.8 1.8 %collective-permute-done.8.other = bf16[2880,128]{1,0:T(8,128)(2,1)S(1)} collective-permute-done((bf16[2880,128]{1,0:T(8,128)(2,1)S(1)}, bf16[2880,128]{1,0:T(8,128)(2,1)S(1)}, u32[]{:S(2)}, u32[]{:S(2)}) %collective-permute-start.8) | collective-permute-done | bytes 737312 | tf_op jit(solution)/shard_map/ppermute | solution.py:32
  113.6 2.1 %shard_map.150 = (f32[192,576]{1,0:T(8,128)}, f32[192,192]{1,0:T(8,128)}, f32[1536,384]{1,0:T(8,128)}, f32[3,192,384]{2,1,0:T(8,128)}, f32[192,384]{1,0:T(8,128)}) custom-call(s32[1]{0:T(128)} %bitcast.7.core_ref, bf16[5376,128]{1,0:T(8,128)(2,1)S(1)} %bitcast.14, bf16[2880,128]{1,0:T(8,128)(2,1)S(1)} %collective-permute-done.8.other), custom_call_target="tpu_custom_call" | custom-call | flops 2000000000 | bytes 2000000 | tf_op jit(solution)/shard_map/pallas_call | solution.py:510
  (3 shorter events, 0.1 us)
Async XLA Ops:
  0.6 15.2 %collective-permute-start.3 = (bf16[576,384]{1,0:T(8,128)(2,1)}, bf16[576,384]{1,0:T(8,128)(2,1)}, u32[]{:S(2)}, u32[]{:S(2)}) collective-permute-start(bf16[576,384]{1,0:T(8,128)(2,1)} %bitcast.23), channel_id=1, source_target_pairs={{0,1},{1,0},{2,3},{3,2},{4,5},{5,4},{6,7},{7,6},{8,9},{9,8},{10,11... | collective-permute-start | bytes 1327112 | tf_op jit(solution)/shard_map/ppermute | solution.py:32
  4.0 10.7 %collective-permute-start.1 = (s32[1,512]{1,0:T(1,128)}, s32[1,512]{1,0:T(1,128)S(1)}, u32[]{:S(2)}, u32[]{:S(2)}) collective-permute-start(s32[1,512]{1,0:T(1,128)} %bitcast.15), channel_id=1, source_target_pairs={{1,0},{2,1},{3,2},{4,3},{5,4},{6,5},{7,6},{8,7},{9,8},{10,9},{11,1... | collective-permute-start | bytes 6152 | tf_op jit(solution)/shard_map/ppermute | solution.py:28
  5.9 8.8 %collective-permute-start.2 = (s32[1,512]{1,0:T(1,128)}, s32[1,512]{1,0:T(1,128)S(1)}, u32[]{:S(2)}, u32[]{:S(2)}) collective-permute-start(s32[1,512]{1,0:T(1,128)} %bitcast.19), channel_id=1, source_target_pairs={{1,0},{2,1},{3,2},{4,3},{5,4},{6,5},{7,6},{8,7},{9,8},{10,9},{11,1... | collective-permute-start | bytes 6152 | tf_op jit(solution)/shard_map/ppermute | solution.py:28
  7.8 6.9 %collective-permute-start.4 = (bf16[192,384]{1,0:T(8,128)(2,1)}, bf16[192,384]{1,0:T(8,128)(2,1)}, u32[]{:S(2)}, u32[]{:S(2)}) collective-permute-start(bf16[192,384]{1,0:T(8,128)(2,1)} %own_out.1), channel_id=1, source_target_pairs={{0,1},{1,0},{2,3},{3,2},{4,5},{5,4},{6,7},{7,6},{8,9},{9,8},{10,11... | collective-permute-start | bytes 442376 | tf_op jit(solution)/shard_map/ppermute | solution.py:32
  7.9 7.9 %copy-start = (bf16[128,384]{1,0:T(8,128)(2,1)S(1)}, bf16[128,384]{1,0:T(8,128)(2,1)}, u32[]{:S(2)}) copy-start(bf16[128,384]{1,0:T(8,128)(2,1)} %out_grad.3) | copy-start | bytes 294916
  7.9 7.9 %copy-start.1 = (s32[512]{0:T(512)S(1)}, s32[512]{0:T(512)}, u32[]{:S(2)}) copy-start(s32[512]{0:T(512)} %param.15) | copy-start | bytes 6148
  7.9 7.9 %copy-start.2 = (s32[512]{0:T(512)S(1)}, s32[512]{0:T(512)}, u32[]{:S(2)}) copy-start(s32[512]{0:T(512)} %param.16) | copy-start | bytes 6148
  8.0 7.9 %copy-start.4 = (bf16[3,384,192]{1,2,0:T(8,128)(2,1)S(1)}, bf16[3,384,192]{1,2,0:T(8,128)(2,1)}, u32[]{:S(2)}) copy-start(bf16[3,384,192]{1,2,0:T(8,128)(2,1)} %param.13) | copy-start | bytes 1327108
  8.0 7.9 %collective-permute-start = (bf16[192,512]{1,0:T(8,128)(2,1)}, bf16[192,512]{1,0:T(8,128)(2,1)}, u32[]{:S(2)}, u32[]{:S(2)}) collective-permute-start(bf16[192,512]{1,0:T(8,128)(2,1)} %bitcast.25), channel_id=1, source_target_pairs={{1,0},{2,1},{3,2},{4,3},{5,4},{6,5},{7,6},{8,7},{9,8},{10,9},{11,1... | collective-permute-start | bytes 589832 | tf_op jit(solution)/shard_map/ppermute | solution.py:28
  14.0 0.7 copy-start.6
  15.9 1.3 %copy-start.3 = (bf16[1536,384]{1,0:T(8,128)(2,1)S(1)}, bf16[1536,384]{1,0:T(8,128)(2,1)}, u32[]{:S(2)}) copy-start(bf16[1536,384]{1,0:T(8,128)(2,1)} %pool_weight.1) | copy-start | bytes 3538948
  17.1 0.9 copy-start.5
  18.1 0.9 copy-start.7
  28.8 10.7 %collective-permute-start.6 = (bf16[4608,128]{1,0:T(8,128)(2,1)S(1)}, bf16[4608,128]{1,0:T(8,128)(2,1)S(1)}, u32[]{:S(2)}, u32[]{:S(2)}) collective-permute-start(bf16[4608,128]{1,0:T(8,128)(2,1)S(1)} %get-tuple-element.59), channel_id=1, source_target_pairs={{0,1},{1,0},{2,3},{3,2},{4,5},{5,4},{6,7},{7,6},{8,9},{9,8},{10,11... | collective-permute-start | bytes 3538952 | tf_op jit(solution)/shard_map/ppermute | solution.py:32
  28.9 6.9 %collective-permute-start.5 = (bf16[16,192]{1,0:T(8,128)(2,1)S(1)}, bf16[16,192]{1,0:T(8,128)(2,1)S(1)}, u32[]{:S(2)}, u32[]{:S(2)}) collective-permute-start(bf16[16,192]{1,0:T(8,128)(2,1)S(1)} %get-tuple-element.53), channel_id=1, source_target_pairs={{0,1},{1,2},{2,3},{3,4},{4,5},{5,6},{6,7},{7,8},{8,9},{9,10},{10,1... | collective-permute-start | bytes 18440 | tf_op jit(solution)/shard_map/ppermute | solution.py:28
  38.1 1.4 %collective-permute-start.7 = (bf16[576,128]{1,0:T(8,128)(2,1)S(1)}, bf16[576,128]{1,0:T(8,128)(2,1)S(1)}, u32[]{:S(2)}, u32[]{:S(2)}) collective-permute-start(bf16[576,128]{1,0:T(8,128)(2,1)S(1)} %get-tuple-element.61), channel_id=1, source_target_pairs={{0,1},{1,0},{2,3},{3,2},{4,5},{5,4},{6,7},{7,6},{8,9},{9,8},{10,11... | collective-permute-start | bytes 442376 | tf_op jit(solution)/shard_map/ppermute | solution.py:32
  107.6 6.0 %collective-permute-start.8 = (bf16[2880,128]{1,0:T(8,128)(2,1)S(1)}, bf16[2880,128]{1,0:T(8,128)(2,1)S(1)}, u32[]{:S(2)}, u32[]{:S(2)}) collective-permute-start(bf16[2880,128]{1,0:T(8,128)(2,1)S(1)} %slice.4), channel_id=1, source_target_pairs={{0,1},{1,0},{2,3},{3,2},{4,5},{5,4},{6,7},{7,6},{8,9},{9,8},{10,11... | collective-permute-start | bytes 2211848 | tf_op jit(solution)/shard_map/ppermute | solution.py:32

commit v3 on v2

--- a/solution.py
+++ b/solution.py
@@ -137,35 +137,26 @@
         wide[slot, heads * HD :] = mask_rows(window_of, heads)
 
 
-def fine_forward(
-    rows_in,
-    qkv_in,
-    out_in,
-    rows,
-    qkv_weight,
-    out_weight,
-    hidden,
-    mixed,
-    qkv,
-    exponents,
-    inverses,
-    wide,
-    arrived,
-):
-    pairs = ((rows_in, rows), (qkv_in, qkv_weight), (out_in, out_weight))
+def fetch(pairs, arrived):
     copies = [
         pltpu.make_async_copy(source, target, arrived.at[i])
         for i, (source, target) in enumerate(pairs)
     ]
     for copy in copies:
         copy.start()
+    return copies
+
+
+def fine_blocks(
+    first, rows, qkv_weight, out_weight, hidden, mixed, qkv, exponents, inverses, wide, wait
+):
     channels, count = hidden.shape
     heads = channels // HD
     clear_wide(wide, heads, fine_window)
     classes = window_rows(fine_window)
-    copies[0].wait()
-    copies[1].wait()
-    rows_float = rows[...].astype(jnp.float32)
+    wait(0)
+    wait(1)
+    rows_float = rows[:, first * LANES : first * LANES + count].astype(jnp.float32)
     normed, _ = layer_norm(rows_float, 0)
     qkv[...] = bround(tn(qkv_weight[...], bround(normed)))
     for block in range(count // LANES):
@@ -184,8 +175,53 @@
             mixed.at[:, lanes],
             store,
         )
-    copies[2].wait()
+    wait(2)
     hidden[...] = bround(rows_float + tn(out_weight[...], mixed[...]))
+
+
+def fine_first(first_parent, *refs):
+    sources, targets = refs[:5], refs[5:10]
+    hidden, mixed, qkv, exponents, inverses, spill, wide, arrived = refs[10:]
+    rows, qkv_weight, out_weight, parent_index, child_slot = targets
+    copies = fetch(tuple(zip(sources, targets)), arrived)
+    fine_blocks(
+        0,
+        rows,
+        qkv_weight,
+        out_weight,
+        hidden,
+        mixed,
+        qkv,
+        exponents,
+        inverses,
+        wide,
+        lambda i: copies[i].wait(),
+    )
+    copies[3].wait()
+    copies[4].wait()
+    spill[...] = bround(nt(leading_slots(parent_index, child_slot, first_parent), hidden[...]))
+
+
+def fine_rest(*refs):
+    sources, (rows, qkv_weight, out_weight) = refs[:4], refs[4:7]
+    targets = refs[7:11]
+    hidden, mixed, qkv, exponents, inverses, wide, arrived = refs[11:]
+    copies = fetch(tuple(zip(sources, targets)), arrived)
+    fine_blocks(
+        1,
+        rows,
+        qkv_weight,
+        out_weight,
+        hidden,
+        mixed,
+        qkv,
+        exponents,
+        inverses,
+        wide,
+        lambda i: None,
+    )
+    for copy in copies:
+        copy.wait()
 
 
 def leading_slots(parent_index, child_slot, first_parent):
@@ -200,16 +236,36 @@
     return jnp.where(mine, child_slot, -1)
 
 
-def coarse_both(
+def pool(
     first_parent,
-    own_hidden,
+    first_hidden,
+    rest_hidden,
     parent_index,
     child_slot,
-    next_rows,
-    next_parent,
-    next_slot,
-    fine_qkv,
-    fine_out,
+    own_out,
+    other_out,
+    out_grad,
+    children,
+    upward,
+    hidden,
+):
+    owned = out_grad.shape[0]
+    hidden[:, :LANES] = first_hidden[...]
+    hidden[:, LANES:] = rest_hidden[...]
+    slot_of = slot_numbers(parent_index[...], child_slot[...], first_parent, owned)
+    for slot in range(0, SLOTS, 2):
+        both = jnp.concatenate([indicator(slot_of == slot), indicator(slot_of == slot + 1)], 0)
+        pair = bround(nt(hidden[...], both))
+        children[slot] = pair[:, :owned]
+        children[slot + 1] = pair[:, owned:]
+    for half, out_weight in enumerate((own_out, other_out)):
+        upward[half] = bround(nt(out_weight[...], out_grad[...]))
+
+
+def coarse_both(
+    children,
+    upward,
+    spill,
     pool_weight,
     own_qkv,
     other_qkv,
@@ -224,45 +280,21 @@
     coarse_input,
     mixed,
     grads,
-    hidden,
-    next_mixed,
-    wide_next,
     wide_query,
     wide_grad,
 ):
     owned, width = out_grad.shape
-    channels, row_count = own_hidden.shape
+    channels = children.shape[1]
     part = own_out.shape[0]
     heads = part // HD
-    fine_heads = channels // HD
-    clear_wide(wide_next, fine_heads, fine_window)
-    rows_float = next_rows[:, :LANES].astype(jnp.float32)
-    normed, _ = layer_norm(rows_float, 0)
-    fine_attention(
-        bround(tn(fine_qkv[...], bround(normed))),
-        wide_next.at[0],
-        window_rows(fine_window),
-        fine_heads,
-        next_mixed,
-        None,
-    )
-    hidden[:, :row_count] = own_hidden[...]
-    hidden[:, row_count:] = bround(rows_float + tn(fine_out[...], next_mixed[...]))
-    slot_of = slot_numbers(
-        jnp.concatenate([parent_index[...], next_parent[:, :LANES]], 1),
-        jnp.concatenate([child_slot[...], next_slot[:, :LANES]], 1),
-        first_parent,
-        owned,
-    )
+    spill_slot = lax.broadcasted_iota(jnp.int32, (SPILL, owned), 0)
+    last = lax.broadcasted_iota(jnp.int32, (SPILL, owned), 1) == owned - 1
     total = jnp.zeros((owned, width), jnp.float32)
-    for slot in range(0, SLOTS, 2):
-        both = jnp.concatenate([indicator(slot_of == slot), indicator(slot_of == slot + 1)], 0)
-        children = bround(nt(hidden[...], both))
-        for i in range(2):
-            chosen = children[:, i * owned : (i + 1) * owned]
-            pooled[slot + i] = chosen
-            at = (slot + i) * channels
-            total += tn(chosen, pool_weight[at : at + channels])
+    for slot in range(SLOTS):
+        edge = tn(spill[...], indicator(last & (spill_slot == slot)))
+        chosen = children[slot] + bround(edge)
+        pooled[slot] = chosen
+        total += tn(chosen, pool_weight[slot * channels : (slot + 1) * channels])
     parents = bround(total).astype(jnp.float32)
     normed, inverse = layer_norm(parents, 1)
     coarse_input[...] = bround(normed)
@@ -275,7 +307,6 @@
     weights = ((own_qkv, own_out), (other_qkv, other_out))
     for half, (qkv_weight, out_weight) in enumerate(weights):
         qkv = bround(nt(qkv_weight[...], coarse_input[...]))
-        upward = bround(nt(out_weight[...], upstream))
         wide_query[half, part:] = mask_rows(coarse_window, heads)
         spread(wide_query.at[half], scaled(qkv[:part]), heads)
         keys = jnp.concatenate([qkv[part : 2 * part], classes], 0)
@@ -287,7 +318,7 @@
             parts.append((exponent, scale))
             value = qkv[2 * part + head * HD : 2 * part + (head + 1) * HD]
             mixed[half, at] = bround(nn(value, exponent) * scale)
-            weighted = scaled(upward[at]).astype(jnp.float32) * scale
+            weighted = scaled(upward[half, at]).astype(jnp.float32) * scale
             wide_grad[half, at, head * LANES : (head + 1) * LANES] = bround(weighted)
         grad_probs = tn(qkv[2 * part :], wide_grad[half])
         for head in range(heads):
@@ -295,7 +326,7 @@
             back = attend_back(
                 qkv[at[0]],
                 qkv[at[1]],
-                upward[at[0]],
+                upward[half, at[0]],
                 *parts[head],
                 grad_probs[:, head * LANES : (head + 1) * LANES],
             )
@@ -308,8 +339,6 @@
         upstream.astype(jnp.float32) + layer_norm_back(normed, inverse, grad_normed, 1)
     )
     grad_parents[...] = upstream_total
-    spill_slot = lax.broadcasted_iota(jnp.int32, (SPILL, owned), 0)
-    last = lax.broadcasted_iota(jnp.int32, (SPILL, owned), 1) == owned - 1
     edge_total = jnp.zeros((SPILL, channels), jnp.float32)
     for slot in range(SLOTS):
         weight = pool_weight[slot * channels : (slot + 1) * channels]
@@ -321,23 +350,18 @@
 
 def coarse_weights(
     core_ref,
-    first_parent,
-    parent_index,
-    child_slot,
     grad_parents,
     pooled,
-    grad_pooled,
     coarse_input,
     mixed,
     grads,
     out_grad,
-    grad_hidden,
     keep,
     give,
 ):
     core = core_ref[0]
-    owned, width = out_grad.shape
-    channels, row_count = grad_hidden.shape
+    width = out_grad.shape[1]
+    channels = pooled.shape[1]
     part = mixed.shape[1]
     panels = width // LANES
 
@@ -356,11 +380,6 @@
         for step in range(SLOTS // 2):
             grad_pool = nn(pooled[first * (SLOTS // 2) + step], grad_parents[...])
             store(target, base + step * panels * channels, grad_pool)
-    slot_of = slot_numbers(parent_index[...], child_slot[...], first_parent, owned)
-    grad_total = jnp.zeros((channels, row_count), jnp.float32)
-    for slot in range(SLOTS):
-        grad_total += nn(grad_pooled[slot], indicator(slot_of == slot))
-    grad_hidden[...] = bround(grad_total)
 
 
 def fine_back(
@@ -368,52 +387,56 @@
     core_ref,
     first_parent,
     rows,
-    grad_hidden,
+    grad_pooled,
+    parent_index,
+    child_slot,
+    qkv_weight,
+    out_weight,
     exponents,
     inverses,
     qkv,
     mixed,
-    qkv_weight,
-    out_weight,
     *rest,
 ):
     if first_block:
         row_grad, qkv_total, out_total, grads, wide = rest
-        spill_grad = None
     else:
-        spill_grad, parent_index, child_slot, row_rest, qkv_rest, out_rest = rest[:6]
-        row_grad, keep, give, grads, wide = rest[6:]
-    channels, count = grads.shape[0] // 3, grads.shape[1]
+        spill_grad, row_rest, qkv_rest, out_rest = rest[:4]
+        row_grad, keep, give, grads, wide = rest[4:]
+    channels, count = mixed.shape
+    owned = grad_pooled.shape[2]
     heads = channels // HD
     span = slice(first_block * LANES, first_block * LANES + count)
     normed, inverse = layer_norm(rows[:, span].astype(jnp.float32), 0)
-    upstream = grad_hidden[:, span]
-    if spill_grad is not None:
+    slot_of = slot_numbers(parent_index[:, span], child_slot[:, span], first_parent, owned)
+    upstream = jnp.zeros((channels, count), jnp.float32)
+    for slot in range(SLOTS):
+        upstream += nn(grad_pooled[slot], indicator(slot_of == slot))
+    if not first_block:
         leading = leading_slots(parent_index, child_slot, first_parent)
-        upstream = bround(upstream.astype(jnp.float32) + tn(spill_grad[...], leading))
+        upstream += tn(spill_grad[...], leading)
+    upstream = bround(upstream)
     upward = bround(nn(out_weight[...], upstream))
     wide[...] = jnp.zeros(wide.shape, wide.dtype)
     for block in range(count // LANES):
         lanes = slice(block * LANES, (block + 1) * LANES)
-        whole = first_block + block
-        outer = slice(whole * LANES, (whole + 1) * LANES)
         grad_rows = wide.at[block % wide.shape[0]]
         scales = [
-            inverses[whole * heads + head : whole * heads + head + 1] for head in range(heads)
+            inverses[block * heads + head : block * heads + head + 1] for head in range(heads)
         ]
         for head in range(heads):
             at = slice(head * HD, (head + 1) * HD)
             weighted = scaled(upward[at, lanes]).astype(jnp.float32) * scales[head]
             grad_rows[at, head * LANES : (head + 1) * LANES] = bround(weighted)
-        grad_probs = tn(qkv[2 * channels :, outer], grad_rows[...])
+        grad_probs = tn(qkv[2 * channels :, lanes], grad_rows[...])
         for head in range(heads):
             at = [slice(i * channels + head * HD, i * channels + (head + 1) * HD) for i in range(3)]
             out = slice(head * LANES, (head + 1) * LANES)
             back = attend_back(
-                qkv[at[0], outer],
-                qkv[at[1], outer],
+                qkv[at[0], lanes],
+                qkv[at[1], lanes],
                 upward[at[0], lanes],
-                exponents[whole, :, out],
+                exponents[block, :, out],
                 scales[head],
                 grad_probs[:, out],
             )
@@ -422,7 +445,7 @@
     grad_normed = nn(qkv_weight[...], grads[...])
     total = upstream.astype(jnp.float32) + layer_norm_back(normed, inverse, grad_normed, 0)
     grad_qkv = nt(bround(normed), grads[...])
-    grad_out = nt(mixed[:, span], upstream)
+    grad_out = nt(mixed[...], upstream)
     if first_block:
         row_grad[...] = bround(total)
         qkv_total[...] = grad_qkv
@@ -442,6 +465,12 @@
         at = slice(i * channels, (i + 1) * channels)
         keep[at] = jnp.where(core == 0, panels[i], panels[half + i])
         give[at] = jnp.where(core == 0, panels[half + i], panels[i])
+
+
+def fine_and_weights(core_ref, first_parent, *refs):
+    fine_in, weight_in, refs = refs[:10], refs[10:16], refs[16:]
+    fine_back(1, core_ref, first_parent, *fine_in, *refs[:3], *refs[5:])
+    coarse_weights(core_ref, *weight_in, *refs[3:5])
 
 
 def merge(keep, got, fine_keep, fine_got, total):
@@ -566,31 +595,66 @@
     own_qkv = coarse_qkv_weight.transpose(0, 2, 1).reshape(3 * part, width)
     other_qkv = swap_cores(own_qkv)
     other_out = swap_cores(coarse_out_weight)
-    next_rows = passed_along(rows, -1)
-    next_parent = passed_along(parent_row, -1)
-    next_slot = passed_along(slot_row, -1)
     wide_rows = heads * LANES
-    rows, fine_qkv, fine_out, hidden, mixed_fine, qkv, exponents, inverses = call(
-        fine_forward,
-        [
-            ((channels, row_count), bf16),
-            ((channels, 3 * channels), bf16),
-            ((channels, channels), bf16),
-            ((channels, row_count), bf16),
-            ((channels, row_count), bf16),
-            ((3 * channels, row_count), bf16),
-            ((blocks, LANES, wide_rows), bf16),
-            ((blocks * heads, LANES), f32),
-        ],
+
+    def in_hbm(*arrays):
+        return [pltpu.with_memory_space_constraint(array, pltpu.HBM) for array in arrays]
+
+    def like(*arrays):
+        return [(array.shape, array.dtype) for array in arrays]
+
+    def block_outs(count):
+        return [
+            ((channels, count * LANES), bf16),
+            ((channels, count * LANES), bf16),
+            ((3 * channels, count * LANES), bf16),
+            ((count, LANES, wide_rows), bf16),
+            ((count * heads, LANES), f32),
+        ]
+
+    sources = (rows, qkv_weight, out_weight, parent_row, slot_row)
+    first = call(
+        fine_first,
+        like(*sources) + block_outs(1) + [((SPILL, channels), bf16)],
+        [(1, channels + SPILL, wide_rows)],
+        first_parent,
+        *in_hbm(*sources),
+        hbm=5,
+        copies=5,
+        micros=3,
+    )
+    rows, fine_qkv, fine_out, parent_row, slot_row = first[:5]
+    hidden_first, *saved_first, spill = first[5:]
+    spill_in = passed_along(spill, -1)
+    sources = (pool_weight, own_qkv, coarse_out_weight, out_grad)
+    second = call(
+        fine_rest,
+        like(*sources) + block_outs(blocks - 1),
         [(2, channels + SPILL, wide_rows)],
-        *(
-            pltpu.with_memory_space_constraint(array, pltpu.HBM)
-            for array in (rows, qkv_weight, out_weight)
-        ),
+        *in_hbm(*sources),
+        rows,
+        fine_qkv,
+        fine_out,
         scalars=0,
-        hbm=3,
-        copies=3,
-        micros=4,
+        hbm=4,
+        copies=4,
+        micros=2,
+    )
+    pool_weight, own_qkv, own_out, out_grad = second[:4]
+    hidden_rest, *saved_rest = second[4:]
+    children, upward = call(
+        pool,
+        [((SLOTS, channels, owned), bf16), ((2, part, owned), bf16)],
+        [(channels, row_count)],
+        first_parent,
+        hidden_first,
+        hidden_rest,
+        parent_row,
+        slot_row,
+        own_out,
+        other_out,
+        out_grad,
+        micros=2,
     )
     coarse_rows, spill_grad, grad_parents, pooled, grad_pooled, coarse_input, mixed, grads = call(
         coarse_both,
@@ -605,78 +669,49 @@
             ((2, 3 * part, owned), bf16),
         ],
         [
-            (channels, row_count + LANES),
-            (channels, LANES),
-            (1, channels + SPILL, wide_rows),
             (2, part + SPILL, coarse_heads * LANES),
             (2, part, coarse_heads * LANES),
         ],
-        first_parent,
-        hidden,
-        parent_row,
-        slot_row,
-        next_rows,
-        next_parent,
-        next_slot,
-        fine_qkv,
-        fine_out,
+        children,
+        upward,
+        spill_in,
         pool_weight,
         own_qkv,
         other_qkv,
-        coarse_out_weight,
+        own_out,
         other_out,
         out_grad,
-        micros=9,
+        scalars=0,
+        micros=8,
     )
     spill_back = passed_along(spill_grad, 1)
-    grad_hidden, keep, give = call(
-        coarse_weights,
+    shared = (core, first_parent, rows, grad_pooled, parent_row, slot_row, fine_qkv, fine_out)
+    rest_count = row_count - LANES
+    row_rest, qkv_rest, out_rest, keep, give = call(
+        fine_and_weights,
         [
-            ((channels, row_count), bf16),
+            ((channels, rest_count), bf16),
+            ((channels, 3 * channels), f32),
+            ((channels, channels), f32),
             ((coarse_count + pool_count, LANES), bf16),
             ((coarse_count + pool_count, LANES), bf16),
         ],
-        [],
-        core,
-        first_parent,
-        parent_row,
-        slot_row,
+        [(3 * channels, rest_count), (2, channels, wide_rows)],
+        *shared,
+        *saved_rest[2:],
+        saved_rest[1],
+        saved_rest[0],
         grad_parents,
         pooled,
-        grad_pooled,
         coarse_input,
         mixed,
         grads,
         out_grad,
         scalars=2,
-        micros=1e-4,
-    )
+        micros=5,
+    )
+    spill_back, give = lax.optimization_barrier((spill_back, give))
     got = swap_cores(give)
-    shared = (
-        core,
-        first_parent,
-        rows,
-        grad_hidden,
-        exponents,
-        inverses,
-        qkv,
-        mixed_fine,
-        fine_qkv,
-        fine_out,
-    )
-    rest_count = row_count - LANES
-    row_rest, qkv_rest, out_rest = call(
-        functools.partial(fine_back, 1),
-        [
-            ((channels, rest_count), bf16),
-            ((channels, 3 * channels), f32),
-            ((channels, channels), f32),
-        ],
-        [(3 * channels, rest_count), (2, channels, wide_rows)],
-        *shared,
-        scalars=2,
-        micros=1e-4,
-    )
     row_grad, fine_keep, fine_give = call(
         functools.partial(fine_back, 0),
         [
@@ -686,9 +721,10 @@
         ],
         [(3 * channels, LANES), (1, channels, wide_rows)],
         *shared,
+        *saved_first[2:],
+        saved_first[1],
+        saved_first[0],
         spill_back,
-        parent_row,
-        slot_row,
         row_rest,
         qkv_rest,
         out_rest,

time: 116 us -> 107 us (0.922)
  starting transfers between devices: 17.9 us -> 13.9 us
  local copies, waits for them, and re-layouts: 4.04 us -> 0.25 us
  waiting for transfers between devices: 4.35 us -> 2.86 us
    ppermute x4 -> x2, starting transfers between devices: 10.2 us -> 5.55 us  [passed_along(): return lax.ppermute(shard, AXES, pairs)]
    unnamed x16 -> x0, local copies, waits for them, and re-layouts: 3.79 us -> none
    pallas_call x7 -> x8, Pallas kernels: 21.1 us -> 21.7 us  [call(): pl.pallas_call(kernel, out_shape=[jax.ShapeDtypeStruct(shape, dtype) for...]
  transfers between devices with their start and end apart: 9 -> 7, of which waited for: 3 -> 2; matrix products, arithmetic and copies ran while one was open for 0% -> 0% of each run, Pallas kernels for 8% -> 11%
where the time goes in v3:
time: 107 us
  blocking collectives  67.5 us (63%)
  Pallas kernels  21.7 us (20%)
  starting transfers between devices  13.9 us (13%)
  waiting for transfers between devices  2.86 us (3%)
    all_to_all x1, blocking collectives, sum_over_chips(): plane = lax.all_to_all(parts, NEAR, 0, 0, tiled=True)  30.2 us
    all_to_all x1, blocking collectives, sum_over_chips(): return lax.all_to_all(copies, NEAR, 0, 0, tiled=True)  22.4 us
    pallas_call x8, Pallas kernels, call(): pl.pallas_call(kernel, out_shape=[jax.ShapeDtypeStruct(shape, dtype) for...  21.7 us
    all_to_all x1, blocking collectives, sum_over_chips(): slab = float_sum(lax.all_to_all(copies, 'zh', 0, 0, tiled=True))  14.9 us
    ppermute x5, starting transfers between devices, swap_cores(): return lax.ppermute(shard, 'sub', [(0, 1), (1, 0)])  8.33 us
    ppermute x2, starting transfers between devices, passed_along(): return lax.ppermute(shard, AXES, pairs)  5.55 us
    ppermute x5, waiting for transfers between devices, swap_cores(): return lax.ppermute(shard, 'sub', [(0, 1), (1, 0)])  2.86 us
  transfers between devices with their start and end apart: 7, of which 2 were waited for; matrix products, arithmetic and copies ran while one was open for 0% of the time, Pallas kernels for 11%

profile of v3, /device:TPU:1, one launch (start us, length us, event | category | flops | bytes accessed | tf_op | source)
XLA Modules:
  0.0 107.2 jit_solution(17676800646555913463)
XLA Ops:
  0.6 3.3 %collective-permute-start = (bf16[192,384]{1,0:T(8,128)(2,1)}, bf16[192,384]{1,0:T(8,128)(2,1)S(1)}, u32[]{:S(2)}, u32[]{:S(2)}) collective-permute-start(bf16[192,384]{1,0:T(8,128)(2,1)} %refs_2_.3), channel_id=1, source_target_pairs={{0,1},{1,0},{2,3},{3,2},{4,5},{5,4},{6,7},{7,6},{8,9},{9,8},{10,11... | collective-permute-start | bytes 442376 | tf_op jit(solution)/shard_map/ppermute | solution.py:32
  4.0 0.1 collective-permute-start.2
  4.1 2.4 %shard_map.144 = (bf16[192,512]{1,0:T(8,128)(2,1)S(1)}, bf16[192,576]{1,0:T(8,128)(2,1)S(1)}, bf16[192,192]{1,0:T(8,128)(2,1)S(1)}, s32[1,512]{1,0:T(1,128)S(1)}...) custom-call(s32[1]{0:T(128)} %bitcast.first_parent, ...), custom_call_target="tpu_custom_call" | custom-call | flops 3000000000 | bytes 3000000 | tf_op jit(solution)/shard_map/pallas_call | solution.py:539
  6.5 2.3 %collective-permute-start.1 = (bf16[16,192]{1,0:T(8,128)(2,1)S(1)}, bf16[16,192]{1,0:T(8,128)(2,1)S(1)}, u32[]{:S(2)}, u32[]{:S(2)}) collective-permute-start(bf16[16,192]{1,0:T(8,128)(2,1)S(1)} %get-tuple-element.63), channel_id=1, source_target_pairs={{1,0},{2,1},{3,2},{4,3},{5,4},{6,5},{7,6},{8,7},{9,8},{10,9},{11,1... | collective-permute-start | bytes 18440 | tf_op jit(solution)/shard_map/ppermute | solution.py:28
  8.8 2.7 %shard_map.145 = (bf16[1536,384]{1,0:T(8,128)(2,1)S(1)}, bf16[576,384]{1,0:T(8,128)(2,1)S(1)}, bf16[192,384]{1,0:T(8,128)(2,1)S(1)}, bf16[128,384]{1,0:T(8,128)(...) custom-call(bf16[1536,384]{1,0:T(8,128)(2,1)} %refs_0_.1, ...), custom_call_target="tpu_custom_call" | custom-call | flops 2000000000 | bytes 2000000 | tf_op jit(solution)/shard_map/pallas_call | solution.py:539
  11.5 0.0 collective-permute-done.other_out
  11.5 0.6 shard_map.146
  12.1 0.0 collective-permute-done.1.spill
  12.1 0.0 collective-permute-done.2.other_qkv
  12.1 7.0 %shard_map.147 = (bf16[128,384]{1,0:T(8,128)(2,1)}, bf16[16,192]{1,0:T(8,128)(2,1)S(1)}, bf16[128,384]{1,0:T(8,128)(2,1)S(1)}, bf16[8,192,128]{2,1,0:T(8,128)(2,...) custom-call(bf16[8,192,128]{2,1,0:T(8,128)(2,1)S(1)} %get-tuple-elem, ...), custom_call_target="tpu_custom_call" | custom-call | flops 8000000000 | bytes 8000000 | tf_op jit(solution)/shard_map/pallas_call | solution.py:539
  19.1 3.2 %collective-permute-start.3 = (bf16[16,192]{1,0:T(8,128)(2,1)S(1)}, bf16[16,192]{1,0:T(8,128)(2,1)S(1)}, u32[]{:S(2)}, u32[]{:S(2)}) collective-permute-start(bf16[16,192]{1,0:T(8,128)(2,1)S(1)} %get-tuple-element.72), channel_id=1, source_target_pairs={{0,1},{1,2},{2,3},{3,4},{4,5},{5,6},{6,7},{7,8},{8,9},{9,10},{10,1... | collective-permute-start | bytes 18440 | tf_op jit(solution)/shard_map/ppermute | solution.py:28
  22.3 4.2 %shard_map.148 = (bf16[192,384]{1,0:T(8,128)(2,1)S(1)}, f32[192,576]{1,0:T(8,128)S(1)}, f32[192,192]{1,0:T(8,128)S(1)}, bf16[4608,128]{1,0:T(8,128)(2,1)S(1)}, bf16[4608,128]{1,0:T(8,128)(2,1)S(1)}) custom-call(s32[1]{0:T(128)} %bitcast.7.core_ref, s32[1]{0:T(128)} %bitcast.first_parent, bf16[192,512]{1,0:T(8,128)(2,1)S(1)} %get-tuple-element.53.refs_4_.refs_0_.rows, ...), custom_call_target="tpu_custom_call" | custom-call | flops 5000000000 | bytes 5000000 | tf_op jit(solution)/shard_map/pallas_call | solution.py:539
  26.6 0.0 collective-permute-done.3.rest_0_
  26.6 0.3 collective-permute-start.4
  26.9 2.4 %shard_map.149 = (bf16[192,512]{1,0:T(8,128)(2,1)}, bf16[576,128]{1,0:T(8,128)(2,1)S(1)}, bf16[576,128]{1,0:T(8,128)(2,1)S(1)}) custom-call(s32[1]{0:T(128)} %bitcast.7.core_ref, s32[1]{0:T(128)} %bitcast.first_parent, bf16[192,512]{1,0:T(8,128)(2,1)S(1)} %get-tuple-element.53.refs_4_.refs_0_.rows, ...), custom_call_target="tpu_custom_call" | custom-call | flops 2000000000 | bytes 2000000 | tf_op jit(solution)/shard_map/pallas_call | solution.py:539
  29.3 0.5 collective-permute-start.5
  29.8 1.0 collective-permute-done.5.fine_got
  30.8 0.0 collective-permute-done.4.got
  30.8 0.3 shard_map.150
  31.1 30.2 %all_to_all.15 = bf16[32,168,128]{2,1,0:T(8,128)(2,1)S(1)} all-to-all(bf16[32,168,128]{2,1,0:T(8,128)(2,1)S(1)} %bitcast.12), channel_id=1, replica_groups=mesh['zh'=4,'zl'=2,'y'=4,'x'=4,'sub'=2] {'zl','y','x'}, dimensions={0} | all-to-all | bytes 2752512 | tf_op jit(solution)/shard_map/all_to_all | solution.py:558
  61.3 0.2 reduce_sum.24
  61.5 14.9 %all_to_all.16 = bf16[4,168,128]{2,1,0:T(8,128)(2,1)S(1)} all-to-all(bf16[4,168,128]{2,1,0:T(8,128)(2,1)S(1)} %broadcast_in_dim.6), channel_id=1, replica_groups=mesh['zh'=4,'zl'=2,'y'=4,'x'=4,'sub'=2] {'zh'}, dimensions={0} | all-to-all | bytes 344064 | tf_op jit(solution)/shard_map/all_to_all | solution.py:561
  76.4 0.2 broadcast_in_dim.7
  76.6 22.4 %all_to_all.17 = bf16[32,168,128]{2,1,0:T(8,128)(2,1)S(1)} all-to-all(bf16[32,168,128]{2,1,0:T(8,128)(2,1)S(1)} %broadcast_in_dim.7), channel_id=1, replica_groups=mesh['zh'=4,'zl'=2,'y'=4,'x'=4,'sub'=2] {'zl','y','x'}, dimensions={0} | all-to-all | bytes 2752512 | tf_op jit(solution)/shard_map/all_to_all | solution.py:563
  99.1 4.1 %collective-permute-start.6 = (bf16[2880,128]{1,0:T(8,128)(2,1)S(1)}, bf16[2880,128]{1,0:T(8,128)(2,1)S(1)}, u32[]{:S(2)}, u32[]{:S(2)}) collective-permute-start(bf16[2880,128]{1,0:T(8,128)(2,1)S(1)} %slice.4), channel_id=1, source_target_pairs={{0,1},{1,0},{2,3},{3,2},{4,5},{5,4},{6,7},{7,6},{8,9},{9,8},{10,11... | collective-permute-start | bytes 2211848 | tf_op jit(solution)/shard_map/ppermute | solution.py:32
  103.2 1.8 %collective-permute-done.6.other = bf16[2880,128]{1,0:T(8,128)(2,1)S(1)} collective-permute-done((bf16[2880,128]{1,0:T(8,128)(2,1)S(1)}, bf16[2880,128]{1,0:T(8,128)(2,1)S(1)}, u32[]{:S(2)}, u32[]{:S(2)}) %collective-permute-start.6) | collective-permute-done | bytes 737312 | tf_op jit(solution)/shard_map/ppermute | solution.py:32
  105.1 2.1 %shard_map.151 = (f32[192,576]{1,0:T(8,128)}, f32[192,192]{1,0:T(8,128)}, f32[1536,384]{1,0:T(8,128)}, f32[3,192,384]{2,1,0:T(8,128)}, f32[192,384]{1,0:T(8,128)}) custom-call(s32[1]{0:T(128)} %bitcast.7.core_ref, bf16[5376,128]{1,0:T(8,128)(2,1)S(1)} %bitcast.14, bf16[2880,128]{1,0:T(8,128)(2,1)S(1)} %collective-permute-done.6.other), custom_call_target="tpu_custom_call" | custom-call | flops 2000000000 | bytes 2000000 | tf_op jit(solution)/shard_map/pallas_call | solution.py:539
  (3 shorter events, 0.1 us)
Async XLA Ops:
  0.6 10.8 %collective-permute-start = (bf16[192,384]{1,0:T(8,128)(2,1)}, bf16[192,384]{1,0:T(8,128)(2,1)S(1)}, u32[]{:S(2)}, u32[]{:S(2)}) collective-permute-start(bf16[192,384]{1,0:T(8,128)(2,1)} %refs_2_.3), channel_id=1, source_target_pairs={{0,1},{1,0},{2,3},{3,2},{4,5},{5,4},{6,7},{7,6},{8,9},{9,8},{10,11... | collective-permute-start | bytes 442376 | tf_op jit(solution)/shard_map/ppermute | solution.py:32
  4.0 8.1 %collective-permute-start.2 = (bf16[576,384]{1,0:T(8,128)(2,1)}, bf16[576,384]{1,0:T(8,128)(2,1)S(1)}, u32[]{:S(2)}, u32[]{:S(2)}) collective-permute-start(bf16[576,384]{1,0:T(8,128)(2,1)} %bitcast.15), channel_id=1, source_target_pairs={{0,1},{1,0},{2,3},{3,2},{4,5},{5,4},{6,7},{7,6},{8,9},{9,8},{10,11... | collective-permute-start | bytes 1327112 | tf_op jit(solution)/shard_map/ppermute | solution.py:32
  6.5 5.6 %collective-permute-start.1 = (bf16[16,192]{1,0:T(8,128)(2,1)S(1)}, bf16[16,192]{1,0:T(8,128)(2,1)S(1)}, u32[]{:S(2)}, u32[]{:S(2)}) collective-permute-start(bf16[16,192]{1,0:T(8,128)(2,1)S(1)} %get-tuple-element.63), channel_id=1, source_target_pairs={{1,0},{2,1},{3,2},{4,3},{5,4},{6,5},{7,6},{8,7},{9,8},{10,9},{11,1... | collective-permute-start | bytes 18440 | tf_op jit(solution)/shard_map/ppermute | solution.py:28
  19.1 7.5 %collective-permute-start.3 = (bf16[16,192]{1,0:T(8,128)(2,1)S(1)}, bf16[16,192]{1,0:T(8,128)(2,1)S(1)}, u32[]{:S(2)}, u32[]{:S(2)}) collective-permute-start(bf16[16,192]{1,0:T(8,128)(2,1)S(1)} %get-tuple-element.72), channel_id=1, source_target_pairs={{0,1},{1,2},{2,3},{3,4},{4,5},{5,6},{6,7},{7,8},{8,9},{9,10},{10,1... | collective-permute-start | bytes 18440 | tf_op jit(solution)/shard_map/ppermute | solution.py:28
  26.6 4.2 %collective-permute-start.4 = (bf16[4608,128]{1,0:T(8,128)(2,1)S(1)}, bf16[4608,128]{1,0:T(8,128)(2,1)S(1)}, u32[]{:S(2)}, u32[]{:S(2)}) collective-permute-start(bf16[4608,128]{1,0:T(8,128)(2,1)S(1)} %get-tuple-element.89), channel_id=1, source_target_pairs={{0,1},{1,0},{2,3},{3,2},{4,5},{5,4},{6,7},{7,6},{8,9},{9,8},{10,11... | collective-permute-start | bytes 3538952 | tf_op jit(solution)/shard_map/ppermute | solution.py:32
  29.3 1.5 %collective-permute-start.5 = (bf16[576,128]{1,0:T(8,128)(2,1)S(1)}, bf16[576,128]{1,0:T(8,128)(2,1)S(1)}, u32[]{:S(2)}, u32[]{:S(2)}) collective-permute-start(bf16[576,128]{1,0:T(8,128)(2,1)S(1)} %get-tuple-element.91), channel_id=1, source_target_pairs={{0,1},{1,0},{2,3},{3,2},{4,5},{5,4},{6,7},{7,6},{8,9},{9,8},{10,11... | collective-permute-start | bytes 442376 | tf_op jit(solution)/shard_map/ppermute | solution.py:32
  99.1 6.0 %collective-permute-start.6 = (bf16[2880,128]{1,0:T(8,128)(2,1)S(1)}, bf16[2880,128]{1,0:T(8,128)(2,1)S(1)}, u32[]{:S(2)}, u32[]{:S(2)}) collective-permute-start(bf16[2880,128]{1,0:T(8,128)(2,1)S(1)} %slice.4), channel_id=1, source_target_pairs={{0,1},{1,0},{2,3},{3,2},{4,5},{5,4},{6,7},{7,6},{8,9},{9,8},{10,11... | collective-permute-start | bytes 2211848 | tf_op jit(solution)/shard_map/ppermute | solution.py:32

commit v4 on v3

--- a/solution.py
+++ b/solution.py
@@ -245,8 +245,10 @@
     own_out,
     other_out,
     out_grad,
+    pool_weight,
     children,
     upward,
+    partial,
     hidden,
 ):
     owned = out_grad.shape[0]
@@ -258,12 +260,17 @@
         pair = bround(nt(hidden[...], both))
         children[slot] = pair[:, :owned]
         children[slot + 1] = pair[:, owned:]
+    channels = hidden.shape[0]
+    total = jnp.zeros(partial.shape, jnp.float32)
+    for slot in range(SLOTS):
+        total += tn(children[slot], pool_weight[slot * channels : (slot + 1) * channels])
+    partial[...] = total
     for half, out_weight in enumerate((own_out, other_out)):
         upward[half] = bround(nt(out_weight[...], out_grad[...]))
 
 
 def coarse_both(
-    children,
+    partial,
     upward,
     spill,
     pool_weight,
@@ -275,7 +282,6 @@
     coarse_rows,
     spill_grad,
     grad_parents,
-    pooled,
     grad_pooled,
     coarse_input,
     mixed,
@@ -284,85 +290,100 @@
     wide_grad,
 ):
     owned, width = out_grad.shape
-    channels = children.shape[1]
+    channels = spill.shape[1]
     part = own_out.shape[0]
     heads = part // HD
-    spill_slot = lax.broadcasted_iota(jnp.int32, (SPILL, owned), 0)
-    last = lax.broadcasted_iota(jnp.int32, (SPILL, owned), 1) == owned - 1
-    total = jnp.zeros((owned, width), jnp.float32)
+    halves = range(2)
+    qkv_weights, out_weights = (own_qkv, other_qkv), (own_out, other_out)
+    for wide in (wide_query, wide_grad):
+        wide[...] = jnp.zeros(wide.shape, wide.dtype)
+    for half in halves:
+        wide_query[half, part:] = mask_rows(coarse_window, heads)
+    spill_row = lax.broadcasted_iota(jnp.int32, (SPILL, channels), 0)
+    late = jnp.zeros((SPILL, width), jnp.float32)
     for slot in range(SLOTS):
-        edge = tn(spill[...], indicator(last & (spill_slot == slot)))
-        chosen = children[slot] + bround(edge)
-        pooled[slot] = chosen
-        total += tn(chosen, pool_weight[slot * channels : (slot + 1) * channels])
-    parents = bround(total).astype(jnp.float32)
+        chosen = jnp.where(spill_row == slot, spill[...], jnp.zeros_like(spill))
+        late += nn(chosen, pool_weight[slot * channels : (slot + 1) * channels])
+    late = jnp.sum(late, 0, keepdims=True)
+    at_last = lax.broadcasted_iota(jnp.int32, (owned, width), 0) == owned - 1
+    parents = bround(partial[...] + jnp.where(at_last, late, 0.0)).astype(jnp.float32)
     normed, inverse = layer_norm(parents, 1)
     coarse_input[...] = bround(normed)
     upstream = out_grad[...]
     classes = window_rows(coarse_window)
-    grad_normed = jnp.zeros((owned, width), jnp.float32)
-    summed = jnp.zeros((owned, width), jnp.float32)
-    for wide in (wide_query, wide_grad):
-        wide[...] = jnp.zeros(wide.shape, wide.dtype)
-    weights = ((own_qkv, own_out), (other_qkv, other_out))
-    for half, (qkv_weight, out_weight) in enumerate(weights):
-        qkv = bround(nt(qkv_weight[...], coarse_input[...]))
-        wide_query[half, part:] = mask_rows(coarse_window, heads)
-        spread(wide_query.at[half], scaled(qkv[:part]), heads)
-        keys = jnp.concatenate([qkv[part : 2 * part], classes], 0)
-        scores = tn(keys, wide_query[half])
-        parts = []
+    qkvs = [bround(nt(qkv_weights[half][...], coarse_input[...])) for half in halves]
+    for half in halves:
+        spread(wide_query.at[half], scaled(qkvs[half][:part]), heads)
+    scores = [
+        tn(jnp.concatenate([qkvs[half][part : 2 * part], classes], 0), wide_query[half])
+        for half in halves
+    ]
+    parts = {}
+    for half in halves:
         for head in range(heads):
             at = slice(head * HD, (head + 1) * HD)
-            exponent, scale = softmax_parts(scores[:, head * LANES : (head + 1) * LANES])
-            parts.append((exponent, scale))
-            value = qkv[2 * part + head * HD : 2 * part + (head + 1) * HD]
+            lanes = slice(head * LANES, (head + 1) * LANES)
+            exponent, scale = softmax_parts(scores[half][:, lanes])
+            parts[half, head] = (exponent, scale)
+            value = qkvs[half][2 * part + head * HD : 2 * part + (head + 1) * HD]
             mixed[half, at] = bround(nn(value, exponent) * scale)
             weighted = scaled(upward[half, at]).astype(jnp.float32) * scale
-            wide_grad[half, at, head * LANES : (head + 1) * LANES] = bround(weighted)
-        grad_probs = tn(qkv[2 * part :], wide_grad[half])
+            wide_grad[half, at, lanes] = bround(weighted)
+    grad_probs = [tn(qkvs[half][2 * part :], wide_grad[half]) for half in halves]
+    for half in halves:
         for head in range(heads):
             at = [slice(i * part + head * HD, i * part + (head + 1) * HD) for i in range(3)]
             back = attend_back(
-                qkv[at[0]],
-                qkv[at[1]],
+                qkvs[half][at[0]],
+                qkvs[half][at[1]],
                 upward[half, at[0]],
-                *parts[head],
-                grad_probs[:, head * LANES : (head + 1) * LANES],
+                *parts[half, head],
+                grad_probs[half][:, head * LANES : (head + 1) * LANES],
             )
             for which in range(3):
                 grads[half, at[which]] = back[which]
-        summed += tn(mixed[half], out_weight[...])
-        grad_normed += tn(grads[half], qkv_weight[...])
-    coarse_rows[...] = bround(parents + summed)
+    grad_normed = sum(tn(grads[half], qkv_weights[half][...]) for half in halves)
     upstream_total = bround(
         upstream.astype(jnp.float32) + layer_norm_back(normed, inverse, grad_normed, 1)
     )
     grad_parents[...] = upstream_total
+    grad_all = bround(nt(pool_weight[...], upstream_total))
+    last = lax.broadcasted_iota(jnp.int32, (SPILL, owned), 1) == owned - 1
+    spill_slot = lax.broadcasted_iota(jnp.int32, (SPILL, owned), 0)
     edge_total = jnp.zeros((SPILL, channels), jnp.float32)
     for slot in range(SLOTS):
-        weight = pool_weight[slot * channels : (slot + 1) * channels]
-        grad_slot = bround(nt(weight, upstream_total))
-        grad_pooled[slot] = grad_slot
+        grad_slot = grad_all[slot * channels : (slot + 1) * channels]
+        grad_pooled[slot // 2, :, slot % 2 * owned : (slot % 2 + 1) * owned] = grad_slot
         edge_total += nt(indicator(last & (spill_slot == slot)), grad_slot)
     spill_grad[...] = bround(edge_total)
+    summed = sum(tn(mixed[half], out_weights[half][...]) for half in halves)
+    coarse_rows[...] = bround(parents + summed)
 
 
 def coarse_weights(
     core_ref,
     grad_parents,
-    pooled,
+    children,
+    spill,
     coarse_input,
     mixed,
     grads,
     out_grad,
     keep,
     give,
+    pooled,
 ):
     core = core_ref[0]
     width = out_grad.shape[1]
-    channels = pooled.shape[1]
+    owned, channels = out_grad.shape[0], pooled.shape[1]
     part = mixed.shape[1]
+    last = lax.broadcasted_iota(jnp.int32, (SPILL, owned), 1) == owned - 1
+    spill_slot = lax.broadcasted_iota(jnp.int32, (SPILL, owned), 0)
+    for slot in range(0, SLOTS, 2):
+        edges = [indicator(last & (spill_slot == at)) for at in (slot, slot + 1)]
+        edge = bround(tn(spill[...], jnp.concatenate(edges, 1)))
+        pooled[slot] = children[slot] + edge[:, :owned]
+        pooled[slot + 1] = children[slot + 1] + edge[:, owned:]
     panels = width // LANES
 
     def store(target, start, value):
@@ -404,14 +425,15 @@
         spill_grad, row_rest, qkv_rest, out_rest = rest[:4]
         row_grad, keep, give, grads, wide = rest[4:]
     channels, count = mixed.shape
-    owned = grad_pooled.shape[2]
+    owned = grad_pooled.shape[2] // 2
     heads = channels // HD
     span = slice(first_block * LANES, first_block * LANES + count)
     normed, inverse = layer_norm(rows[:, span].astype(jnp.float32), 0)
     slot_of = slot_numbers(parent_index[:, span], child_slot[:, span], first_parent, owned)
     upstream = jnp.zeros((channels, count), jnp.float32)
-    for slot in range(SLOTS):
-        upstream += nn(grad_pooled[slot], indicator(slot_of == slot))
+    for slot in range(0, SLOTS, 2):
+        both = jnp.concatenate([indicator(slot_of == slot), indicator(slot_of == slot + 1)], 0)
+        upstream += nn(grad_pooled[slot // 2], both)
     if not first_block:
         leading = leading_slots(parent_index, child_slot, first_parent)
         upstream += tn(spill_grad[...], leading)
@@ -468,9 +490,9 @@
 
 
 def fine_and_weights(core_ref, first_parent, *refs):
-    fine_in, weight_in, refs = refs[:10], refs[10:16], refs[16:]
-    fine_back(1, core_ref, first_parent, *fine_in, *refs[:3], *refs[5:])
-    coarse_weights(core_ref, *weight_in, *refs[3:5])
+    fine_in, weight_in, refs = refs[:10], refs[10:17], refs[17:]
+    fine_back(1, core_ref, first_parent, *fine_in, *refs[:3], *refs[5:7])
+    coarse_weights(core_ref, *weight_in, *refs[3:5], *refs[7:])
 
 
 def merge(keep, got, fine_keep, fine_got, total):
@@ -481,49 +503,71 @@
     total[first + second :] = jnp.zeros((pad, LANES), total.dtype)
 
 
-def assemble(
-    fine_scale,
-    coarse_scale,
-    core_ref,
-    mine,
-    other,
-    grad_qkv,
-    grad_out,
-    grad_pool,
-    grad_coarse_qkv,
-    grad_coarse_out,
+def unpack_pool(source, start, target, scale):
+    panels = target.shape[1] // LANES
+    channels = target.shape[0] * 2 // SLOTS
+    for step in range(SLOTS // 2):
+        for panel in range(panels):
+            at = start + (step * panels + panel) * channels
+            rows = slice(step * channels, (step + 1) * channels)
+            target[rows, panel * LANES : (panel + 1) * LANES] = (
+                source[at : at + channels].astype(jnp.float32) * scale
+            )
+
+
+def place_half(half, staged, target, arrived):
+    rows = staged.shape[0]
+    start = pl.multiple_of(half * rows, 8)
+    return pltpu.make_async_copy(staged, target.at[pl.ds(start, rows)], arrived.at[0])
+
+
+def assemble_own(
+    scale, core_ref, mine, grad_coarse_qkv, grad_coarse_out, grad_pool, staged, arrived
 ):
-    core = core_ref[0]
-    channels = grad_out.shape[0]
     part, width = grad_coarse_out.shape
     panels = width // LANES
-    edge = channels % LANES
-
-    def coarse(start, count):
-        return mine[start : start + count].astype(jnp.float32) * coarse_scale
+    unpack_pool(mine, 4 * part * panels, staged, scale)
+    copy = place_half(core_ref[0], staged, grad_pool, arrived)
+    copy.start()
+
+    def coarse(start):
+        return mine[start : start + part].astype(jnp.float32) * scale
 
     first = 3 * part * panels
     for panel in range(panels):
         lanes = slice(panel * LANES, (panel + 1) * LANES)
         for which in range(3):
-            grad_coarse_qkv[which, :, lanes] = coarse((3 * panel + which) * part, part)
-        grad_coarse_out[:, lanes] = coarse(first + panel * part, part)
-    first += panels * part
-    half_rows = SLOTS // 2 * channels
-    for source, start, half in ((mine, first, core), (other, 0, 1 - core)):
-        for step in range(SLOTS // 2):
-            row = pl.multiple_of(half * half_rows + step * channels, 8)
-            for panel in range(panels):
-                at = start + (step * panels + panel) * channels
-                grad_pool[pl.ds(row, channels), panel * LANES : (panel + 1) * LANES] = (
-                    source[at : at + channels].astype(jnp.float32) * coarse_scale
-                )
-    skip = half_rows * panels
+            grad_coarse_qkv[which, :, lanes] = coarse((3 * panel + which) * part)
+        grad_coarse_out[:, lanes] = coarse(first + panel * part)
+    copy.wait()
+
+
+def assemble_other(
+    fine_scale,
+    coarse_scale,
+    base,
+    core_ref,
+    pool_in,
+    mine,
+    other,
+    grad_pool,
+    grad_qkv,
+    grad_out,
+    staged,
+    arrived,
+):
+    core = core_ref[0]
+    channels = grad_out.shape[0]
+    edge = channels % LANES
+    unpack_pool(other, 0, staged, coarse_scale)
+    copy = place_half(1 - core, staged, grad_pool, arrived)
+    copy.start()
+    skip = staged.shape[0] * staged.shape[1] // LANES
     fine = []
     for half in range(2):
         for i in range(3):
             at = skip + i * channels
-            near = mine[first + at : first + at + channels].astype(jnp.float32)
+            near = mine[base + at : base + at + channels].astype(jnp.float32)
             far = other[at : at + channels].astype(jnp.float32)
             fine.append(jnp.where(core == half, near, far) * fine_scale)
     for i in range(4):
@@ -531,17 +575,34 @@
     grad_qkv[:, 4 * LANES :] = fine[4][:, :edge]
     grad_out[:, :LANES] = fine[5]
     grad_out[:, LANES:] = fine[4][:, edge:]
-
-
-def call(kernel, outs, scratch, *operands, scalars=1, micros=1, hbm=0, copies=0):
+    copy.wait()
+
+
+def call(
+    kernel,
+    outs,
+    scratch,
+    *operands,
+    scalars=1,
+    micros=1,
+    hbm=0,
+    copies=0,
+    staged=(),
+    in_place=None,
+):
     spaces = [pltpu.SMEM] * scalars + [pltpu.HBM] * hbm
     spaces += [pltpu.VMEM] * (len(operands) - len(spaces))
+    out_spaces = [pltpu.VMEM] * len(outs)
+    if in_place is not None:
+        out_spaces[in_place] = pltpu.HBM
     return pl.pallas_call(
         kernel,
         out_shape=[jax.ShapeDtypeStruct(shape, dtype) for shape, dtype in outs],
         in_specs=[pl.BlockSpec(memory_space=space) for space in spaces],
-        out_specs=[pl.BlockSpec(memory_space=pltpu.VMEM)] * len(outs),
+        out_specs=[pl.BlockSpec(memory_space=space) for space in out_spaces],
+        input_output_aliases={scalars: in_place} if in_place is not None and hbm else {},
         scratch_shapes=[pltpu.VMEM(shape, jnp.bfloat16) for shape in scratch]
+        + [pltpu.VMEM(shape, jnp.float32) for shape in staged]
         + ([pltpu.SemaphoreType.DMA((copies,))] if copies else []),
         compiler_params=pltpu.CompilerParams(vmem_limit_bytes=VMEM_BYTES),
         cost_estimate=pl.CostEstimate(
@@ -642,9 +703,9 @@
     )
     pool_weight, own_qkv, own_out, out_grad = second[:4]
     hidden_rest, *saved_rest = second[4:]
-    children, upward = call(
+    children, upward, partial = call(
         pool,
-        [((SLOTS, channels, owned), bf16), ((2, part, owned), bf16)],
+        [((SLOTS, channels, owned), bf16), ((2, part, owned), bf16), ((owned, width), f32)],
         [(channels, row_count)],
         first_parent,
         hidden_first,
@@ -654,16 +715,16 @@
         own_out,
         other_out,
         out_grad,
+        pool_weight,
         micros=2,
     )
-    coarse_rows, spill_grad, grad_parents, pooled, grad_pooled, coarse_input, mixed, grads = call(
+    coarse_rows, spill_grad, grad_parents, grad_pooled, coarse_input, mixed, grads = call(
         coarse_both,
         [
             ((owned, width), bf16),
             ((SPILL, channels), bf16),
             ((owned, width), bf16),
-            ((SLOTS, channels, owned), bf16),
-            ((SLOTS, channels, owned), bf16),
+            ((SLOTS // 2, channels, 2 * owned), bf16),
             ((owned, width), bf16),
             ((2, part, owned), bf16),
             ((2, 3 * part, owned), bf16),
@@ -672,7 +733,7 @@
             (2, part + SPILL, coarse_heads * LANES),
             (2, part, coarse_heads * LANES),
         ],
-        children,
+        partial,
         upward,
         spill_in,
         pool_weight,
@@ -696,13 +757,18 @@
             ((coarse_count + pool_count, LANES), bf16),
             ((coarse_count + pool_count, LANES), bf16),
         ],
-        [(3 * channels, rest_count), (2, channels, wide_rows)],
+        [
+            (3 * channels, rest_count),
+            (2, channels, wide_rows),
+            (SLOTS, channels, owned),
+        ],
         *shared,
         *saved_rest[2:],
         saved_rest[1],
         saved_rest[0],
         grad_parents,
-        pooled,
+        children,
+        spill_in,
         coarse_input,
         mixed,
         grads,
@@ -741,21 +807,34 @@
     )
     total = sum_over_chips(merged.reshape(plane, padded // plane, LANES)).reshape(padded, LANES)
     other = swap_cores(total[coarse_count:count])
-    grad_qkv, grad_out, grad_pool, grad_coarse_qkv, grad_coarse_out = call(
-        functools.partial(
-            assemble, (row_count * devices) ** (-0.5), (owned * devices) ** (-0.5)
-        ),
-        [
-            ((channels, 3 * channels), f32),
-            ((channels, channels), f32),
-            ((SLOTS * channels, width), f32),
-            ((3, part, width), f32),
-            ((part, width), f32),
-        ],
+    coarse_scale = (owned * devices) ** (-0.5)
+    pool_shape = (SLOTS * channels, width)
+    half_pool = [(SLOTS // 2 * channels, width)]
+    grad_coarse_qkv, grad_coarse_out, grad_pool = call(
+        functools.partial(assemble_own, coarse_scale),
+        [((3, part, width), f32), ((part, width), f32), (pool_shape, f32)],
         [],
         core,
         total,
+        copies=1,
+        staged=half_pool,
+        in_place=2,
+        micros=3,
+    )
+    grad_pool, grad_qkv, grad_out = call(
+        functools.partial(
+            assemble_other, (row_count * devices) ** (-0.5), coarse_scale, coarse_count
+        ),
+        [(pool_shape, f32), ((channels, 3 * channels), f32), ((channels, channels), f32)],
+        [],
+        core,
+        grad_pool,
+        total,
         other,
+        hbm=1,
+        copies=1,
+        staged=half_pool,
+        in_place=0,
         micros=2,
     )
     return (

time: 107 us -> 106 us (level)
  waiting for transfers between devices: 2.86 us -> 1.02 us
    ppermute x5, waiting for transfers between devices: 2.86 us -> 1.02 us  [swap_cores(): return lax.ppermute(shard, 'sub', [(0, 1), (1, 0)])]
    pallas_call x8 -> x9, Pallas kernels: 21.7 us -> 21.6 us  [call(): pl.pallas_call(kernel, out_shape=[jax.ShapeDtypeStruct(shape, dtype) for...]
  transfers between devices with their start and end apart: 7 -> 7, of which waited for: 2 -> 1; matrix products, arithmetic and copies ran while one was open for 0% -> 0% of each run, Pallas kernels for 11% -> 14%
where the time goes in v4:
time: 106 us; the launch traced here: 105 us
  blocking collectives  67.5 us (64%)
  Pallas kernels  21.6 us (20%)
  starting transfers between devices  13.9 us (13%)
    all_to_all x1, blocking collectives, sum_over_chips(): plane = lax.all_to_all(parts, NEAR, 0, 0, tiled=True)  30.2 us
    all_to_all x1, blocking collectives, sum_over_chips(): return lax.all_to_all(copies, NEAR, 0, 0, tiled=True)  22.4 us
    pallas_call x9, Pallas kernels, call(): pl.pallas_call(kernel, out_shape=[jax.ShapeDtypeStruct(shape, dtype) for...  21.6 us
    all_to_all x1, blocking collectives, sum_over_chips(): slab = float_sum(lax.all_to_all(copies, 'zh', 0, 0, tiled=True))  14.9 us
    ppermute x5, starting transfers between devices, swap_cores(): return lax.ppermute(shard, 'sub', [(0, 1), (1, 0)])  8.34 us
    ppermute x2, starting transfers between devices, passed_along(): return lax.ppermute(shard, AXES, pairs)  5.55 us
  transfers between devices with their start and end apart: 7, of which 1 were waited for; matrix products, arithmetic and copies ran while one was open for 0% of the time, Pallas kernels for 14%

profile of v4, /device:TPU:1, one launch (start us, length us, event | category | flops | bytes accessed | tf_op | source)
XLA Modules:
  0.0 105.4 jit_solution(4309225023480946004)
XLA Ops:
  0.6 3.3 %collective-permute-start = (bf16[192,384]{1,0:T(8,128)(2,1)}, bf16[192,384]{1,0:T(8,128)(2,1)S(1)}, u32[]{:S(2)}, u32[]{:S(2)}) collective-permute-start(bf16[192,384]{1,0:T(8,128)(2,1)} %refs_2_.3), channel_id=1, source_target_pairs={{0,1},{1,0},{2,3},{3,2},{4,5},{5,4},{6,7},{7,6},{8,9},{9,8},{10,11... | collective-permute-start | bytes 442376 | tf_op jit(solution)/shard_map/ppermute | solution.py:32
  4.0 0.1 collective-permute-start.2
  4.1 2.4 %shard_map.144 = (bf16[192,512]{1,0:T(8,128)(2,1)S(1)}, bf16[192,576]{1,0:T(8,128)(2,1)S(1)}, bf16[192,192]{1,0:T(8,128)(2,1)S(1)}, s32[1,512]{1,0:T(1,128)S(1)}...) custom-call(s32[1]{0:T(128)} %bitcast.first_parent, ...), custom_call_target="tpu_custom_call" | custom-call | flops 3000000000 | bytes 3000000 | tf_op jit(solution)/shard_map/pallas_call | solution.py:598
  6.5 2.3 %collective-permute-start.1 = (bf16[16,192]{1,0:T(8,128)(2,1)S(1)}, bf16[16,192]{1,0:T(8,128)(2,1)S(1)}, u32[]{:S(2)}, u32[]{:S(2)}) collective-permute-start(bf16[16,192]{1,0:T(8,128)(2,1)S(1)} %get-tuple-element.65), channel_id=1, source_target_pairs={{1,0},{2,1},{3,2},{4,3},{5,4},{6,5},{7,6},{8,7},{9,8},{10,9},{11,1... | collective-permute-start | bytes 18440 | tf_op jit(solution)/shard_map/ppermute | solution.py:28
  8.8 2.7 %shard_map.145 = (bf16[1536,384]{1,0:T(8,128)(2,1)S(1)}, bf16[576,384]{1,0:T(8,128)(2,1)S(1)}, bf16[192,384]{1,0:T(8,128)(2,1)S(1)}, bf16[128,384]{1,0:T(8,128)(...) custom-call(bf16[1536,384]{1,0:T(8,128)(2,1)} %refs_0_.1, ...), custom_call_target="tpu_custom_call" | custom-call | flops 2000000000 | bytes 2000000 | tf_op jit(solution)/shard_map/pallas_call | solution.py:598
  11.5 0.0 collective-permute-done.other_out
  11.5 1.0 shard_map.146
  12.4 0.0 collective-permute-done.1.spill.refs_12_
  12.5 0.0 collective-permute-done.2.other_qkv
  12.5 4.6 %shard_map.147 = (bf16[128,384]{1,0:T(8,128)(2,1)}, bf16[16,192]{1,0:T(8,128)(2,1)S(1)}, bf16[128,384]{1,0:T(8,128)(2,1)S(1)}, bf16[4,192,256]{2,1,0:T(8,128)(2,...) custom-call(f32[128,384]{1,0:T(8,128)S(1)} %get-tuple-element.63.partial, ...), custom_call_target="tpu_custom_call" | custom-call | flops 8000000000 | bytes 8000000 | tf_op jit(solution)/shard_map/pallas_call | solution.py:598
  17.1 3.2 %collective-permute-start.3 = (bf16[16,192]{1,0:T(8,128)(2,1)S(1)}, bf16[16,192]{1,0:T(8,128)(2,1)S(1)}, u32[]{:S(2)}, u32[]{:S(2)}) collective-permute-start(bf16[16,192]{1,0:T(8,128)(2,1)S(1)} %get-tuple-element.73), channel_id=1, source_target_pairs={{0,1},{1,2},{2,3},{3,4},{4,5},{5,6},{6,7},{7,8},{8,9},{9,10},{10,1... | collective-permute-start | bytes 18440 | tf_op jit(solution)/shard_map/ppermute | solution.py:28
  20.4 4.2 %shard_map.148 = (bf16[192,384]{1,0:T(8,128)(2,1)S(1)}, f32[192,576]{1,0:T(8,128)S(1)}, f32[192,192]{1,0:T(8,128)S(1)}, bf16[4608,128]{1,0:T(8,128)(2,1)S(1)}, bf16[4608,128]{1,0:T(8,128)(2,1)S(1)}) custom-call(s32[1]{0:T(128)} %bitcast.7.core_ref, s32[1]{0:T(128)} %bitcast.first_parent, bf16[192,512]{1,0:T(8,128)(2,1)S(1)} %get-tuple-element.54.refs_4_.refs_0_.rows, ...), custom_call_target="tpu_custom_call" | custom-call | flops 5000000000 | bytes 5000000 | tf_op jit(solution)/shard_map/pallas_call | solution.py:598
  24.5 0.0 collective-permute-done.3.rest_0_
  24.5 0.3 collective-permute-start.4
  24.8 2.3 %shard_map.149 = (bf16[192,512]{1,0:T(8,128)(2,1)}, bf16[576,128]{1,0:T(8,128)(2,1)S(1)}, bf16[576,128]{1,0:T(8,128)(2,1)S(1)}) custom-call(s32[1]{0:T(128)} %bitcast.7.core_ref, s32[1]{0:T(128)} %bitcast.first_parent, bf16[192,512]{1,0:T(8,128)(2,1)S(1)} %get-tuple-element.54.refs_4_.refs_0_.rows, ...), custom_call_target="tpu_custom_call" | custom-call | flops 2000000000 | bytes 2000000 | tf_op jit(solution)/shard_map/pallas_call | solution.py:598
  27.2 0.5 collective-permute-start.5
  27.6 1.0 collective-permute-done.5.fine_got
  28.6 0.0 collective-permute-done.4.got
  28.6 0.3 shard_map.150
  28.9 30.2 %all_to_all.15 = bf16[32,168,128]{2,1,0:T(8,128)(2,1)S(1)} all-to-all(bf16[32,168,128]{2,1,0:T(8,128)(2,1)S(1)} %bitcast.12), channel_id=1, replica_groups=mesh['zh'=4,'zl'=2,'y'=4,'x'=4,'sub'=2] {'zl','y','x'}, dimensions={0} | all-to-all | bytes 2752512 | tf_op jit(solution)/shard_map/all_to_all | solution.py:619
  59.2 0.2 reduce_sum.24
  59.4 14.9 %all_to_all.16 = bf16[4,168,128]{2,1,0:T(8,128)(2,1)S(1)} all-to-all(bf16[4,168,128]{2,1,0:T(8,128)(2,1)S(1)} %broadcast_in_dim.6), channel_id=1, replica_groups=mesh['zh'=4,'zl'=2,'y'=4,'x'=4,'sub'=2] {'zh'}, dimensions={0} | all-to-all | bytes 344064 | tf_op jit(solution)/shard_map/all_to_all | solution.py:622
  74.3 0.2 broadcast_in_dim.7
  74.5 22.4 %all_to_all.17 = bf16[32,168,128]{2,1,0:T(8,128)(2,1)S(1)} all-to-all(bf16[32,168,128]{2,1,0:T(8,128)(2,1)S(1)} %broadcast_in_dim.7), channel_id=1, replica_groups=mesh['zh'=4,'zl'=2,'y'=4,'x'=4,'sub'=2] {'zl','y','x'}, dimensions={0} | all-to-all | bytes 2752512 | tf_op jit(solution)/shard_map/all_to_all | solution.py:624
  97.0 4.1 %collective-permute-start.6 = (bf16[2880,128]{1,0:T(8,128)(2,1)S(1)}, bf16[2880,128]{1,0:T(8,128)(2,1)S(1)}, u32[]{:S(2)}, u32[]{:S(2)}) collective-permute-start(bf16[2880,128]{1,0:T(8,128)(2,1)S(1)} %slice.4), channel_id=1, source_target_pairs={{0,1},{1,0},{2,3},{3,2},{4,5},{5,4},{6,7},{7,6},{8,9},{9,8},{10,11... | collective-permute-start | bytes 2211848 | tf_op jit(solution)/shard_map/ppermute | solution.py:32
  101.1 2.1 %shard_map.151 = (f32[3,192,384]{2,1,0:T(8,128)}, f32[192,384]{1,0:T(8,128)}, f32[1536,384]{1,0:T(8,128)}) custom-call(s32[1]{0:T(128)} %bitcast.7.core_ref, bf16[5376,128]{1,0:T(8,128)(2,1)S(1)} %bitcast.14), custom_call_target="tpu_custom_call" | custom-call | flops 3000000000 | bytes 3000000 | tf_op jit(solution)/shard_map/pallas_call | solution.py:598
  103.2 0.0 collective-permute-done.6.other
  103.2 2.0 %shard_map.152 = (f32[1536,384]{1,0:T(8,128)}, f32[192,576]{1,0:T(8,128)}, f32[192,192]{1,0:T(8,128)}) custom-call(s32[1]{0:T(128)} %bitcast.7.core_ref, f32[1536,384]{1,0:T(8,128)} %get-tuple-element.93.pool_in, bf16[5376,128]{1,0:T(8,128)(2,1)S(1)} %bitcast.15, bf16[2880,128]{1,0:T(8,128)(2,1)S(1)} %collective-permute-done.6.other), custom_call_target="tpu_custom_call", output_to_operand_aliasing={{0}: (1, {})} | custom-call | flops 2000000000 | bytes 2000000 | tf_op jit(solution)/shard_map/pallas_call | solution.py:598
  (3 shorter events, 0.1 us)
Async XLA Ops:
  0.6 10.8 %collective-permute-start = (bf16[192,384]{1,0:T(8,128)(2,1)}, bf16[192,384]{1,0:T(8,128)(2,1)S(1)}, u32[]{:S(2)}, u32[]{:S(2)}) collective-permute-start(bf16[192,384]{1,0:T(8,128)(2,1)} %refs_2_.3), channel_id=1, source_target_pairs={{0,1},{1,0},{2,3},{3,2},{4,5},{5,4},{6,7},{7,6},{8,9},{9,8},{10,11... | collective-permute-start | bytes 442376 | tf_op jit(solution)/shard_map/ppermute | solution.py:32
  4.0 8.5 %collective-permute-start.2 = (bf16[576,384]{1,0:T(8,128)(2,1)}, bf16[576,384]{1,0:T(8,128)(2,1)S(1)}, u32[]{:S(2)}, u32[]{:S(2)}) collective-permute-start(bf16[576,384]{1,0:T(8,128)(2,1)} %bitcast.16), channel_id=1, source_target_pairs={{0,1},{1,0},{2,3},{3,2},{4,5},{5,4},{6,7},{7,6},{8,9},{9,8},{10,11... | collective-permute-start | bytes 1327112 | tf_op jit(solution)/shard_map/ppermute | solution.py:32
  6.5 6.0 %collective-permute-start.1 = (bf16[16,192]{1,0:T(8,128)(2,1)S(1)}, bf16[16,192]{1,0:T(8,128)(2,1)S(1)}, u32[]{:S(2)}, u32[]{:S(2)}) collective-permute-start(bf16[16,192]{1,0:T(8,128)(2,1)S(1)} %get-tuple-element.65), channel_id=1, source_target_pairs={{1,0},{2,1},{3,2},{4,3},{5,4},{6,5},{7,6},{8,7},{9,8},{10,9},{11,1... | collective-permute-start | bytes 18440 | tf_op jit(solution)/shard_map/ppermute | solution.py:28
  17.1 7.4 %collective-permute-start.3 = (bf16[16,192]{1,0:T(8,128)(2,1)S(1)}, bf16[16,192]{1,0:T(8,128)(2,1)S(1)}, u32[]{:S(2)}, u32[]{:S(2)}) collective-permute-start(bf16[16,192]{1,0:T(8,128)(2,1)S(1)} %get-tuple-element.73), channel_id=1, source_target_pairs={{0,1},{1,2},{2,3},{3,4},{4,5},{5,6},{6,7},{7,8},{8,9},{9,10},{10,1... | collective-permute-start | bytes 18440 | tf_op jit(solution)/shard_map/ppermute | solution.py:28
  24.5 4.1 %collective-permute-start.4 = (bf16[4608,128]{1,0:T(8,128)(2,1)S(1)}, bf16[4608,128]{1,0:T(8,128)(2,1)S(1)}, u32[]{:S(2)}, u32[]{:S(2)}) collective-permute-start(bf16[4608,128]{1,0:T(8,128)(2,1)S(1)} %get-tuple-element.90), channel_id=1, source_target_pairs={{0,1},{1,0},{2,3},{3,2},{4,5},{5,4},{6,7},{7,6},{8,9},{9,8},{10,11... | collective-permute-start | bytes 3538952 | tf_op jit(solution)/shard_map/ppermute | solution.py:32
  27.2 1.5 %collective-permute-start.5 = (bf16[576,128]{1,0:T(8,128)(2,1)S(1)}, bf16[576,128]{1,0:T(8,128)(2,1)S(1)}, u32[]{:S(2)}, u32[]{:S(2)}) collective-permute-start(bf16[576,128]{1,0:T(8,128)(2,1)S(1)} %get-tuple-element.92), channel_id=1, source_target_pairs={{0,1},{1,0},{2,3},{3,2},{4,5},{5,4},{6,7},{7,6},{8,9},{9,8},{10,11... | collective-permute-start | bytes 442376 | tf_op jit(solution)/shard_map/ppermute | solution.py:32
  97.0 6.3 %collective-permute-start.6 = (bf16[2880,128]{1,0:T(8,128)(2,1)S(1)}, bf16[2880,128]{1,0:T(8,128)(2,1)S(1)}, u32[]{:S(2)}, u32[]{:S(2)}) collective-permute-start(bf16[2880,128]{1,0:T(8,128)(2,1)S(1)} %slice.4), channel_id=1, source_target_pairs={{0,1},{1,0},{2,3},{3,2},{4,5},{5,4},{6,7},{7,6},{8,9},{9,8},{10,11... | collective-permute-start | bytes 2211848 | tf_op jit(solution)/shard_map/ppermute | solution.py:32

commit v5 on v4

--- a/solution.py
+++ b/solution.py
@@ -276,10 +276,8 @@
     pool_weight,
     own_qkv,
     other_qkv,
-    own_out,
-    other_out,
     out_grad,
-    coarse_rows,
+    parents,
     spill_grad,
     grad_parents,
     grad_pooled,
@@ -291,10 +289,10 @@
 ):
     owned, width = out_grad.shape
     channels = spill.shape[1]
-    part = own_out.shape[0]
+    part = upward.shape[1]
     heads = part // HD
     halves = range(2)
-    qkv_weights, out_weights = (own_qkv, other_qkv), (own_out, other_out)
+    qkv_weights = (own_qkv, other_qkv)
     for wide in (wide_query, wide_grad):
         wide[...] = jnp.zeros(wide.shape, wide.dtype)
     for half in halves:
@@ -306,8 +304,8 @@
         late += nn(chosen, pool_weight[slot * channels : (slot + 1) * channels])
     late = jnp.sum(late, 0, keepdims=True)
     at_last = lax.broadcasted_iota(jnp.int32, (owned, width), 0) == owned - 1
-    parents = bround(partial[...] + jnp.where(at_last, late, 0.0)).astype(jnp.float32)
-    normed, inverse = layer_norm(parents, 1)
+    parents[...] = bround(partial[...] + jnp.where(at_last, late, 0.0))
+    normed, inverse = layer_norm(parents[...].astype(jnp.float32), 1)
     coarse_input[...] = bround(normed)
     upstream = out_grad[...]
     classes = window_rows(coarse_window)
@@ -356,8 +354,6 @@
         grad_pooled[slot // 2, :, slot % 2 * owned : (slot % 2 + 1) * owned] = grad_slot
         edge_total += nt(indicator(last & (spill_slot == slot)), grad_slot)
     spill_grad[...] = bround(edge_total)
-    summed = sum(tn(mixed[half], out_weights[half][...]) for half in halves)
-    coarse_rows[...] = bround(parents + summed)
 
 
 def coarse_weights(
@@ -422,8 +418,8 @@
     if first_block:
         row_grad, qkv_total, out_total, grads, wide = rest
     else:
-        spill_grad, row_rest, qkv_rest, out_rest = rest[:4]
-        row_grad, keep, give, grads, wide = rest[4:]
+        spill_grad, qkv_rest, out_rest = rest[:3]
+        row_grad, keep, give, grads, wide = rest[3:]
     channels, count = mixed.shape
     owned = grad_pooled.shape[2] // 2
     heads = channels // HD
@@ -468,13 +464,11 @@
     total = upstream.astype(jnp.float32) + layer_norm_back(normed, inverse, grad_normed, 0)
     grad_qkv = nt(bround(normed), grads[...])
     grad_out = nt(mixed[...], upstream)
+    row_grad[...] = bround(total)
     if first_block:
-        row_grad[...] = bround(total)
         qkv_total[...] = grad_qkv
         out_total[...] = grad_out
         return
-    row_grad[:, span] = bround(total)
-    row_grad[:, count:] = row_rest[...]
     grad_qkv = bround(grad_qkv + qkv_rest[...])
     grad_out = bround(grad_out + out_rest[...])
     core = core_ref[0]
@@ -503,43 +497,80 @@
     total[first + second :] = jnp.zeros((pad, LANES), total.dtype)
 
 
-def unpack_pool(source, start, target, scale):
-    panels = target.shape[1] // LANES
-    channels = target.shape[0] * 2 // SLOTS
+class Copies:
+    def __init__(self, arrived):
+        self.arrived, self.started = arrived, []
+
+    def start(self, source, target):
+        copy = pltpu.make_async_copy(source, target, self.arrived.at[len(self.started)])
+        copy.start()
+        self.started.append(copy)
+
+    def finish(self):
+        for copy in self.started:
+            copy.wait()
+
+
+def unpack_pool(copies, source, start, half, staged, target, scale):
+    panels = staged.shape[1] // LANES
+    channels = staged.shape[0] * 2 // SLOTS
     for step in range(SLOTS // 2):
+        rows = slice(step * channels, (step + 1) * channels)
         for panel in range(panels):
             at = start + (step * panels + panel) * channels
-            rows = slice(step * channels, (step + 1) * channels)
-            target[rows, panel * LANES : (panel + 1) * LANES] = (
+            staged[rows, panel * LANES : (panel + 1) * LANES] = (
                 source[at : at + channels].astype(jnp.float32) * scale
             )
-
-
-def place_half(half, staged, target, arrived):
-    rows = staged.shape[0]
-    start = pl.multiple_of(half * rows, 8)
-    return pltpu.make_async_copy(staged, target.at[pl.ds(start, rows)], arrived.at[0])
+        row = pl.multiple_of(half * staged.shape[0] + step * channels, 8)
+        copies.start(staged.at[rows], target.at[pl.ds(row, channels)])
 
 
 def assemble_own(
-    scale, core_ref, mine, grad_coarse_qkv, grad_coarse_out, grad_pool, staged, arrived
+    scale,
+    core_ref,
+    mine,
+    row_first,
+    row_rest,
+    parents,
+    mixed,
+    own_out,
+    other_out,
+    grad_coarse_qkv,
+    grad_coarse_out,
+    grad_pool,
+    row_grad,
+    coarse_rows,
+    rows_staged,
+    pool_staged,
+    qkv_staged,
+    out_staged,
+    arrived,
 ):
-    part, width = grad_coarse_out.shape
+    copies = Copies(arrived)
+    copies.start(row_first, row_grad.at[:, :LANES])
+    copies.start(row_rest, row_grad.at[:, LANES:])
+    part, width = out_staged.shape
     panels = width // LANES
-    unpack_pool(mine, 4 * part * panels, staged, scale)
-    copy = place_half(core_ref[0], staged, grad_pool, arrived)
-    copy.start()
+    unpack_pool(
+        copies, mine, 4 * part * panels, core_ref[0], pool_staged, grad_pool, scale
+    )
 
     def coarse(start):
         return mine[start : start + part].astype(jnp.float32) * scale
 
     first = 3 * part * panels
+    for which in range(3):
+        for panel in range(panels):
+            lanes = slice(panel * LANES, (panel + 1) * LANES)
+            qkv_staged[which, :, lanes] = coarse((3 * panel + which) * part)
+        copies.start(qkv_staged.at[which], grad_coarse_qkv.at[which])
     for panel in range(panels):
-        lanes = slice(panel * LANES, (panel + 1) * LANES)
-        for which in range(3):
-            grad_coarse_qkv[which, :, lanes] = coarse((3 * panel + which) * part)
-        grad_coarse_out[:, lanes] = coarse(first + panel * part)
-    copy.wait()
+        out_staged[:, panel * LANES : (panel + 1) * LANES] = coarse(first + panel * part)
+    copies.start(out_staged, grad_coarse_out)
+    summed = tn(mixed[0], own_out[...]) + tn(mixed[1], other_out[...])
+    rows_staged[...] = bround(parents[...].astype(jnp.float32) + summed)
+    copies.start(rows_staged, coarse_rows)
+    copies.finish()
 
 
 def assemble_other(
@@ -553,16 +584,16 @@
     grad_pool,
     grad_qkv,
     grad_out,
-    staged,
+    pool_staged,
+    qkv_staged,
+    out_staged,
     arrived,
 ):
+    copies = Copies(arrived)
     core = core_ref[0]
-    channels = grad_out.shape[0]
+    channels = out_staged.shape[0]
     edge = channels % LANES
-    unpack_pool(other, 0, staged, coarse_scale)
-    copy = place_half(1 - core, staged, grad_pool, arrived)
-    copy.start()
-    skip = staged.shape[0] * staged.shape[1] // LANES
+    skip = pool_staged.shape[0] * pool_staged.shape[1] // LANES
     fine = []
     for half in range(2):
         for i in range(3):
@@ -571,11 +602,14 @@
             far = other[at : at + channels].astype(jnp.float32)
             fine.append(jnp.where(core == half, near, far) * fine_scale)
     for i in range(4):
-        grad_qkv[:, i * LANES : (i + 1) * LANES] = fine[i]
-    grad_qkv[:, 4 * LANES :] = fine[4][:, :edge]
-    grad_out[:, :LANES] = fine[5]
-    grad_out[:, LANES:] = fine[4][:, edge:]
-    copy.wait()
+        qkv_staged[:, i * LANES : (i + 1) * LANES] = fine[i]
+    qkv_staged[:, 4 * LANES :] = fine[4][:, :edge]
+    copies.start(qkv_staged, grad_qkv)
+    out_staged[:, :LANES] = fine[5]
+    out_staged[:, LANES:] = fine[4][:, edge:]
+    copies.start(out_staged, grad_out)
+    unpack_pool(copies, other, 0, 1 - core, pool_staged, grad_pool, coarse_scale)
+    copies.finish()
 
 
 def call(
@@ -588,19 +622,18 @@
     hbm=0,
     copies=0,
     staged=(),
-    in_place=None,
+    to_hbm=False,
+    aliases=None,
 ):
     spaces = [pltpu.SMEM] * scalars + [pltpu.HBM] * hbm
     spaces += [pltpu.VMEM] * (len(operands) - len(spaces))
-    out_spaces = [pltpu.VMEM] * len(outs)
-    if in_place is not None:
-        out_spaces[in_place] = pltpu.HBM
+    out_spaces = [pltpu.HBM if to_hbm else pltpu.VMEM] * len(outs)
     return pl.pallas_call(
         kernel,
         out_shape=[jax.ShapeDtypeStruct(shape, dtype) for shape, dtype in outs],
         in_specs=[pl.BlockSpec(memory_space=space) for space in spaces],
         out_specs=[pl.BlockSpec(memory_space=space) for space in out_spaces],
-        input_output_aliases={scalars: in_place} if in_place is not None and hbm else {},
+        input_output_aliases=aliases or {},
         scratch_shapes=[pltpu.VMEM(shape, jnp.bfloat16) for shape in scratch]
         + [pltpu.VMEM(shape, jnp.float32) for shape in staged]
         + ([pltpu.SemaphoreType.DMA((copies,))] if copies else []),
@@ -718,7 +751,7 @@
         pool_weight,
         micros=2,
     )
-    coarse_rows, spill_grad, grad_parents, grad_pooled, coarse_input, mixed, grads = call(
+    parents, spill_grad, grad_parents, grad_pooled, coarse_input, mixed, grads = call(
         coarse_both,
         [
             ((owned, width), bf16),
@@ -739,8 +772,6 @@
         pool_weight,
         own_qkv,
         other_qkv,
-        own_out,
-        other_out,
         out_grad,
         scalars=0,
         micros=8,
@@ -778,10 +809,10 @@
     )
     spill_back, give = lax.optimization_barrier((spill_back, give))
     got = swap_cores(give)
-    row_grad, fine_keep, fine_give = call(
+    row_first, fine_keep, fine_give = call(
         functools.partial(fine_back, 0),
         [
-            ((channels, row_count), bf16),
+            ((channels, LANES), bf16),
             ((fine_count, LANES), bf16),
             ((fine_count, LANES), bf16),
         ],
@@ -791,7 +822,6 @@
         saved_first[1],
         saved_first[0],
         spill_back,
-        row_rest,
         qkv_rest,
         out_rest,
         scalars=2,
@@ -809,16 +839,28 @@
     other = swap_cores(total[coarse_count:count])
     coarse_scale = (owned * devices) ** (-0.5)
     pool_shape = (SLOTS * channels, width)
-    half_pool = [(SLOTS // 2 * channels, width)]
-    grad_coarse_qkv, grad_coarse_out, grad_pool = call(
+    half_pool = (SLOTS // 2 * channels, width)
+    grad_coarse_qkv, grad_coarse_out, grad_pool, row_grad, coarse_rows = call(
         functools.partial(assemble_own, coarse_scale),
-        [((3, part, width), f32), ((part, width), f32), (pool_shape, f32)],
-        [],
+        [
+            ((3, part, width), f32),
+            ((part, width), f32),
+            (pool_shape, f32),
+            ((channels, row_count), bf16),
+            ((owned, width), bf16),
+        ],
+        [(owned, width)],
         core,
         total,
-        copies=1,
-        staged=half_pool,
-        in_place=2,
+        row_first,
+        row_rest,
+        parents,
+        mixed,
+        own_out,
+        other_out,
+        copies=7 + SLOTS // 2,
+        staged=[half_pool, (3, part, width), (part, width)],
+        to_hbm=True,
         micros=3,
     )
     grad_pool, grad_qkv, grad_out = call(
@@ -832,9 +874,10 @@
         total,
         other,
         hbm=1,
-        copies=1,
-        staged=half_pool,
-        in_place=0,
+        copies=2 + SLOTS // 2,
+        staged=[half_pool, (channels, 3 * channels), (channels, channels)],
+        to_hbm=True,
+        aliases={1: 0},
         micros=2,
     )
     return (

time: 106 us -> 104 us (0.981)
  Pallas kernels: 21.6 us -> 19.3 us
    pallas_call x9, Pallas kernels: 21.6 us -> 19.3 us  [call(): pl.pallas_call(kernel, out_shape=[jax.ShapeDtypeStruct(shape, dtype) for...]
  transfers between devices with their start and end apart: 7 -> 7, of which waited for: 1 -> 2; matrix products, arithmetic and copies ran while one was open for 0% -> 0% of each run, Pallas kernels for 14% -> 13%
where the time goes in v5:
time: 104 us; the launch traced here: 103 us
  blocking collectives  67.5 us (65%)
  Pallas kernels  19.3 us (19%)
  starting transfers between devices  14 us (13%)
  waiting for transfers between devices  1.15 us (1%)
    all_to_all x1, blocking collectives, sum_over_chips(): plane = lax.all_to_all(parts, NEAR, 0, 0, tiled=True)  30.2 us
    all_to_all x1, blocking collectives, sum_over_chips(): return lax.all_to_all(copies, NEAR, 0, 0, tiled=True)  22.4 us
    pallas_call x9, Pallas kernels, call(): pl.pallas_call(kernel, out_shape=[jax.ShapeDtypeStruct(shape, dtype) for...  19.3 us
    all_to_all x1, blocking collectives, sum_over_chips(): slab = float_sum(lax.all_to_all(copies, 'zh', 0, 0, tiled=True))  14.9 us
    ppermute x5, starting transfers between devices, swap_cores(): return lax.ppermute(shard, 'sub', [(0, 1), (1, 0)])  8.43 us
    ppermute x2, starting transfers between devices, passed_along(): return lax.ppermute(shard, AXES, pairs)  5.59 us
  transfers between devices with their start and end apart: 7, of which 2 were waited for; matrix products, arithmetic and copies ran while one was open for 0% of the time, Pallas kernels for 13%

profile of v5, /device:TPU:1, one launch (start us, length us, event | category | flops | bytes accessed | tf_op | source)
XLA Modules:
  0.0 103.3 jit_solution(13906782822179775171)
XLA Ops:
  0.6 3.3 %collective-permute-start = (bf16[192,384]{1,0:T(8,128)(2,1)}, bf16[192,384]{1,0:T(8,128)(2,1)S(1)}, u32[]{:S(2)}, u32[]{:S(2)}) collective-permute-start(bf16[192,384]{1,0:T(8,128)(2,1)} %refs_2_.3), channel_id=1, source_target_pairs={{0,1},{1,0},{2,3},{3,2},{4,5},{5,4},{6,7},{7,6},{8,9},{9,8},{10,11... | collective-permute-start | bytes 442376 | tf_op jit(solution)/shard_map/ppermute | solution.py:32
  4.0 0.1 collective-permute-start.2
  4.1 2.4 %shard_map.144 = (bf16[192,512]{1,0:T(8,128)(2,1)S(1)}, bf16[192,576]{1,0:T(8,128)(2,1)S(1)}, bf16[192,192]{1,0:T(8,128)(2,1)S(1)}, s32[1,512]{1,0:T(1,128)S(1)}...) custom-call(s32[1]{0:T(128)} %bitcast.1.first_parent, ...), custom_call_target="tpu_custom_call" | custom-call | flops 3000000000 | bytes 3000000 | tf_op jit(solution)/shard_map/pallas_call | solution.py:631
  6.5 2.3 %collective-permute-start.1 = (bf16[16,192]{1,0:T(8,128)(2,1)S(1)}, bf16[16,192]{1,0:T(8,128)(2,1)S(1)}, u32[]{:S(2)}, u32[]{:S(2)}) collective-permute-start(bf16[16,192]{1,0:T(8,128)(2,1)S(1)} %get-tuple-element.67), channel_id=1, source_target_pairs={{1,0},{2,1},{3,2},{4,3},{5,4},{6,5},{7,6},{8,7},{9,8},{10,9},{11,1... | collective-permute-start | bytes 18440 | tf_op jit(solution)/shard_map/ppermute | solution.py:28
  8.8 2.7 %shard_map.145 = (bf16[1536,384]{1,0:T(8,128)(2,1)S(1)}, bf16[576,384]{1,0:T(8,128)(2,1)S(1)}, bf16[192,384]{1,0:T(8,128)(2,1)S(1)}, bf16[128,384]{1,0:T(8,128)(...) custom-call(bf16[1536,384]{1,0:T(8,128)(2,1)} %refs_0_.1, ...), custom_call_target="tpu_custom_call" | custom-call | flops 2000000000 | bytes 2000000 | tf_op jit(solution)/shard_map/pallas_call | solution.py:631
  11.5 0.0 collective-permute-done.other_out
  11.5 1.0 shard_map.146
  12.4 0.0 collective-permute-done.1.spill.refs_12_
  12.4 0.0 collective-permute-done.2.other_qkv
  12.5 4.0 %shard_map.147 = (bf16[128,384]{1,0:T(8,128)(2,1)S(1)}, bf16[16,192]{1,0:T(8,128)(2,1)S(1)}, bf16[128,384]{1,0:T(8,128)(2,1)S(1)}, bf16[4,192,256]{2,1,0:T(8,128...) custom-call(f32[128,384]{1,0:T(8,128)S(1)} %get-tuple-element.65.partia, ...), custom_call_target="tpu_custom_call" | custom-call | flops 8000000000 | bytes 8000000 | tf_op jit(solution)/shard_map/pallas_call | solution.py:631
  16.5 3.3 %collective-permute-start.3 = (bf16[16,192]{1,0:T(8,128)(2,1)S(1)}, bf16[16,192]{1,0:T(8,128)(2,1)S(1)}, u32[]{:S(2)}, u32[]{:S(2)}) collective-permute-start(bf16[16,192]{1,0:T(8,128)(2,1)S(1)} %get-tuple-element.80), channel_id=1, source_target_pairs={{0,1},{1,2},{2,3},{3,4},{4,5},{5,6},{6,7},{7,8},{8,9},{9,10},{10,1... | collective-permute-start | bytes 18440 | tf_op jit(solution)/shard_map/ppermute | solution.py:28
  19.8 4.2 %shard_map.148 = (bf16[192,384]{1,0:T(8,128)(2,1)S(1)}, f32[192,576]{1,0:T(8,128)S(1)}, f32[192,192]{1,0:T(8,128)S(1)}, bf16[4608,128]{1,0:T(8,128)(2,1)S(1)}, bf16[4608,128]{1,0:T(8,128)(2,1)S(1)}) custom-call(s32[1]{0:T(128)} %bitcast.core_ref, s32[1]{0:T(128)} %bitcast.1.first_parent, bf16[192,512]{1,0:T(8,128)(2,1)S(1)} %get-tuple-element.55.refs_4_.refs_0_.rows, ...), custom_call_target="tpu_custom_call" | custom-call | flops 5000000000 | bytes 5000000 | tf_op jit(solution)/shard_map/pallas_call | solution.py:631
  24.0 0.0 collective-permute-done.3.rest_0_
  24.0 0.3 collective-permute-start.4
  24.2 1.7 %shard_map.149 = (bf16[192,128]{1,0:T(8,128)(2,1)S(1)}, bf16[576,128]{1,0:T(8,128)(2,1)S(1)}, bf16[576,128]{1,0:T(8,128)(2,1)S(1)}) custom-call(s32[1]{0:T(128)} %bitcast.core_ref, s32[1]{0:T(128)} %bitcast.1.first_parent, bf16[192,512]{1,0:T(8,128)(2,1)S(1)} %get-tuple-element.55.refs_4_.refs_0_.rows, ...), custom_call_target="tpu_custom_call" | custom-call | flops 2000000000 | bytes 2000000 | tf_op jit(solution)/shard_map/pallas_call | solution.py:631
  25.9 0.6 collective-permute-start.5
  26.5 1.0 collective-permute-done.5.fine_got
  27.5 0.0 collective-permute-done.4.got
  27.5 0.3 shard_map.150
  27.8 30.2 %all_to_all.15 = bf16[32,168,128]{2,1,0:T(8,128)(2,1)S(1)} all-to-all(bf16[32,168,128]{2,1,0:T(8,128)(2,1)S(1)} %bitcast.12), channel_id=1, replica_groups=mesh['zh'=4,'zl'=2,'y'=4,'x'=4,'sub'=2] {'zl','y','x'}, dimensions={0} | all-to-all | bytes 2752512 | tf_op jit(solution)/shard_map/all_to_all | solution.py:652
  58.1 0.2 reduce_sum.24
  58.3 14.9 %all_to_all.16 = bf16[4,168,128]{2,1,0:T(8,128)(2,1)S(1)} all-to-all(bf16[4,168,128]{2,1,0:T(8,128)(2,1)S(1)} %broadcast_in_dim.6), channel_id=1, replica_groups=mesh['zh'=4,'zl'=2,'y'=4,'x'=4,'sub'=2] {'zh'}, dimensions={0} | all-to-all | bytes 344064 | tf_op jit(solution)/shard_map/all_to_all | solution.py:655
  73.2 0.2 broadcast_in_dim.7
  73.4 22.4 %all_to_all.17 = bf16[32,168,128]{2,1,0:T(8,128)(2,1)S(1)} all-to-all(bf16[32,168,128]{2,1,0:T(8,128)(2,1)S(1)} %broadcast_in_dim.7), channel_id=1, replica_groups=mesh['zh'=4,'zl'=2,'y'=4,'x'=4,'sub'=2] {'zl','y','x'}, dimensions={0} | all-to-all | bytes 2752512 | tf_op jit(solution)/shard_map/all_to_all | solution.py:657
  95.8 4.1 %collective-permute-start.6 = (bf16[2880,128]{1,0:T(8,128)(2,1)S(1)}, bf16[2880,128]{1,0:T(8,128)(2,1)S(1)}, u32[]{:S(2)}, u32[]{:S(2)}) collective-permute-start(bf16[2880,128]{1,0:T(8,128)(2,1)S(1)} %slice.4), channel_id=1, source_target_pairs={{0,1},{1,0},{2,3},{3,2},{4,5},{5,4},{6,7},{7,6},{8,9},{9,8},{10,11... | collective-permute-start | bytes 2211848 | tf_op jit(solution)/shard_map/ppermute | solution.py:32
  100.0 1.7 %shard_map.151 = (f32[3,192,384]{2,1,0:T(8,128)}, f32[192,384]{1,0:T(8,128)}, f32[1536,384]{1,0:T(8,128)}, bf16[192,512]{1,0:T(8,128)(2,1)}, bf16[128,384]{1,0:T(8,128)(2,1)}) custom-call(s32[1]{0:T(128)} %bitcast.core_ref, bf16[5376,128]{1,0:T(8,128)(2,1)S(1)} %bitcast.14, bf16[192,128]{1,0:T(8,128)(2,1)S(1)} %get-tuple-element.92.row_first, ...), custom_call_target="tpu_custom_call" | custom-call | flops 3000000000 | bytes 3000000 | tf_op jit(solution)/shard_map/pallas_call | solution.py:631
  101.7 0.1 collective-permute-done.6.other
  101.8 1.3 %shard_map.152 = (f32[1536,384]{1,0:T(8,128)}, f32[192,576]{1,0:T(8,128)}, f32[192,192]{1,0:T(8,128)}) custom-call(s32[1]{0:T(128)} %bitcast.core_ref, f32[1536,384]{1,0:T(8,128)} %get-tuple-element.97.pool_in, bf16[5376,128]{1,0:T(8,128)(2,1)S(1)} %bitcast.15, bf16[2880,128]{1,0:T(8,128)(2,1)S(1)} %collective-permute-done.6.other), custom_call_target="tpu_custom_call", output_to_operand_aliasing={{0}: (1, {})} | custom-call | flops 2000000000 | bytes 2000000 | tf_op jit(solution)/shard_map/pallas_call | solution.py:631
  (3 shorter events, 0.1 us)
Async XLA Ops:
  0.6 10.8 %collective-permute-start = (bf16[192,384]{1,0:T(8,128)(2,1)}, bf16[192,384]{1,0:T(8,128)(2,1)S(1)}, u32[]{:S(2)}, u32[]{:S(2)}) collective-permute-start(bf16[192,384]{1,0:T(8,128)(2,1)} %refs_2_.3), channel_id=1, source_target_pairs={{0,1},{1,0},{2,3},{3,2},{4,5},{5,4},{6,7},{7,6},{8,9},{9,8},{10,11... | collective-permute-start | bytes 442376 | tf_op jit(solution)/shard_map/ppermute | solution.py:32
  4.0 8.5 %collective-permute-start.2 = (bf16[576,384]{1,0:T(8,128)(2,1)}, bf16[576,384]{1,0:T(8,128)(2,1)S(1)}, u32[]{:S(2)}, u32[]{:S(2)}) collective-permute-start(bf16[576,384]{1,0:T(8,128)(2,1)} %bitcast.16), channel_id=1, source_target_pairs={{0,1},{1,0},{2,3},{3,2},{4,5},{5,4},{6,7},{7,6},{8,9},{9,8},{10,11... | collective-permute-start | bytes 1327112 | tf_op jit(solution)/shard_map/ppermute | solution.py:32
  6.5 6.0 %collective-permute-start.1 = (bf16[16,192]{1,0:T(8,128)(2,1)S(1)}, bf16[16,192]{1,0:T(8,128)(2,1)S(1)}, u32[]{:S(2)}, u32[]{:S(2)}) collective-permute-start(bf16[16,192]{1,0:T(8,128)(2,1)S(1)} %get-tuple-element.67), channel_id=1, source_target_pairs={{1,0},{2,1},{3,2},{4,3},{5,4},{6,5},{7,6},{8,7},{9,8},{10,9},{11,1... | collective-permute-start | bytes 18440 | tf_op jit(solution)/shard_map/ppermute | solution.py:28
  16.5 7.5 %collective-permute-start.3 = (bf16[16,192]{1,0:T(8,128)(2,1)S(1)}, bf16[16,192]{1,0:T(8,128)(2,1)S(1)}, u32[]{:S(2)}, u32[]{:S(2)}) collective-permute-start(bf16[16,192]{1,0:T(8,128)(2,1)S(1)} %get-tuple-element.80), channel_id=1, source_target_pairs={{0,1},{1,2},{2,3},{3,4},{4,5},{5,6},{6,7},{7,8},{8,9},{9,10},{10,1... | collective-permute-start | bytes 18440 | tf_op jit(solution)/shard_map/ppermute | solution.py:28
  24.0 3.6 %collective-permute-start.4 = (bf16[4608,128]{1,0:T(8,128)(2,1)S(1)}, bf16[4608,128]{1,0:T(8,128)(2,1)S(1)}, u32[]{:S(2)}, u32[]{:S(2)}) collective-permute-start(bf16[4608,128]{1,0:T(8,128)(2,1)S(1)} %get-tuple-element.82), channel_id=1, source_target_pairs={{0,1},{1,0},{2,3},{3,2},{4,5},{5,4},{6,7},{7,6},{8,9},{9,8},{10,11... | collective-permute-start | bytes 3538952 | tf_op jit(solution)/shard_map/ppermute | solution.py:32
  25.9 1.6 %collective-permute-start.5 = (bf16[576,128]{1,0:T(8,128)(2,1)S(1)}, bf16[576,128]{1,0:T(8,128)(2,1)S(1)}, u32[]{:S(2)}, u32[]{:S(2)}) collective-permute-start(bf16[576,128]{1,0:T(8,128)(2,1)S(1)} %get-tuple-element.91), channel_id=1, source_target_pairs={{0,1},{1,0},{2,3},{3,2},{4,5},{5,4},{6,7},{7,6},{8,9},{9,8},{10,11... | collective-permute-start | bytes 442376 | tf_op jit(solution)/shard_map/ppermute | solution.py:32
  95.8 6.0 %collective-permute-start.6 = (bf16[2880,128]{1,0:T(8,128)(2,1)S(1)}, bf16[2880,128]{1,0:T(8,128)(2,1)S(1)}, u32[]{:S(2)}, u32[]{:S(2)}) collective-permute-start(bf16[2880,128]{1,0:T(8,128)(2,1)S(1)} %slice.4), channel_id=1, source_target_pairs={{0,1},{1,0},{2,3},{3,2},{4,5},{5,4},{6,7},{7,6},{8,9},{9,8},{10,11... | collective-permute-start | bytes 2211848 | tf_op jit(solution)/shard_map/ppermute | solution.py:32

commit v6 on v5

--- a/solution.py
+++ b/solution.py
@@ -148,15 +148,13 @@
 
 
 def fine_blocks(
-    first, rows, qkv_weight, out_weight, hidden, mixed, qkv, exponents, inverses, wide, wait
+    rows, qkv_weight, out_weight, hidden, mixed, qkv, exponents, inverses, wide
 ):
     channels, count = hidden.shape
     heads = channels // HD
     clear_wide(wide, heads, fine_window)
     classes = window_rows(fine_window)
-    wait(0)
-    wait(1)
-    rows_float = rows[:, first * LANES : first * LANES + count].astype(jnp.float32)
+    rows_float = rows[...].astype(jnp.float32)
     normed, _ = layer_norm(rows_float, 0)
     qkv[...] = bround(tn(qkv_weight[...], bround(normed)))
     for block in range(count // LANES):
@@ -175,51 +173,27 @@
             mixed.at[:, lanes],
             store,
         )
-    wait(2)
     hidden[...] = bround(rows_float + tn(out_weight[...], mixed[...]))
 
 
-def fine_first(first_parent, *refs):
-    sources, targets = refs[:5], refs[5:10]
-    hidden, mixed, qkv, exponents, inverses, spill, wide, arrived = refs[10:]
-    rows, qkv_weight, out_weight, parent_index, child_slot = targets
+def bring(first_parent, *refs):
+    sources, targets, packed, arrived = refs[:5], refs[5:10], refs[10], refs[11]
     copies = fetch(tuple(zip(sources, targets)), arrived)
-    fine_blocks(
-        0,
-        rows,
-        qkv_weight,
-        out_weight,
-        hidden,
-        mixed,
-        qkv,
-        exponents,
-        inverses,
-        wide,
-        lambda i: copies[i].wait(),
-    )
-    copies[3].wait()
-    copies[4].wait()
-    spill[...] = bround(nt(leading_slots(parent_index, child_slot, first_parent), hidden[...]))
-
-
-def fine_rest(*refs):
+    rows, _, _, parent_index, child_slot = targets
+    for i in (0, 3, 4):
+        copies[i].wait()
+    channels = rows.shape[0]
+    packed[:channels] = rows[:, :LANES]
+    packed[channels:] = leading_slots(parent_index, child_slot, first_parent)
+    copies[1].wait()
+    copies[2].wait()
+
+
+def fine_forward(*refs):
     sources, (rows, qkv_weight, out_weight) = refs[:4], refs[4:7]
-    targets = refs[7:11]
-    hidden, mixed, qkv, exponents, inverses, wide, arrived = refs[11:]
+    targets, outs, wide, arrived = refs[7:11], refs[11:16], refs[16], refs[17]
     copies = fetch(tuple(zip(sources, targets)), arrived)
-    fine_blocks(
-        1,
-        rows,
-        qkv_weight,
-        out_weight,
-        hidden,
-        mixed,
-        qkv,
-        exponents,
-        inverses,
-        wide,
-        lambda i: None,
-    )
+    fine_blocks(rows, qkv_weight, out_weight, *outs, wide)
     for copy in copies:
         copy.wait()
 
@@ -238,8 +212,7 @@
 
 def pool(
     first_parent,
-    first_hidden,
-    rest_hidden,
+    hidden,
     parent_index,
     child_slot,
     own_out,
@@ -249,11 +222,8 @@
     children,
     upward,
     partial,
-    hidden,
 ):
     owned = out_grad.shape[0]
-    hidden[:, :LANES] = first_hidden[...]
-    hidden[:, LANES:] = rest_hidden[...]
     slot_of = slot_numbers(parent_index[...], child_slot[...], first_parent, owned)
     for slot in range(0, SLOTS, 2):
         both = jnp.concatenate([indicator(slot_of == slot), indicator(slot_of == slot + 1)], 0)
@@ -270,25 +240,47 @@
 
 
 def coarse_both(
+    packed,
+    fine_qkv,
+    fine_out,
     partial,
     upward,
-    spill,
     pool_weight,
     own_qkv,
     other_qkv,
     out_grad,
     parents,
-    spill_grad,
+    spill,
+    next_upstream,
     grad_parents,
     grad_pooled,
     coarse_input,
     mixed,
     grads,
+    next_mixed,
+    next_qkv,
+    next_exponents,
+    next_inverses,
+    next_hidden,
+    wide_next,
     wide_query,
     wide_grad,
 ):
     owned, width = out_grad.shape
-    channels = spill.shape[1]
+    channels = fine_out.shape[0]
+    fine_blocks(
+        packed.at[:channels],
+        fine_qkv,
+        fine_out,
+        next_hidden,
+        next_mixed,
+        next_qkv,
+        next_exponents,
+        next_inverses,
+        wide_next,
+    )
+    leading = packed[channels:]
+    spill[...] = bround(nt(leading, next_hidden[...]))
     part = upward.shape[1]
     heads = part // HD
     halves = range(2)
@@ -353,7 +345,7 @@
         grad_slot = grad_all[slot * channels : (slot + 1) * channels]
         grad_pooled[slot // 2, :, slot % 2 * owned : (slot % 2 + 1) * owned] = grad_slot
         edge_total += nt(indicator(last & (spill_slot == slot)), grad_slot)
-    spill_grad[...] = bround(edge_total)
+    next_upstream[...] = bround(tn(bround(edge_total), leading))
 
 
 def coarse_weights(
@@ -400,77 +392,64 @@
 
 
 def fine_back(
-    first_block,
     core_ref,
     first_parent,
     rows,
+    packed,
     grad_pooled,
+    next_upstream,
     parent_index,
     child_slot,
-    qkv_weight,
     out_weight,
-    exponents,
-    inverses,
-    qkv,
-    mixed,
     *rest,
 ):
-    if first_block:
-        row_grad, qkv_total, out_total, grads, wide = rest
-    else:
-        spill_grad, qkv_rest, out_rest = rest[:3]
-        row_grad, keep, give, grads, wide = rest[3:]
-    channels, count = mixed.shape
+    own, beyond = rest[:4], rest[4:8]
+    upstreams, grads, keep, give, wide = rest[8:]
+    channels, row_count = rows.shape
     owned = grad_pooled.shape[2] // 2
     heads = channels // HD
-    span = slice(first_block * LANES, first_block * LANES + count)
-    normed, inverse = layer_norm(rows[:, span].astype(jnp.float32), 0)
-    slot_of = slot_numbers(parent_index[:, span], child_slot[:, span], first_parent, owned)
-    upstream = jnp.zeros((channels, count), jnp.float32)
+    all_rows = jnp.concatenate([rows[...], packed[:channels]], 1)
+    mixed = jnp.concatenate([own[3][...], beyond[3][...]], 1)
+    normed, _ = layer_norm(all_rows.astype(jnp.float32), 0)
+    slot_of = slot_numbers(parent_index[...], child_slot[...], first_parent, owned)
+    upstream = jnp.zeros((channels, row_count), jnp.float32)
     for slot in range(0, SLOTS, 2):
         both = jnp.concatenate([indicator(slot_of == slot), indicator(slot_of == slot + 1)], 0)
         upstream += nn(grad_pooled[slot // 2], both)
-    if not first_block:
-        leading = leading_slots(parent_index, child_slot, first_parent)
-        upstream += tn(spill_grad[...], leading)
-    upstream = bround(upstream)
+    upstream = jnp.concatenate([bround(upstream), next_upstream[...]], 1)
+    upstreams[...] = upstream
     upward = bround(nn(out_weight[...], upstream))
     wide[...] = jnp.zeros(wide.shape, wide.dtype)
-    for block in range(count // LANES):
+    blocks = row_count // LANES
+    for block in range(blocks + 1):
+        exponents, inverses, qkv, _ = own if block < blocks else beyond
+        within = block % blocks
         lanes = slice(block * LANES, (block + 1) * LANES)
+        inner = slice(within * LANES, (within + 1) * LANES)
         grad_rows = wide.at[block % wide.shape[0]]
         scales = [
-            inverses[block * heads + head : block * heads + head + 1] for head in range(heads)
+            inverses[within * heads + head : within * heads + head + 1] for head in range(heads)
         ]
         for head in range(heads):
             at = slice(head * HD, (head + 1) * HD)
             weighted = scaled(upward[at, lanes]).astype(jnp.float32) * scales[head]
             grad_rows[at, head * LANES : (head + 1) * LANES] = bround(weighted)
-        grad_probs = tn(qkv[2 * channels :, lanes], grad_rows[...])
+        grad_probs = tn(qkv[2 * channels :, inner], grad_rows[...])
         for head in range(heads):
             at = [slice(i * channels + head * HD, i * channels + (head + 1) * HD) for i in range(3)]
             out = slice(head * LANES, (head + 1) * LANES)
             back = attend_back(
-                qkv[at[0], lanes],
-                qkv[at[1], lanes],
+                qkv[at[0], inner],
+                qkv[at[1], inner],
                 upward[at[0], lanes],
-                exponents[block, :, out],
+                exponents[within, :, out],
                 scales[head],
                 grad_probs[:, out],
             )
             for which in range(3):
                 grads[at[which], lanes] = back[which]
-    grad_normed = nn(qkv_weight[...], grads[...])
-    total = upstream.astype(jnp.float32) + layer_norm_back(normed, inverse, grad_normed, 0)
-    grad_qkv = nt(bround(normed), grads[...])
-    grad_out = nt(mixed[...], upstream)
-    row_grad[...] = bround(total)
-    if first_block:
-        qkv_total[...] = grad_qkv
-        out_total[...] = grad_out
-        return
-    grad_qkv = bround(grad_qkv + qkv_rest[...])
-    grad_out = bround(grad_out + out_rest[...])
+    grad_qkv = bround(nt(bround(normed), grads[...]))
+    grad_out = bround(nt(mixed, upstream))
     core = core_ref[0]
     whole = 3 * channels // LANES
     panels = [grad_qkv[:, i * LANES : (i + 1) * LANES] for i in range(whole)]
@@ -483,10 +462,15 @@
         give[at] = jnp.where(core == 0, panels[half + i], panels[i])
 
 
-def fine_and_weights(core_ref, first_parent, *refs):
-    fine_in, weight_in, refs = refs[:10], refs[10:17], refs[17:]
-    fine_back(1, core_ref, first_parent, *fine_in, *refs[:3], *refs[5:7])
-    coarse_weights(core_ref, *weight_in, *refs[3:5], *refs[7:])
+def row_gradients(rows, packed, qkv_weight, upstream, grads, row_first, row_rest, row_next):
+    channels, row_count = rows.shape
+    all_rows = jnp.concatenate([rows[...], packed[:channels]], 1)
+    normed, inverse = layer_norm(all_rows.astype(jnp.float32), 0)
+    grad_normed = nn(qkv_weight[...], grads[...])
+    total = upstream[...].astype(jnp.float32) + layer_norm_back(normed, inverse, grad_normed, 0)
+    row_first[...] = total[:, :LANES]
+    row_rest[...] = bround(total[:, LANES:row_count])
+    row_next[...] = bround(total[:, row_count:])
 
 
 def merge(keep, got, fine_keep, fine_got, total):
@@ -530,6 +514,7 @@
     core_ref,
     mine,
     row_first,
+    row_late,
     row_rest,
     parents,
     mixed,
@@ -541,13 +526,15 @@
     row_grad,
     coarse_rows,
     rows_staged,
+    first_staged,
     pool_staged,
     qkv_staged,
     out_staged,
     arrived,
 ):
     copies = Copies(arrived)
-    copies.start(row_first, row_grad.at[:, :LANES])
+    first_staged[...] = bround(row_first[...] + row_late[...].astype(jnp.float32))
+    copies.start(first_staged, row_grad.at[:, :LANES])
     copies.start(row_rest, row_grad.at[:, LANES:])
     part, width = out_staged.shape
     panels = width // LANES
@@ -648,13 +635,14 @@
     return bround(jnp.sum(stacked.astype(jnp.float32), 0))
 
 
-def sum_over_chips(parts):
-    plane = lax.all_to_all(parts, NEAR, 0, 0, tiled=True)
-    slab = float_sum(plane)
+def sum_over_chips(parts, rows_after):
+    slab = float_sum(lax.all_to_all(parts, NEAR, 0, 0, tiled=True))
     copies = jnp.broadcast_to(slab, (lax.axis_size("zh"),) + slab.shape)
     slab = float_sum(lax.all_to_all(copies, "zh", 0, 0, tiled=True))
+    slab, *row_parts = rows_after(slab)
     copies = jnp.broadcast_to(slab, parts.shape)
-    return lax.all_to_all(copies, NEAR, 0, 0, tiled=True)
+    total = lax.all_to_all(copies, NEAR, 0, 0, tiled=True)
+    return lax.optimization_barrier((total, *row_parts))
 
 
 def on_device(
@@ -707,23 +695,22 @@
         ]
 
     sources = (rows, qkv_weight, out_weight, parent_row, slot_row)
-    first = call(
-        fine_first,
-        like(*sources) + block_outs(1) + [((SPILL, channels), bf16)],
-        [(1, channels + SPILL, wide_rows)],
+    *brought, packed = call(
+        bring,
+        like(*sources) + [((channels + SPILL, LANES), bf16)],
+        [],
         first_parent,
         *in_hbm(*sources),
         hbm=5,
         copies=5,
-        micros=3,
-    )
-    rows, fine_qkv, fine_out, parent_row, slot_row = first[:5]
-    hidden_first, *saved_first, spill = first[5:]
-    spill_in = passed_along(spill, -1)
+        micros=1,
+    )
+    rows, fine_qkv, fine_out, parent_row, slot_row = brought
+    packed = passed_along(packed, -1)
     sources = (pool_weight, own_qkv, coarse_out_weight, out_grad)
     second = call(
-        fine_rest,
-        like(*sources) + block_outs(blocks - 1),
+        fine_forward,
+        like(*sources) + block_outs(blocks),
         [(2, channels + SPILL, wide_rows)],
         *in_hbm(*sources),
         rows,
@@ -732,17 +719,16 @@
         scalars=0,
         hbm=4,
         copies=4,
-        micros=2,
+        micros=4,
     )
     pool_weight, own_qkv, own_out, out_grad = second[:4]
-    hidden_rest, *saved_rest = second[4:]
+    hidden, mixed_fine, qkv, exponents, inverses = second[4:]
     children, upward, partial = call(
         pool,
         [((SLOTS, channels, owned), bf16), ((2, part, owned), bf16), ((owned, width), f32)],
-        [(channels, row_count)],
+        [],
         first_parent,
-        hidden_first,
-        hidden_rest,
+        hidden,
         parent_row,
         slot_row,
         own_out,
@@ -751,24 +737,43 @@
         pool_weight,
         micros=2,
     )
-    parents, spill_grad, grad_parents, grad_pooled, coarse_input, mixed, grads = call(
+    (
+        parents,
+        spill,
+        next_upstream,
+        grad_parents,
+        grad_pooled,
+        coarse_input,
+        mixed,
+        grads,
+        next_mixed,
+        next_qkv,
+        next_exponents,
+        next_inverses,
+    ) = call(
         coarse_both,
         [
             ((owned, width), bf16),
             ((SPILL, channels), bf16),
+            ((channels, LANES), bf16),
             ((owned, width), bf16),
             ((SLOTS // 2, channels, 2 * owned), bf16),
             ((owned, width), bf16),
             ((2, part, owned), bf16),
             ((2, 3 * part, owned), bf16),
-        ],
+        ]
+        + block_outs(1)[1:],
         [
+            (channels, LANES),
+            (1, channels + SPILL, wide_rows),
             (2, part + SPILL, coarse_heads * LANES),
             (2, part, coarse_heads * LANES),
         ],
+        packed,
+        fine_qkv,
+        fine_out,
         partial,
         upward,
-        spill_in,
         pool_weight,
         own_qkv,
         other_qkv,
@@ -776,57 +781,74 @@
         scalars=0,
         micros=8,
     )
-    spill_back = passed_along(spill_grad, 1)
-    shared = (core, first_parent, rows, grad_pooled, parent_row, slot_row, fine_qkv, fine_out)
-    rest_count = row_count - LANES
-    row_rest, qkv_rest, out_rest, keep, give = call(
-        fine_and_weights,
+    keep, give = call(
+        coarse_weights,
         [
-            ((channels, rest_count), bf16),
-            ((channels, 3 * channels), f32),
-            ((channels, channels), f32),
             ((coarse_count + pool_count, LANES), bf16),
             ((coarse_count + pool_count, LANES), bf16),
         ],
-        [
-            (3 * channels, rest_count),
-            (2, channels, wide_rows),
-            (SLOTS, channels, owned),
-        ],
-        *shared,
-        *saved_rest[2:],
-        saved_rest[1],
-        saved_rest[0],
+        [(SLOTS, channels, owned)],
+        core,
         grad_parents,
         children,
-        spill_in,
+        spill,
         coarse_input,
         mixed,
         grads,
         out_grad,
-        scalars=2,
-        micros=5,
-    )
-    spill_back, give = lax.optimization_barrier((spill_back, give))
+        micros=1,
+    )
     got = swap_cores(give)
-    row_first, fine_keep, fine_give = call(
-        functools.partial(fine_back, 0),
+    upstream, fine_grads, fine_keep, fine_give = call(
+        fine_back,
         [
-            ((channels, LANES), bf16),
+            ((channels, row_count + LANES), bf16),
+            ((3 * channels, row_count + LANES), bf16),
             ((fine_count, LANES), bf16),
             ((fine_count, LANES), bf16),
         ],
-        [(3 * channels, LANES), (1, channels, wide_rows)],
-        *shared,
-        *saved_first[2:],
-        saved_first[1],
-        saved_first[0],
-        spill_back,
-        qkv_rest,
-        out_rest,
+        [(2, channels, wide_rows)],
+        core,
+        first_parent,
+        rows,
+        packed,
+        grad_pooled,
+        next_upstream,
+        parent_row,
+        slot_row,
+        fine_out,
+        exponents,
+        inverses,
+        qkv,
+        mixed_fine,
+        next_exponents,
+        next_inverses,
+        next_qkv,
+        next_mixed,
         scalars=2,
-        micros=2,
-    )
+        micros=6,
+    )
+
+    def rows_after(dependence):
+        dependence, given = lax.optimization_barrier((dependence, upstream))
+        row_first, row_rest, row_next = call(
+            row_gradients,
+            [
+                ((channels, LANES), f32),
+                ((channels, row_count - LANES), bf16),
+                ((channels, LANES), bf16),
+            ],
+            [],
+            rows,
+            packed,
+            fine_qkv,
+            given,
+            fine_grads,
+            scalars=0,
+            micros=4,
+        )
+        return dependence, row_first, row_rest, passed_along(row_next, 1)
+
     fine_got = swap_cores(fine_give)
     plane = lax.axis_size("zl") * lax.axis_size("y") * lax.axis_size("x")
     count = coarse_count + pool_count + fine_count
@@ -835,7 +857,10 @@
     (merged,) = call(
         merge, [((padded, LANES), bf16)], [], keep, got, fine_keep, fine_got, scalars=0, micros=1
     )
-    total = sum_over_chips(merged.reshape(plane, padded // plane, LANES)).reshape(padded, LANES)
+    total, row_first, row_rest, row_late = sum_over_chips(
+        merged.reshape(plane, padded // plane, LANES), rows_after
+    )
+    total = total.reshape(padded, LANES)
     other = swap_cores(total[coarse_count:count])
     coarse_scale = (owned * devices) ** (-0.5)
     pool_shape = (SLOTS * channels, width)
@@ -849,10 +874,11 @@
             ((channels, row_count), bf16),
             ((owned, width), bf16),
         ],
-        [(owned, width)],
+        [(owned, width), (channels, LANES)],
         core,
         total,
         row_first,
+        row_late,
         row_rest,
         parents,
         mixed,

time: 104 us -> 101 us (0.971)
  blocking collectives: 67.5 us -> 44.2 us
  waiting for transfers between devices: 1.15 us -> 10.2 us
  starting transfers between devices: 14 us -> 22.4 us
  local copies, waits for them, and re-layouts: 0.25 us -> 1.97 us
  Pallas kernels: 19.3 us -> 20.5 us
    all_to_all x2 -> x1, blocking collectives: 52.6 us -> 29.3 us  [sum_over_chips(): slab = float_sum(lax.all_to_all(parts, NEAR, 0, 0, tiled=True))]
    all_to_all x0 -> x1, waiting for transfers between devices: none -> 5.91 us  [sum_over_chips(): total = lax.all_to_all(copies, NEAR, 0, 0, tiled=True)]
    all_to_all x0 -> x1, starting transfers between devices: none -> 4.77 us  [sum_over_chips(): total = lax.all_to_all(copies, NEAR, 0, 0, tiled=True)]
    ppermute x2, waiting for transfers between devices: 0.01 us -> 3.15 us  [passed_along(): return lax.ppermute(shard, AXES, pairs)]
    ppermute x2, starting transfers between devices: 5.59 us -> 8.42 us  [passed_along(): return lax.ppermute(shard, AXES, pairs)]
    pallas_call x9 -> x10, Pallas kernels: 19.3 us -> 20.5 us  [call(): pl.pallas_call(kernel, out_shape=[jax.ShapeDtypeStruct(shape, dtype) for...]
    broadcast_in_dim x1, local copies, waits for them, and re-layouts: 0.18 us -> 1.26 us  [sum_over_chips(): copies = jnp.broadcast_to(slab, parts.shape)]
  transfers between devices with their start and end apart: 7 -> 8, of which waited for: 2 -> 4; matrix products, arithmetic and copies ran while one was open for 0% -> 0% of each run, Pallas kernels for 13% -> 12%
where the time goes in v6:
time: 101 us; the launch traced here: 100 us
  blocking collectives  44.2 us (44%)
  starting transfers between devices  22.4 us (22%)
  Pallas kernels  20.5 us (20%)
  waiting for transfers between devices  10.2 us (10%)
  local copies, waits for them, and re-layouts  1.97 us (2%)
    all_to_all x1, blocking collectives, sum_over_chips(): slab = float_sum(lax.all_to_all(parts, NEAR, 0, 0, tiled=True))  29.3 us
    pallas_call x10, Pallas kernels, call(): pl.pallas_call(kernel, out_shape=[jax.ShapeDtypeStruct(shape, dtype) for...  20.5 us
    all_to_all x1, blocking collectives, sum_over_chips(): slab = float_sum(lax.all_to_all(copies, 'zh', 0, 0, tiled=True))  14.9 us
    ppermute x5, starting transfers between devices, swap_cores(): return lax.ppermute(shard, 'sub', [(0, 1), (1, 0)])  9.21 us
    ppermute x2, starting transfers between devices, passed_along(): return lax.ppermute(shard, AXES, pairs)  8.42 us
    all_to_all x1, waiting for transfers between devices, sum_over_chips(): total = lax.all_to_all(copies, NEAR, 0, 0, tiled=True)  5.91 us
    all_to_all x1, starting transfers between devices, sum_over_chips(): total = lax.all_to_all(copies, NEAR, 0, 0, tiled=True)  4.77 us
    ppermute x2, waiting for transfers between devices, passed_along(): return lax.ppermute(shard, AXES, pairs)  3.15 us
  transfers between devices with their start and end apart: 8, of which 4 were waited for; matrix products, arithmetic and copies ran while one was open for 0% of the time, Pallas kernels for 12%

profile of v6, /device:TPU:1, one launch (start us, length us, event | category | flops | bytes accessed | tf_op | source)
XLA Modules:
  0.0 100.4 jit_solution(9621315062228620812)
XLA Ops:
  0.6 3.3 %collective-permute-start.1 = (bf16[192,384]{1,0:T(8,128)(2,1)}, bf16[192,384]{1,0:T(8,128)(2,1)S(1)}, u32[]{:S(2)}, u32[]{:S(2)}) collective-permute-start(bf16[192,384]{1,0:T(8,128)(2,1)} %refs_2_.3), channel_id=1, source_target_pairs={{0,1},{1,0},{2,3},{3,2},{4,5},{5,4},{6,7},{7,6},{8,9},{9,8},{10,11... | collective-permute-start | bytes 442376 | tf_op jit(solution)/shard_map/ppermute | solution.py:32
  4.0 0.1 collective-permute-start.2
  4.1 1.1 %shard_map.144 = (bf16[192,512]{1,0:T(8,128)(2,1)S(1)}, bf16[192,576]{1,0:T(8,128)(2,1)S(1)}, bf16[192,192]{1,0:T(8,128)(2,1)S(1)}, s32[1,512]{1,0:T(1,128)S(1)}...) custom-call(s32[1]{0:T(128)} %bitcast.1.first_parent, bf16[192,512]{1,0:T(8,128)(2,1)} %bitcast.18, ...), custom_call_target="tpu_custom_call" | custom-call | flops 1000000000 | bytes 1000000 | tf_op jit(solution)/shard_map/pallas_call | solution.py:618
  5.2 2.3 %collective-permute-start = (bf16[208,128]{1,0:T(8,128)(2,1)S(1)}, bf16[208,128]{1,0:T(8,128)(2,1)S(1)}, u32[]{:S(2)}, u32[]{:S(2)}) collective-permute-start(bf16[208,128]{1,0:T(8,128)(2,1)S(1)} %get-tuple-element.60), channel_id=1, source_target_pairs={{1,0},{2,1},{3,2},{4,3},{5,4},{6,5},{7,6},{8,7},{9,8},{10,9},{11,1... | collective-permute-start | bytes 159752 | tf_op jit(solution)/shard_map/ppermute | solution.py:28
  7.5 3.0 %shard_map.145 = (bf16[1536,384]{1,0:T(8,128)(2,1)S(1)}, bf16[576,384]{1,0:T(8,128)(2,1)S(1)}, bf16[192,384]{1,0:T(8,128)(2,1)S(1)}, bf16[128,384]{1,0:T(8,128)(...) custom-call(bf16[1536,384]{1,0:T(8,128)(2,1)} %refs_0_.1, ...), custom_call_target="tpu_custom_call" | custom-call | flops 4000000000 | bytes 4000000 | tf_op jit(solution)/shard_map/pallas_call | solution.py:618
  10.6 0.0 collective-permute-done.1.other_out
  10.6 1.0 shard_map.146
  11.6 0.0 collective-permute-done.packed
  11.6 0.0 collective-permute-done.2.other_qkv
  11.6 5.4 %shard_map.147 = (bf16[128,384]{1,0:T(8,128)(2,1)S(1)}, bf16[16,192]{1,0:T(8,128)(2,1)S(1)}, bf16[192,128]{1,0:T(8,128)(2,1)S(1)}, bf16[128,384]{1,0:T(8,128)(2,...) custom-call(bf16[208,128]{1,0:T(8,128)(2,1)S(1)} %collective-permute, ...), custom_call_target="tpu_custom_call" | custom-call | flops 8000000000 | bytes 8000000 | tf_op jit(solution)/shard_map/pallas_call | solution.py:618
  17.0 0.9 shard_map.148
  17.9 0.3 collective-permute-start.3
  18.2 5.1 %shard_map.149 = (bf16[192,640]{1,0:T(8,128)(2,1)S(1)}, bf16[576,640]{1,0:T(8,128)(2,1)S(1)}, bf16[576,128]{1,0:T(8,128)(2,1)S(1)}, bf16[576,128]{1,0:T(8,128)(2,1)S(1)}) custom-call(s32[1]{0:T(128)} %bitcast.core_ref, s32[1]{0:T(128)} %bitcast.1.first_parent, bf16[192,512]{1,0:T(8,128)(2,1)S(1)} %get-tuple-element.63.refs_4_.rows, ...), custom_call_target="tpu_custom_call" | custom-call | flops 6000000000 | bytes 6000000 | tf_op jit(solution)/shard_map/pallas_call | solution.py:618
  23.3 0.6 collective-permute-start.4
  23.9 1.0 %collective-permute-done.4.fine_got = bf16[576,128]{1,0:T(8,128)(2,1)S(1)} collective-permute-done((bf16[576,128]{1,0:T(8,128)(2,1)S(1)}, bf16[576,128]{1,0:T(8,128)(2,1)S(1)}, u32[]{:S(2)}, u32[]{:S(2)}) %collective-permute-start.4) | collective-permute-done | bytes 147488 | tf_op jit(solution)/shard_map/ppermute | solution.py:32
  24.9 0.0 collective-permute-done.3.got
  24.9 0.3 shard_map.150
  25.2 29.3 %all_to_all.15 = bf16[32,168,128]{2,1,0:T(8,128)(2,1)S(1)} all-to-all(bf16[32,168,128]{2,1,0:T(8,128)(2,1)S(1)} %bitcast.12), channel_id=1, replica_groups=mesh['zh'=4,'zl'=2,'y'=4,'x'=4,'sub'=2] {'zl','y','x'}, dimensions={0} | all-to-all | bytes 2752512 | tf_op jit(solution)/shard_map/all_to_all | solution.py:639
  54.5 0.2 reduce_sum.24
  54.7 14.9 %all_to_all.16 = bf16[4,168,128]{2,1,0:T(8,128)(2,1)S(1)} all-to-all(bf16[4,168,128]{2,1,0:T(8,128)(2,1)S(1)} %broadcast_in_dim.6), channel_id=1, replica_groups=mesh['zh'=4,'zl'=2,'y'=4,'x'=4,'sub'=2] {'zh'}, dimensions={0} | all-to-all | bytes 344064 | tf_op jit(solution)/shard_map/all_to_all | solution.py:641
  69.7 1.3 %broadcast_in_dim.7 = bf16[32,168,128]{2,1,0:T(8,128)(2,1)} broadcast(bf16[168,128]{1,0:T(8,128)(2,1)S(1)} %reduce_sum.25), dimensions={1,2} | broadcast | bytes 1419264 | tf_op jit(solution)/shard_map/broadcast_in_dim | solution.py:643
  70.9 4.8 %all-to-all-start.2 = ((bf16[32,168,128]{2,1,0:T(8,128)(2,1)}), bf16[32,168,128]{2,1,0:T(8,128)(2,1)S(1)}, u32[]{:S(2)}, u32[]{:S(2)}) async-start(bf16[32,168,128]{2,1,0:T(8,128)(2,1)} %broadcast_in_dim.7), calls=%async_computation.2 | async-start | bytes 2752512 | tf_op jit(solution)/shard_map/all_to_all | solution.py:644
  75.7 0.6 shard_map.151
  76.3 0.0 copy-start
  76.3 0.6 copy-done
  76.9 0.0 copy-start.1
  76.9 6.1 %collective-permute-start.5 = (bf16[192,128]{1,0:T(8,128)(2,1)S(1)}, bf16[192,128]{1,0:T(8,128)(2,1)S(1)}, u32[]{:S(2)}, u32[]{:S(2)}) collective-permute-start(bf16[192,128]{1,0:T(8,128)(2,1)S(1)} %get-tuple-element.99), channel_id=1, source_target_pairs={{0,1},{1,2},{2,3},{3,4},{4,5},{5,6},{6,7},{7,8},{8,9},{9,10},{10,1... | collective-permute-start | bytes 147464 | tf_op jit(solution)/shard_map/ppermute | solution.py:28
  83.0 3.2 %collective-permute-done.5.row_late = bf16[192,128]{1,0:T(8,128)(2,1)S(1)} collective-permute-done((bf16[192,128]{1,0:T(8,128)(2,1)S(1)}, bf16[192,128]{1,0:T(8,128)(2,1)S(1)}, u32[]{:S(2)}, u32[]{:S(2)}) %collective-permute-start.5) | collective-permute-done | bytes 49184 | tf_op jit(solution)/shard_map/ppermute | solution.py:28
  86.2 5.9 %all-to-all-done.2 = bf16[32,168,128]{2,1,0:T(8,128)(2,1)S(1)} async-done(((bf16[32,168,128]{2,1,0:T(8,128)(2,1)}), bf16[32,168,128]{2,1,0:T(8,128)(2,1)S(1)}, u32[]{:S(2)}, u32[]{:S(2)}) %all-to-all-start.2) | async-done | bytes 1376288 | tf_op jit(solution)/shard_map/all_to_all | solution.py:644
  92.1 4.9 %collective-permute-start.6 = (bf16[2880,128]{1,0:T(8,128)(2,1)S(1)}, bf16[2880,128]{1,0:T(8,128)(2,1)S(1)}, u32[]{:S(2)}, u32[]{:S(2)}) collective-permute-start(bf16[2880,128]{1,0:T(8,128)(2,1)S(1)} %slice.4), channel_id=1, source_target_pairs={{0,1},{1,0},{2,3},{3,2},{4,5},{5,4},{6,7},{7,6},{8,9},{9,8},{10,11... | collective-permute-start | bytes 2211848 | tf_op jit(solution)/shard_map/ppermute | solution.py:32
  97.1 0.0 copy-done.1
  97.1 1.7 %shard_map.152 = (f32[3,192,384]{2,1,0:T(8,128)}, f32[192,384]{1,0:T(8,128)}, f32[1536,384]{1,0:T(8,128)}, bf16[192,512]{1,0:T(8,128)(2,1)}, bf16[128,384]{1,0:T(8,128)(2,1)}) custom-call(s32[1]{0:T(128)} %bitcast.core_ref, bf16[5376,128]{1,0:T(8,128)(2,1)S(1)} %bitcast.14, f32[192,128]{1,0:T(8,128)S(1)} %copy-done.1, ...), custom_call_target="tpu_custom_call" | custom-call | flops 3000000000 | bytes 3000000 | tf_op jit(solution)/shard_map/pallas_call | solution.py:618
  98.8 0.1 collective-permute-done.6.other
  98.9 1.3 %shard_map.153 = (f32[1536,384]{1,0:T(8,128)}, f32[192,576]{1,0:T(8,128)}, f32[192,192]{1,0:T(8,128)}) custom-call(s32[1]{0:T(128)} %bitcast.core_ref, f32[1536,384]{1,0:T(8,128)} %get-tuple-element.107.pool_in, bf16[5376,128]{1,0:T(8,128)(2,1)S(1)} %bitcast.15, bf16[2880,128]{1,0:T(8,128)(2,1)S(1)} %collective-permute-done.6.other), custom_call_target="tpu_custom_call", output_to_operand_aliasing={{0}: (1, {})} | custom-call | flops 2000000000 | bytes 2000000 | tf_op jit(solution)/shard_map/pallas_call | solution.py:618
  (3 shorter events, 0.1 us)
Async XLA Ops:
  0.6 10.0 %collective-permute-start.1 = (bf16[192,384]{1,0:T(8,128)(2,1)}, bf16[192,384]{1,0:T(8,128)(2,1)S(1)}, u32[]{:S(2)}, u32[]{:S(2)}) collective-permute-start(bf16[192,384]{1,0:T(8,128)(2,1)} %refs_2_.3), channel_id=1, source_target_pairs={{0,1},{1,0},{2,3},{3,2},{4,5},{5,4},{6,7},{7,6},{8,9},{9,8},{10,11... | collective-permute-start | bytes 442376 | tf_op jit(solution)/shard_map/ppermute | solution.py:32
  4.0 7.6 %collective-permute-start.2 = (bf16[576,384]{1,0:T(8,128)(2,1)}, bf16[576,384]{1,0:T(8,128)(2,1)S(1)}, u32[]{:S(2)}, u32[]{:S(2)}) collective-permute-start(bf16[576,384]{1,0:T(8,128)(2,1)} %bitcast.16), channel_id=1, source_target_pairs={{0,1},{1,0},{2,3},{3,2},{4,5},{5,4},{6,7},{7,6},{8,9},{9,8},{10,11... | collective-permute-start | bytes 1327112 | tf_op jit(solution)/shard_map/ppermute | solution.py:32
  5.2 6.3 %collective-permute-start = (bf16[208,128]{1,0:T(8,128)(2,1)S(1)}, bf16[208,128]{1,0:T(8,128)(2,1)S(1)}, u32[]{:S(2)}, u32[]{:S(2)}) collective-permute-start(bf16[208,128]{1,0:T(8,128)(2,1)S(1)} %get-tuple-element.60), channel_id=1, source_target_pairs={{1,0},{2,1},{3,2},{4,3},{5,4},{6,5},{7,6},{8,7},{9,8},{10,9},{11,1... | collective-permute-start | bytes 159752 | tf_op jit(solution)/shard_map/ppermute | solution.py:28
  17.9 7.0 %collective-permute-start.3 = (bf16[4608,128]{1,0:T(8,128)(2,1)S(1)}, bf16[4608,128]{1,0:T(8,128)(2,1)S(1)}, u32[]{:S(2)}, u32[]{:S(2)}) collective-permute-start(bf16[4608,128]{1,0:T(8,128)(2,1)S(1)} %get-tuple-element.80), channel_id=1, source_target_pairs={{0,1},{1,0},{2,3},{3,2},{4,5},{5,4},{6,7},{7,6},{8,9},{9,8},{10,11... | collective-permute-start | bytes 3538952 | tf_op jit(solution)/shard_map/ppermute | solution.py:32
  23.3 1.6 %collective-permute-start.4 = (bf16[576,128]{1,0:T(8,128)(2,1)S(1)}, bf16[576,128]{1,0:T(8,128)(2,1)S(1)}, u32[]{:S(2)}, u32[]{:S(2)}) collective-permute-start(bf16[576,128]{1,0:T(8,128)(2,1)S(1)} %get-tuple-element.92), channel_id=1, source_target_pairs={{0,1},{1,0},{2,3},{3,2},{4,5},{5,4},{6,7},{7,6},{8,9},{9,8},{10,11... | collective-permute-start | bytes 442376 | tf_op jit(solution)/shard_map/ppermute | solution.py:32
  70.9 21.2 %all-to-all-start.2 = ((bf16[32,168,128]{2,1,0:T(8,128)(2,1)}), bf16[32,168,128]{2,1,0:T(8,128)(2,1)S(1)}, u32[]{:S(2)}, u32[]{:S(2)}) async-start(bf16[32,168,128]{2,1,0:T(8,128)(2,1)} %broadcast_in_dim.7), calls=%async_computation.2 | async-start | bytes 2752512 | tf_op jit(solution)/shard_map/all_to_all | solution.py:644
  76.3 0.6 copy-start
  76.9 20.2 %copy-start.1 = (f32[192,128]{1,0:T(8,128)S(1)}, f32[192,128]{1,0:T(8,128)}, u32[]{:S(2)}) copy-start(f32[192,128]{1,0:T(8,128)} %copy-done) | copy-start | bytes 294916
  76.9 9.3 %collective-permute-start.5 = (bf16[192,128]{1,0:T(8,128)(2,1)S(1)}, bf16[192,128]{1,0:T(8,128)(2,1)S(1)}, u32[]{:S(2)}, u32[]{:S(2)}) collective-permute-start(bf16[192,128]{1,0:T(8,128)(2,1)S(1)} %get-tuple-element.99), channel_id=1, source_target_pairs={{0,1},{1,2},{2,3},{3,4},{4,5},{5,6},{6,7},{7,8},{8,9},{9,10},{10,1... | collective-permute-start | bytes 147464 | tf_op jit(solution)/shard_map/ppermute | solution.py:28
  92.1 6.8 %collective-permute-start.6 = (bf16[2880,128]{1,0:T(8,128)(2,1)S(1)}, bf16[2880,128]{1,0:T(8,128)(2,1)S(1)}, u32[]{:S(2)}, u32[]{:S(2)}) collective-permute-start(bf16[2880,128]{1,0:T(8,128)(2,1)S(1)} %slice.4), channel_id=1, source_target_pairs={{0,1},{1,0},{2,3},{3,2},{4,5},{5,4},{6,7},{7,6},{8,9},{9,8},{10,11... | collective-permute-start | bytes 2211848 | tf_op jit(solution)/shard_map/ppermute | solution.py:32

commit v7 on v6

--- a/solution.py
+++ b/solution.py
@@ -675,8 +675,6 @@
     parent_row = parent_index.reshape(1, row_count)
     slot_row = child_slot.reshape(1, row_count)
     own_qkv = coarse_qkv_weight.transpose(0, 2, 1).reshape(3 * part, width)
-    other_qkv = swap_cores(own_qkv)
-    other_out = swap_cores(coarse_out_weight)
     wide_rows = heads * LANES
 
     def in_hbm(*arrays):
@@ -706,7 +704,10 @@
         micros=1,
     )
     rows, fine_qkv, fine_out, parent_row, slot_row = brought
+    packed, give_qkv, give_out = lax.optimization_barrier((packed, own_qkv, coarse_out_weight))
     packed = passed_along(packed, -1)
+    other_qkv = swap_cores(give_qkv)
+    other_out = swap_cores(give_out)
     sources = (pool_weight, own_qkv, coarse_out_weight, out_grad)
     second = call(
         fine_forward,

time: 101 us -> 100 us (0.990)
    ppermute x2, starting transfers between devices: 8.42 us -> 11.3 us  [passed_along(): return lax.ppermute(shard, AXES, pairs)]
    ppermute x5, starting transfers between devices: 9.21 us -> 6.38 us  [swap_cores(): return lax.ppermute(shard, 'sub', [(0, 1), (1, 0)])]
  transfers between devices with their start and end apart: 8 -> 8, of which waited for: 4 -> 4; matrix products, arithmetic and copies ran while one was open for 0% -> 0% of each run, Pallas kernels for 12% -> 11%
where the time goes in v7:
time: 100 us; the launch traced here: 99.7 us
  blocking collectives  43.3 us (43%)
  starting transfers between devices  22.4 us (22%)
  Pallas kernels  20.6 us (21%)
  waiting for transfers between devices  10.2 us (10%)
  local copies, waits for them, and re-layouts  1.98 us (2%)
    all_to_all x1, blocking collectives, sum_over_chips(): slab = float_sum(lax.all_to_all(parts, NEAR, 0, 0, tiled=True))  28.4 us
    pallas_call x10, Pallas kernels, call(): pl.pallas_call(kernel, out_shape=[jax.ShapeDtypeStruct(shape, dtype) for...  20.6 us
    all_to_all x1, blocking collectives, sum_over_chips(): slab = float_sum(lax.all_to_all(copies, 'zh', 0, 0, tiled=True))  14.9 us
    ppermute x2, starting transfers between devices, passed_along(): return lax.ppermute(shard, AXES, pairs)  11.3 us
    ppermute x5, starting transfers between devices, swap_cores(): return lax.ppermute(shard, 'sub', [(0, 1), (1, 0)])  6.38 us
    all_to_all x1, waiting for transfers between devices, sum_over_chips(): total = lax.all_to_all(copies, NEAR, 0, 0, tiled=True)  5.91 us
    all_to_all x1, starting transfers between devices, sum_over_chips(): total = lax.all_to_all(copies, NEAR, 0, 0, tiled=True)  4.77 us
    ppermute x2, waiting for transfers between devices, passed_along(): return lax.ppermute(shard, AXES, pairs)  3.16 us
  transfers between devices with their start and end apart: 8, of which 4 were waited for; matrix products, arithmetic and copies ran while one was open for 0% of the time, Pallas kernels for 11%

profile of v7, /device:TPU:1, one launch (start us, length us, event | category | flops | bytes accessed | tf_op | source)
XLA Modules:
  0.0 99.7 jit_solution(10053715398568427669)
XLA Ops:
  0.7 0.0 copy-start.3
  0.7 0.0 copy-start.2
  0.7 1.2 %shard_map.144 = (bf16[192,512]{1,0:T(8,128)(2,1)S(1)}, bf16[192,576]{1,0:T(8,128)(2,1)S(1)}, bf16[192,192]{1,0:T(8,128)(2,1)S(1)}, s32[1,512]{1,0:T(1,128)S(1)}...) custom-call(s32[1]{0:T(128)} %bitcast.1.first_parent, bf16[192,512]{1,0:T(8,128)(2,1)} %bitcast.18, ...), custom_call_target="tpu_custom_call" | custom-call | flops 1000000000 | bytes 1000000 | tf_op jit(solution)/shard_map/pallas_call | solution.py:618
  1.9 5.1 %collective-permute-start = (bf16[208,128]{1,0:T(8,128)(2,1)S(1)}, bf16[208,128]{1,0:T(8,128)(2,1)S(1)}, u32[]{:S(2)}, u32[]{:S(2)}) collective-permute-start(bf16[208,128]{1,0:T(8,128)(2,1)S(1)} %get-tuple-element.64), channel_id=1, source_target_pairs={{1,0},{2,1},{3,2},{4,3},{5,4},{6,5},{7,6},{8,7},{9,8},{10,9},{11,1... | collective-permute-start | bytes 159752 | tf_op jit(solution)/shard_map/ppermute | solution.py:28
  7.0 0.0 copy-done.3
  7.1 0.1 collective-permute-start.1
  7.2 0.0 copy-done.2
  7.2 0.5 collective-permute-start.2
  7.7 3.0 %shard_map.145 = (bf16[1536,384]{1,0:T(8,128)(2,1)S(1)}, bf16[576,384]{1,0:T(8,128)(2,1)S(1)}, bf16[192,384]{1,0:T(8,128)(2,1)S(1)}, bf16[128,384]{1,0:T(8,128)(...) custom-call(bf16[1536,384]{1,0:T(8,128)(2,1)} %refs_0_.1, ...), custom_call_target="tpu_custom_call" | custom-call | flops 4000000000 | bytes 4000000 | tf_op jit(solution)/shard_map/pallas_call | solution.py:618
  10.7 0.0 collective-permute-done.1.other_out
  10.7 1.0 shard_map.146
  11.7 0.0 collective-permute-done.packed
  11.7 0.0 collective-permute-done.2.other_qkv
  11.7 5.4 %shard_map.147 = (bf16[128,384]{1,0:T(8,128)(2,1)S(1)}, bf16[16,192]{1,0:T(8,128)(2,1)S(1)}, bf16[192,128]{1,0:T(8,128)(2,1)S(1)}, bf16[128,384]{1,0:T(8,128)(2,...) custom-call(bf16[208,128]{1,0:T(8,128)(2,1)S(1)} %collective-permute, ...), custom_call_target="tpu_custom_call" | custom-call | flops 8000000000 | bytes 8000000 | tf_op jit(solution)/shard_map/pallas_call | solution.py:618
  17.1 0.9 shard_map.148
  18.0 0.4 collective-permute-start.3
  18.4 5.1 %shard_map.149 = (bf16[192,640]{1,0:T(8,128)(2,1)S(1)}, bf16[576,640]{1,0:T(8,128)(2,1)S(1)}, bf16[576,128]{1,0:T(8,128)(2,1)S(1)}, bf16[576,128]{1,0:T(8,128)(2,1)S(1)}) custom-call(s32[1]{0:T(128)} %bitcast.core_ref, s32[1]{0:T(128)} %bitcast.1.first_parent, bf16[192,512]{1,0:T(8,128)(2,1)S(1)} %get-tuple-element.67.refs_4_.rows, ...), custom_call_target="tpu_custom_call" | custom-call | flops 6000000000 | bytes 6000000 | tf_op jit(solution)/shard_map/pallas_call | solution.py:618
  23.5 0.5 collective-permute-start.4
  24.0 1.0 %collective-permute-done.4.fine_got = bf16[576,128]{1,0:T(8,128)(2,1)S(1)} collective-permute-done((bf16[576,128]{1,0:T(8,128)(2,1)S(1)}, bf16[576,128]{1,0:T(8,128)(2,1)S(1)}, u32[]{:S(2)}, u32[]{:S(2)}) %collective-permute-start.4) | collective-permute-done | bytes 147488 | tf_op jit(solution)/shard_map/ppermute | solution.py:32
  25.0 0.0 collective-permute-done.3.got
  25.0 0.3 shard_map.150
  25.3 28.4 %all_to_all.15 = bf16[32,168,128]{2,1,0:T(8,128)(2,1)S(1)} all-to-all(bf16[32,168,128]{2,1,0:T(8,128)(2,1)S(1)} %bitcast.12), channel_id=1, replica_groups=mesh['zh'=4,'zl'=2,'y'=4,'x'=4,'sub'=2] {'zl','y','x'}, dimensions={0} | all-to-all | bytes 2752512 | tf_op jit(solution)/shard_map/all_to_all | solution.py:639
  53.7 0.2 reduce_sum.24
  54.0 14.9 %all_to_all.16 = bf16[4,168,128]{2,1,0:T(8,128)(2,1)S(1)} all-to-all(bf16[4,168,128]{2,1,0:T(8,128)(2,1)S(1)} %broadcast_in_dim.6), channel_id=1, replica_groups=mesh['zh'=4,'zl'=2,'y'=4,'x'=4,'sub'=2] {'zh'}, dimensions={0} | all-to-all | bytes 344064 | tf_op jit(solution)/shard_map/all_to_all | solution.py:641
  68.9 1.3 %broadcast_in_dim.7 = bf16[32,168,128]{2,1,0:T(8,128)(2,1)} broadcast(bf16[168,128]{1,0:T(8,128)(2,1)S(1)} %reduce_sum.25), dimensions={1,2} | broadcast | bytes 1419264 | tf_op jit(solution)/shard_map/broadcast_in_dim | solution.py:643
  70.1 4.8 %all-to-all-start.2 = ((bf16[32,168,128]{2,1,0:T(8,128)(2,1)}), bf16[32,168,128]{2,1,0:T(8,128)(2,1)S(1)}, u32[]{:S(2)}, u32[]{:S(2)}) async-start(bf16[32,168,128]{2,1,0:T(8,128)(2,1)} %broadcast_in_dim.7), calls=%async_computation.2 | async-start | bytes 2752512 | tf_op jit(solution)/shard_map/all_to_all | solution.py:644
  74.9 0.6 shard_map.151
  75.5 0.0 copy-start
  75.5 0.6 copy-done
  76.2 0.0 copy-start.1
  76.2 6.1 %collective-permute-start.5 = (bf16[192,128]{1,0:T(8,128)(2,1)S(1)}, bf16[192,128]{1,0:T(8,128)(2,1)S(1)}, u32[]{:S(2)}, u32[]{:S(2)}) collective-permute-start(bf16[192,128]{1,0:T(8,128)(2,1)S(1)} %get-tuple-element.105), channel_id=1, source_target_pairs={{0,1},{1,2},{2,3},{3,4},{4,5},{5,6},{6,7},{7,8},{8,9},{9,10},{10,1... | collective-permute-start | bytes 147464 | tf_op jit(solution)/shard_map/ppermute | solution.py:28
  82.3 3.2 %collective-permute-done.5.row_late = bf16[192,128]{1,0:T(8,128)(2,1)S(1)} collective-permute-done((bf16[192,128]{1,0:T(8,128)(2,1)S(1)}, bf16[192,128]{1,0:T(8,128)(2,1)S(1)}, u32[]{:S(2)}, u32[]{:S(2)}) %collective-permute-start.5) | collective-permute-done | bytes 49184 | tf_op jit(solution)/shard_map/ppermute | solution.py:28
  85.4 5.9 %all-to-all-done.2 = bf16[32,168,128]{2,1,0:T(8,128)(2,1)S(1)} async-done(((bf16[32,168,128]{2,1,0:T(8,128)(2,1)}), bf16[32,168,128]{2,1,0:T(8,128)(2,1)S(1)}, u32[]{:S(2)}, u32[]{:S(2)}) %all-to-all-start.2) | async-done | bytes 1376288 | tf_op jit(solution)/shard_map/all_to_all | solution.py:644
  91.4 4.9 %collective-permute-start.6 = (bf16[2880,128]{1,0:T(8,128)(2,1)S(1)}, bf16[2880,128]{1,0:T(8,128)(2,1)S(1)}, u32[]{:S(2)}, u32[]{:S(2)}) collective-permute-start(bf16[2880,128]{1,0:T(8,128)(2,1)S(1)} %slice.4), channel_id=1, source_target_pairs={{0,1},{1,0},{2,3},{3,2},{4,5},{5,4},{6,7},{7,6},{8,9},{9,8},{10,11... | collective-permute-start | bytes 2211848 | tf_op jit(solution)/shard_map/ppermute | solution.py:32
  96.3 0.0 copy-done.1
  96.3 1.7 %shard_map.152 = (f32[3,192,384]{2,1,0:T(8,128)}, f32[192,384]{1,0:T(8,128)}, f32[1536,384]{1,0:T(8,128)}, bf16[192,512]{1,0:T(8,128)(2,1)}, bf16[128,384]{1,0:T(8,128)(2,1)}) custom-call(s32[1]{0:T(128)} %bitcast.core_ref, bf16[5376,128]{1,0:T(8,128)(2,1)S(1)} %bitcast.14, f32[192,128]{1,0:T(8,128)S(1)} %copy-done.1, ...), custom_call_target="tpu_custom_call" | custom-call | flops 3000000000 | bytes 3000000 | tf_op jit(solution)/shard_map/pallas_call | solution.py:618
  98.1 0.1 collective-permute-done.6.other
  98.2 1.3 %shard_map.153 = (f32[1536,384]{1,0:T(8,128)}, f32[192,576]{1,0:T(8,128)}, f32[192,192]{1,0:T(8,128)}) custom-call(s32[1]{0:T(128)} %bitcast.core_ref, f32[1536,384]{1,0:T(8,128)} %get-tuple-element.113.pool_in, bf16[5376,128]{1,0:T(8,128)(2,1)S(1)} %bitcast.15, bf16[2880,128]{1,0:T(8,128)(2,1)S(1)} %collective-permute-done.6.other), custom_call_target="tpu_custom_call", output_to_operand_aliasing={{0}: (1, {})} | custom-call | flops 2000000000 | bytes 2000000 | tf_op jit(solution)/shard_map/pallas_call | solution.py:618
  (3 shorter events, 0.1 us)
Async XLA Ops:
  0.7 6.4 %copy-start.3 = (bf16[192,384]{1,0:T(8,128)(2,1)S(1)}, bf16[192,384]{1,0:T(8,128)(2,1)}, u32[]{:S(2)}) copy-start(bf16[192,384]{1,0:T(8,128)(2,1)} %refs_2_.3) | copy-start | bytes 442372
  0.7 6.5 %copy-start.2 = (bf16[3,384,192]{1,2,0:T(8,128)(2,1)S(1)}, bf16[3,384,192]{1,2,0:T(8,128)(2,1)}, u32[]{:S(2)}) copy-start(bf16[3,384,192]{1,2,0:T(8,128)(2,1)} %param.13) | copy-start | bytes 1327108
  1.9 9.8 %collective-permute-start = (bf16[208,128]{1,0:T(8,128)(2,1)S(1)}, bf16[208,128]{1,0:T(8,128)(2,1)S(1)}, u32[]{:S(2)}, u32[]{:S(2)}) collective-permute-start(bf16[208,128]{1,0:T(8,128)(2,1)S(1)} %get-tuple-element.64), channel_id=1, source_target_pairs={{1,0},{2,1},{3,2},{4,3},{5,4},{6,5},{7,6},{8,7},{9,8},{10,9},{11,1... | collective-permute-start | bytes 159752 | tf_op jit(solution)/shard_map/ppermute | solution.py:28
  7.1 3.6 %collective-permute-start.1 = (bf16[192,384]{1,0:T(8,128)(2,1)S(1)}, bf16[192,384]{1,0:T(8,128)(2,1)S(1)}, u32[]{:S(2)}, u32[]{:S(2)}) collective-permute-start(bf16[192,384]{1,0:T(8,128)(2,1)S(1)} %copy-done.3), channel_id=1, source_target_pairs={{0,1},{1,0},{2,3},{3,2},{4,5},{5,4},{6,7},{7,6},{8,9},{9,8},{10,11... | collective-permute-start | bytes 442376 | tf_op jit(solution)/shard_map/ppermute | solution.py:32
  7.2 4.5 %collective-permute-start.2 = (bf16[576,384]{1,0:T(8,128)(2,1)S(1)}, bf16[576,384]{1,0:T(8,128)(2,1)S(1)}, u32[]{:S(2)}, u32[]{:S(2)}) collective-permute-start(bf16[576,384]{1,0:T(8,128)(2,1)S(1)} %bitcast.17), channel_id=1, source_target_pairs={{0,1},{1,0},{2,3},{3,2},{4,5},{5,4},{6,7},{7,6},{8,9},{9,8},{10,11... | collective-permute-start | bytes 1327112 | tf_op jit(solution)/shard_map/ppermute | solution.py:32
  18.0 7.0 %collective-permute-start.3 = (bf16[4608,128]{1,0:T(8,128)(2,1)S(1)}, bf16[4608,128]{1,0:T(8,128)(2,1)S(1)}, u32[]{:S(2)}, u32[]{:S(2)}) collective-permute-start(bf16[4608,128]{1,0:T(8,128)(2,1)S(1)} %get-tuple-element.86), channel_id=1, source_target_pairs={{0,1},{1,0},{2,3},{3,2},{4,5},{5,4},{6,7},{7,6},{8,9},{9,8},{10,11... | collective-permute-start | bytes 3538952 | tf_op jit(solution)/shard_map/ppermute | solution.py:32
  23.5 1.5 %collective-permute-start.4 = (bf16[576,128]{1,0:T(8,128)(2,1)S(1)}, bf16[576,128]{1,0:T(8,128)(2,1)S(1)}, u32[]{:S(2)}, u32[]{:S(2)}) collective-permute-start(bf16[576,128]{1,0:T(8,128)(2,1)S(1)} %get-tuple-element.98), channel_id=1, source_target_pairs={{0,1},{1,0},{2,3},{3,2},{4,5},{5,4},{6,7},{7,6},{8,9},{9,8},{10,11... | collective-permute-start | bytes 442376 | tf_op jit(solution)/shard_map/ppermute | solution.py:32
  70.1 21.2 %all-to-all-start.2 = ((bf16[32,168,128]{2,1,0:T(8,128)(2,1)}), bf16[32,168,128]{2,1,0:T(8,128)(2,1)S(1)}, u32[]{:S(2)}, u32[]{:S(2)}) async-start(bf16[32,168,128]{2,1,0:T(8,128)(2,1)} %broadcast_in_dim.7), calls=%async_computation.2 | async-start | bytes 2752512 | tf_op jit(solution)/shard_map/all_to_all | solution.py:644
  75.5 0.6 copy-start
  76.2 20.2 %copy-start.1 = (f32[192,128]{1,0:T(8,128)S(1)}, f32[192,128]{1,0:T(8,128)}, u32[]{:S(2)}) copy-start(f32[192,128]{1,0:T(8,128)} %copy-done) | copy-start | bytes 294916
  76.2 9.3 %collective-permute-start.5 = (bf16[192,128]{1,0:T(8,128)(2,1)S(1)}, bf16[192,128]{1,0:T(8,128)(2,1)S(1)}, u32[]{:S(2)}, u32[]{:S(2)}) collective-permute-start(bf16[192,128]{1,0:T(8,128)(2,1)S(1)} %get-tuple-element.105), channel_id=1, source_target_pairs={{0,1},{1,2},{2,3},{3,4},{4,5},{5,6},{6,7},{7,8},{8,9},{9,10},{10,1... | collective-permute-start | bytes 147464 | tf_op jit(solution)/shard_map/ppermute | solution.py:28
  91.4 6.8 %collective-permute-start.6 = (bf16[2880,128]{1,0:T(8,128)(2,1)S(1)}, bf16[2880,128]{1,0:T(8,128)(2,1)S(1)}, u32[]{:S(2)}, u32[]{:S(2)}) collective-permute-start(bf16[2880,128]{1,0:T(8,128)(2,1)S(1)} %slice.4), channel_id=1, source_target_pairs={{0,1},{1,0},{2,3},{3,2},{4,5},{5,4},{6,7},{7,6},{8,9},{9,8},{10,11... | collective-permute-start | bytes 2211848 | tf_op jit(solution)/shard_map/ppermute | solution.py:32

commit v8 on v7

--- a/solution.py
+++ b/solution.py
@@ -104,14 +104,29 @@
     return (bround(exponent), 1.0 / jnp.sum(exponent, 0, keepdims=True))
 
 
-def attend_back(query, key, upstream, exponent, inverse, grad_prob):
-    weighted = exponent.astype(jnp.float32)
-    mean = inverse * jnp.sum(weighted * grad_prob, 0, keepdims=True)
-    grad_score = bround(weighted * (grad_prob - mean))
-    grad_value = nt(bround(upstream.astype(jnp.float32) * inverse), exponent)
-    grad_query = nn(key, grad_score)
-    grad_key = nt(query, grad_score)
-    return (bround(grad_query), bround(grad_key), bround(grad_value))
+def diagonal(product):
+    return jnp.concatenate([product[:HD, :LANES], product[HD:, LANES:]], 0)
+
+
+def mix_pair(values, parts):
+    exponents = jnp.concatenate([exponent for exponent, _ in parts], 1)
+    scales = [jnp.broadcast_to(inverse, (HD, LANES)) for _, inverse in parts]
+    return bround(diagonal(nn(values, exponents)) * jnp.concatenate(scales, 0))
+
+
+def attend_back(query, key, upstream, parts, grad_probs):
+    scores, scales = [], []
+    for i, (exponent, inverse) in enumerate(parts):
+        grad_prob = grad_probs[:, i * LANES : (i + 1) * LANES]
+        weighted = exponent.astype(jnp.float32)
+        mean = inverse * jnp.sum(weighted * grad_prob, 0, keepdims=True)
+        scores.append(bround(weighted * (grad_prob - mean)))
+        scales.append(jnp.broadcast_to(inverse, (HD, LANES)))
+    spread_up = bround(upstream.astype(jnp.float32) * jnp.concatenate(scales, 0))
+    grad_value = nt(spread_up, jnp.concatenate([exponent for exponent, _ in parts], 0))
+    grad_query = nn(key, jnp.concatenate(scores, 1))
+    grad_key = nt(query, jnp.concatenate(scores, 0))
+    return tuple(bround(diagonal(grad)) for grad in (grad_query, grad_key, grad_value))
 
 
 def scaled(value):
@@ -123,12 +138,14 @@
     spread(wide, scaled(qkv[:channels]), heads)
     keys = jnp.concatenate([qkv[channels : 2 * channels], classes], 0)
     scores = tn(keys, wide[...])
-    for head in range(heads):
-        exponent, inverse = softmax_parts(scores[:, head * LANES : (head + 1) * LANES])
-        value = qkv[2 * channels + head * HD : 2 * channels + (head + 1) * HD]
-        mixed[head * HD : (head + 1) * HD] = bround(nn(value, exponent) * inverse)
-        if store is not None:
-            store(head, exponent, inverse)
+    for head in range(0, heads, 2):
+        parts = [
+            softmax_parts(scores[:, at * LANES : (at + 1) * LANES]) for at in (head, head + 1)
+        ]
+        values = qkv[2 * channels + head * HD : 2 * channels + (head + 2) * HD]
+        mixed[head * HD : (head + 2) * HD] = mix_pair(values, parts)
+        for i in range(2):
+            store(head + i, *parts[i])
 
 
 def clear_wide(wide, heads, window_of):
@@ -310,25 +327,30 @@
     ]
     parts = {}
     for half in halves:
-        for head in range(heads):
-            at = slice(head * HD, (head + 1) * HD)
-            lanes = slice(head * LANES, (head + 1) * LANES)
-            exponent, scale = softmax_parts(scores[half][:, lanes])
-            parts[half, head] = (exponent, scale)
-            value = qkvs[half][2 * part + head * HD : 2 * part + (head + 1) * HD]
-            mixed[half, at] = bround(nn(value, exponent) * scale)
-            weighted = scaled(upward[half, at]).astype(jnp.float32) * scale
-            wide_grad[half, at, lanes] = bround(weighted)
+        for head in range(0, heads, 2):
+            at = slice(head * HD, (head + 2) * HD)
+            pair = [
+                softmax_parts(scores[half][:, i * LANES : (i + 1) * LANES])
+                for i in (head, head + 1)
+            ]
+            parts[half, head] = pair
+            values = qkvs[half][2 * part + head * HD : 2 * part + (head + 2) * HD]
+            mixed[half, at] = mix_pair(values, pair)
+            for i in range(2):
+                rows = slice((head + i) * HD, (head + i + 1) * HD)
+                lanes = slice((head + i) * LANES, (head + i + 1) * LANES)
+                weighted = scaled(upward[half, rows]).astype(jnp.float32) * pair[i][1]
+                wide_grad[half, rows, lanes] = bround(weighted)
     grad_probs = [tn(qkvs[half][2 * part :], wide_grad[half]) for half in halves]
     for half in halves:
-        for head in range(heads):
-            at = [slice(i * part + head * HD, i * part + (head + 1) * HD) for i in range(3)]
+        for head in range(0, heads, 2):
+            at = [slice(i * part + head * HD, i * part + (head + 2) * HD) for i in range(3)]
             back = attend_back(
                 qkvs[half][at[0]],
                 qkvs[half][at[1]],
                 upward[half, at[0]],
-                *parts[half, head],
-                grad_probs[half][:, head * LANES : (head + 1) * LANES],
+                parts[half, head],
+                grad_probs[half][:, head * LANES : (head + 2) * LANES],
             )
             for which in range(3):
                 grads[half, at[which]] = back[which]
@@ -435,16 +457,18 @@
             weighted = scaled(upward[at, lanes]).astype(jnp.float32) * scales[head]
             grad_rows[at, head * LANES : (head + 1) * LANES] = bround(weighted)
         grad_probs = tn(qkv[2 * channels :, inner], grad_rows[...])
-        for head in range(heads):
-            at = [slice(i * channels + head * HD, i * channels + (head + 1) * HD) for i in range(3)]
-            out = slice(head * LANES, (head + 1) * LANES)
+        for head in range(0, heads, 2):
+            at = [slice(i * channels + head * HD, i * channels + (head + 2) * HD) for i in range(3)]
+            parts = [
+                (exponents[within, :, i * LANES : (i + 1) * LANES], scales[i])
+                for i in (head, head + 1)
+            ]
             back = attend_back(
                 qkv[at[0], inner],
                 qkv[at[1], inner],
                 upward[at[0], lanes],
-                exponents[within, :, out],
-                scales[head],
-                grad_probs[:, out],
+                parts,
+                grad_probs[:, head * LANES : (head + 2) * LANES],
             )
             for which in range(3):
                 grads[at[which], lanes] = back[which]

time: 100 us -> 98.3 us (0.983)
  Pallas kernels: 20.6 us -> 19.3 us
    pallas_call x10, Pallas kernels: 20.6 us -> 19.3 us  [call(): pl.pallas_call(kernel, out_shape=[jax.ShapeDtypeStruct(shape, dtype) for...]
where the time goes in v8:
time: 98.3 us; the launch traced here: 97.9 us
  blocking collectives  42.8 us (44%)
  starting transfers between devices  22.4 us (23%)
  Pallas kernels  19.3 us (20%)
  waiting for transfers between devices  10.2 us (10%)
  local copies, waits for them, and re-layouts  1.98 us (2%)
  between operations  0.99 us (1%)
    all_to_all x1, blocking collectives, sum_over_chips(): slab = float_sum(lax.all_to_all(parts, NEAR, 0, 0, tiled=True))  27.9 us
    pallas_call x10, Pallas kernels, call(): pl.pallas_call(kernel, out_shape=[jax.ShapeDtypeStruct(shape, dtype) for...  19.3 us
    all_to_all x1, blocking collectives, sum_over_chips(): slab = float_sum(lax.all_to_all(copies, 'zh', 0, 0, tiled=True))  14.9 us
    ppermute x2, starting transfers between devices, passed_along(): return lax.ppermute(shard, AXES, pairs)  11.3 us
    ppermute x5, starting transfers between devices, swap_cores(): return lax.ppermute(shard, 'sub', [(0, 1), (1, 0)])  6.38 us
    all_to_all x1, waiting for transfers between devices, sum_over_chips(): total = lax.all_to_all(copies, NEAR, 0, 0, tiled=True)  5.91 us
    all_to_all x1, starting transfers between devices, sum_over_chips(): total = lax.all_to_all(copies, NEAR, 0, 0, tiled=True)  4.77 us
    ppermute x2, waiting for transfers between devices, passed_along(): return lax.ppermute(shard, AXES, pairs)  3.15 us
  transfers between devices with their start and end apart: 8, of which 4 were waited for; matrix products, arithmetic and copies ran while one was open for 0% of the time, Pallas kernels for 11%

profile of v8, /device:TPU:1, one launch (start us, length us, event | category | flops | bytes accessed | tf_op | source)
XLA Modules:
  0.0 97.9 jit_solution(1812309361014694218)
XLA Ops:
  0.7 0.0 copy-start.3
  0.7 0.0 copy-start.2
  0.7 1.2 %shard_map.144 = (bf16[192,512]{1,0:T(8,128)(2,1)S(1)}, bf16[192,576]{1,0:T(8,128)(2,1)S(1)}, bf16[192,192]{1,0:T(8,128)(2,1)S(1)}, s32[1,512]{1,0:T(1,128)S(1)}...) custom-call(s32[1]{0:T(128)} %bitcast.1.first_parent, bf16[192,512]{1,0:T(8,128)(2,1)} %bitcast.18, ...), custom_call_target="tpu_custom_call" | custom-call | flops 1000000000 | bytes 1000000 | tf_op jit(solution)/shard_map/pallas_call | solution.py:642
  1.9 5.1 %collective-permute-start = (bf16[208,128]{1,0:T(8,128)(2,1)S(1)}, bf16[208,128]{1,0:T(8,128)(2,1)S(1)}, u32[]{:S(2)}, u32[]{:S(2)}) collective-permute-start(bf16[208,128]{1,0:T(8,128)(2,1)S(1)} %get-tuple-element.64), channel_id=1, source_target_pairs={{1,0},{2,1},{3,2},{4,3},{5,4},{6,5},{7,6},{8,7},{9,8},{10,9},{11,1... | collective-permute-start | bytes 159752 | tf_op jit(solution)/shard_map/ppermute | solution.py:28
  7.0 0.0 copy-done.3
  7.1 0.1 collective-permute-start.1
  7.2 0.0 copy-done.2
  7.2 0.5 collective-permute-start.2
  7.7 3.6 %shard_map.145 = (bf16[1536,384]{1,0:T(8,128)(2,1)S(1)}, bf16[576,384]{1,0:T(8,128)(2,1)S(1)}, bf16[192,384]{1,0:T(8,128)(2,1)S(1)}, bf16[128,384]{1,0:T(8,128)(...) custom-call(bf16[1536,384]{1,0:T(8,128)(2,1)} %refs_0_.1, ...), custom_call_target="tpu_custom_call" | custom-call | flops 4000000000 | bytes 4000000 | tf_op jit(solution)/shard_map/pallas_call | solution.py:642
  11.3 0.0 collective-permute-done.1.other_out
  11.3 1.0 shard_map.146
  12.2 0.0 collective-permute-done.packed
  12.2 0.0 collective-permute-done.2.other_qkv
  12.3 4.9 %shard_map.147 = (bf16[128,384]{1,0:T(8,128)(2,1)S(1)}, bf16[16,192]{1,0:T(8,128)(2,1)S(1)}, bf16[192,128]{1,0:T(8,128)(2,1)S(1)}, bf16[128,384]{1,0:T(8,128)(2,...) custom-call(bf16[208,128]{1,0:T(8,128)(2,1)S(1)} %collective-permute, ...), custom_call_target="tpu_custom_call" | custom-call | flops 8000000000 | bytes 8000000 | tf_op jit(solution)/shard_map/pallas_call | solution.py:642
  17.2 0.9 shard_map.148
  18.1 0.2 collective-permute-start.3
  18.3 3.8 %shard_map.149 = (bf16[192,640]{1,0:T(8,128)(2,1)S(1)}, bf16[576,640]{1,0:T(8,128)(2,1)S(1)}, bf16[576,128]{1,0:T(8,128)(2,1)S(1)}, bf16[576,128]{1,0:T(8,128)(2,1)S(1)}) custom-call(s32[1]{0:T(128)} %bitcast.core_ref, s32[1]{0:T(128)} %bitcast.1.first_parent, bf16[192,512]{1,0:T(8,128)(2,1)S(1)} %get-tuple-element.67.refs_4_.rows, ...), custom_call_target="tpu_custom_call" | custom-call | flops 6000000000 | bytes 6000000 | tf_op jit(solution)/shard_map/pallas_call | solution.py:642
  22.1 0.7 collective-permute-start.4
  22.8 1.0 %collective-permute-done.4.fine_got = bf16[576,128]{1,0:T(8,128)(2,1)S(1)} collective-permute-done((bf16[576,128]{1,0:T(8,128)(2,1)S(1)}, bf16[576,128]{1,0:T(8,128)(2,1)S(1)}, u32[]{:S(2)}, u32[]{:S(2)}) %collective-permute-start.4) | collective-permute-done | bytes 147488 | tf_op jit(solution)/shard_map/ppermute | solution.py:32
  23.8 0.0 collective-permute-done.3.got
  23.8 0.3 shard_map.150
  24.1 27.9 %all_to_all.15 = bf16[32,168,128]{2,1,0:T(8,128)(2,1)S(1)} all-to-all(bf16[32,168,128]{2,1,0:T(8,128)(2,1)S(1)} %bitcast.12), channel_id=1, replica_groups=mesh['zh'=4,'zl'=2,'y'=4,'x'=4,'sub'=2] {'zl','y','x'}, dimensions={0} | all-to-all | bytes 2752512 | tf_op jit(solution)/shard_map/all_to_all | solution.py:663
  52.0 0.2 reduce_sum.24
  52.2 14.9 %all_to_all.16 = bf16[4,168,128]{2,1,0:T(8,128)(2,1)S(1)} all-to-all(bf16[4,168,128]{2,1,0:T(8,128)(2,1)S(1)} %broadcast_in_dim.6), channel_id=1, replica_groups=mesh['zh'=4,'zl'=2,'y'=4,'x'=4,'sub'=2] {'zh'}, dimensions={0} | all-to-all | bytes 344064 | tf_op jit(solution)/shard_map/all_to_all | solution.py:665
  67.1 1.3 %broadcast_in_dim.7 = bf16[32,168,128]{2,1,0:T(8,128)(2,1)} broadcast(bf16[168,128]{1,0:T(8,128)(2,1)S(1)} %reduce_sum.25), dimensions={1,2} | broadcast | bytes 1419264 | tf_op jit(solution)/shard_map/broadcast_in_dim | solution.py:667
  68.4 4.8 %all-to-all-start.2 = ((bf16[32,168,128]{2,1,0:T(8,128)(2,1)}), bf16[32,168,128]{2,1,0:T(8,128)(2,1)S(1)}, u32[]{:S(2)}, u32[]{:S(2)}) async-start(bf16[32,168,128]{2,1,0:T(8,128)(2,1)} %broadcast_in_dim.7), calls=%async_computation.2 | async-start | bytes 2752512 | tf_op jit(solution)/shard_map/all_to_all | solution.py:668
  73.2 0.6 shard_map.151
  73.7 0.0 copy-start
  73.7 0.6 copy-done
  74.4 0.0 copy-start.1
  74.4 6.1 %collective-permute-start.5 = (bf16[192,128]{1,0:T(8,128)(2,1)S(1)}, bf16[192,128]{1,0:T(8,128)(2,1)S(1)}, u32[]{:S(2)}, u32[]{:S(2)}) collective-permute-start(bf16[192,128]{1,0:T(8,128)(2,1)S(1)} %get-tuple-element.105), channel_id=1, source_target_pairs={{0,1},{1,2},{2,3},{3,4},{4,5},{5,6},{6,7},{7,8},{8,9},{9,10},{10,1... | collective-permute-start | bytes 147464 | tf_op jit(solution)/shard_map/ppermute | solution.py:28
  80.5 3.2 %collective-permute-done.5.row_late = bf16[192,128]{1,0:T(8,128)(2,1)S(1)} collective-permute-done((bf16[192,128]{1,0:T(8,128)(2,1)S(1)}, bf16[192,128]{1,0:T(8,128)(2,1)S(1)}, u32[]{:S(2)}, u32[]{:S(2)}) %collective-permute-start.5) | collective-permute-done | bytes 49184 | tf_op jit(solution)/shard_map/ppermute | solution.py:28
  83.6 5.9 %all-to-all-done.2 = bf16[32,168,128]{2,1,0:T(8,128)(2,1)S(1)} async-done(((bf16[32,168,128]{2,1,0:T(8,128)(2,1)}), bf16[32,168,128]{2,1,0:T(8,128)(2,1)S(1)}, u32[]{:S(2)}, u32[]{:S(2)}) %all-to-all-start.2) | async-done | bytes 1376288 | tf_op jit(solution)/shard_map/all_to_all | solution.py:668
  89.6 4.9 %collective-permute-start.6 = (bf16[2880,128]{1,0:T(8,128)(2,1)S(1)}, bf16[2880,128]{1,0:T(8,128)(2,1)S(1)}, u32[]{:S(2)}, u32[]{:S(2)}) collective-permute-start(bf16[2880,128]{1,0:T(8,128)(2,1)S(1)} %slice.4), channel_id=1, source_target_pairs={{0,1},{1,0},{2,3},{3,2},{4,5},{5,4},{6,7},{7,6},{8,9},{9,8},{10,11... | collective-permute-start | bytes 2211848 | tf_op jit(solution)/shard_map/ppermute | solution.py:32
  94.5 0.0 copy-done.1
  94.5 1.7 %shard_map.152 = (f32[3,192,384]{2,1,0:T(8,128)}, f32[192,384]{1,0:T(8,128)}, f32[1536,384]{1,0:T(8,128)}, bf16[192,512]{1,0:T(8,128)(2,1)}, bf16[128,384]{1,0:T(8,128)(2,1)}) custom-call(s32[1]{0:T(128)} %bitcast.core_ref, bf16[5376,128]{1,0:T(8,128)(2,1)S(1)} %bitcast.14, f32[192,128]{1,0:T(8,128)S(1)} %copy-done.1, ...), custom_call_target="tpu_custom_call" | custom-call | flops 3000000000 | bytes 3000000 | tf_op jit(solution)/shard_map/pallas_call | solution.py:642
  96.3 0.1 collective-permute-done.6.other
  96.4 1.3 %shard_map.153 = (f32[1536,384]{1,0:T(8,128)}, f32[192,576]{1,0:T(8,128)}, f32[192,192]{1,0:T(8,128)}) custom-call(s32[1]{0:T(128)} %bitcast.core_ref, f32[1536,384]{1,0:T(8,128)} %get-tuple-element.113.pool_in, bf16[5376,128]{1,0:T(8,128)(2,1)S(1)} %bitcast.15, bf16[2880,128]{1,0:T(8,128)(2,1)S(1)} %collective-permute-done.6.other), custom_call_target="tpu_custom_call", output_to_operand_aliasing={{0}: (1, {})} | custom-call | flops 2000000000 | bytes 2000000 | tf_op jit(solution)/shard_map/pallas_call | solution.py:642
  (3 shorter events, 0.1 us)
Async XLA Ops:
  0.7 6.4 %copy-start.3 = (bf16[192,384]{1,0:T(8,128)(2,1)S(1)}, bf16[192,384]{1,0:T(8,128)(2,1)}, u32[]{:S(2)}) copy-start(bf16[192,384]{1,0:T(8,128)(2,1)} %refs_2_.3) | copy-start | bytes 442372
  0.7 6.5 %copy-start.2 = (bf16[3,384,192]{1,2,0:T(8,128)(2,1)S(1)}, bf16[3,384,192]{1,2,0:T(8,128)(2,1)}, u32[]{:S(2)}) copy-start(bf16[3,384,192]{1,2,0:T(8,128)(2,1)} %param.13) | copy-start | bytes 1327108
  1.9 10.3 %collective-permute-start = (bf16[208,128]{1,0:T(8,128)(2,1)S(1)}, bf16[208,128]{1,0:T(8,128)(2,1)S(1)}, u32[]{:S(2)}, u32[]{:S(2)}) collective-permute-start(bf16[208,128]{1,0:T(8,128)(2,1)S(1)} %get-tuple-element.64), channel_id=1, source_target_pairs={{1,0},{2,1},{3,2},{4,3},{5,4},{6,5},{7,6},{8,7},{9,8},{10,9},{11,1... | collective-permute-start | bytes 159752 | tf_op jit(solution)/shard_map/ppermute | solution.py:28
  7.1 4.2 %collective-permute-start.1 = (bf16[192,384]{1,0:T(8,128)(2,1)S(1)}, bf16[192,384]{1,0:T(8,128)(2,1)S(1)}, u32[]{:S(2)}, u32[]{:S(2)}) collective-permute-start(bf16[192,384]{1,0:T(8,128)(2,1)S(1)} %copy-done.3), channel_id=1, source_target_pairs={{0,1},{1,0},{2,3},{3,2},{4,5},{5,4},{6,7},{7,6},{8,9},{9,8},{10,11... | collective-permute-start | bytes 442376 | tf_op jit(solution)/shard_map/ppermute | solution.py:32
  7.2 5.1 %collective-permute-start.2 = (bf16[576,384]{1,0:T(8,128)(2,1)S(1)}, bf16[576,384]{1,0:T(8,128)(2,1)S(1)}, u32[]{:S(2)}, u32[]{:S(2)}) collective-permute-start(bf16[576,384]{1,0:T(8,128)(2,1)S(1)} %bitcast.17), channel_id=1, source_target_pairs={{0,1},{1,0},{2,3},{3,2},{4,5},{5,4},{6,7},{7,6},{8,9},{9,8},{10,11... | collective-permute-start | bytes 1327112 | tf_op jit(solution)/shard_map/ppermute | solution.py:32
  18.1 5.7 %collective-permute-start.3 = (bf16[4608,128]{1,0:T(8,128)(2,1)S(1)}, bf16[4608,128]{1,0:T(8,128)(2,1)S(1)}, u32[]{:S(2)}, u32[]{:S(2)}) collective-permute-start(bf16[4608,128]{1,0:T(8,128)(2,1)S(1)} %get-tuple-element.86), channel_id=1, source_target_pairs={{0,1},{1,0},{2,3},{3,2},{4,5},{5,4},{6,7},{7,6},{8,9},{9,8},{10,11... | collective-permute-start | bytes 3538952 | tf_op jit(solution)/shard_map/ppermute | solution.py:32
  22.1 1.7 %collective-permute-start.4 = (bf16[576,128]{1,0:T(8,128)(2,1)S(1)}, bf16[576,128]{1,0:T(8,128)(2,1)S(1)}, u32[]{:S(2)}, u32[]{:S(2)}) collective-permute-start(bf16[576,128]{1,0:T(8,128)(2,1)S(1)} %get-tuple-element.98), channel_id=1, source_target_pairs={{0,1},{1,0},{2,3},{3,2},{4,5},{5,4},{6,7},{7,6},{8,9},{9,8},{10,11... | collective-permute-start | bytes 442376 | tf_op jit(solution)/shard_map/ppermute | solution.py:32
  68.4 21.2 %all-to-all-start.2 = ((bf16[32,168,128]{2,1,0:T(8,128)(2,1)}), bf16[32,168,128]{2,1,0:T(8,128)(2,1)S(1)}, u32[]{:S(2)}, u32[]{:S(2)}) async-start(bf16[32,168,128]{2,1,0:T(8,128)(2,1)} %broadcast_in_dim.7), calls=%async_computation.2 | async-start | bytes 2752512 | tf_op jit(solution)/shard_map/all_to_all | solution.py:668
  73.7 0.6 copy-start
  74.4 20.2 %copy-start.1 = (f32[192,128]{1,0:T(8,128)S(1)}, f32[192,128]{1,0:T(8,128)}, u32[]{:S(2)}) copy-start(f32[192,128]{1,0:T(8,128)} %copy-done) | copy-start | bytes 294916
  74.4 9.3 %collective-permute-start.5 = (bf16[192,128]{1,0:T(8,128)(2,1)S(1)}, bf16[192,128]{1,0:T(8,128)(2,1)S(1)}, u32[]{:S(2)}, u32[]{:S(2)}) collective-permute-start(bf16[192,128]{1,0:T(8,128)(2,1)S(1)} %get-tuple-element.105), channel_id=1, source_target_pairs={{0,1},{1,2},{2,3},{3,4},{4,5},{5,6},{6,7},{7,8},{8,9},{9,10},{10,1... | collective-permute-start | bytes 147464 | tf_op jit(solution)/shard_map/ppermute | solution.py:28
  89.6 6.8 %collective-permute-start.6 = (bf16[2880,128]{1,0:T(8,128)(2,1)S(1)}, bf16[2880,128]{1,0:T(8,128)(2,1)S(1)}, u32[]{:S(2)}, u32[]{:S(2)}) collective-permute-start(bf16[2880,128]{1,0:T(8,128)(2,1)S(1)} %slice.4), channel_id=1, source_target_pairs={{0,1},{1,0},{2,3},{3,2},{4,5},{5,4},{6,7},{7,6},{8,9},{9,8},{10,11... | collective-permute-start | bytes 2211848 | tf_op jit(solution)/shard_map/ppermute | solution.py:32

commit v9 on v8

--- a/solution.py
+++ b/solution.py
@@ -109,9 +109,11 @@
 
 
 def mix_pair(values, parts):
-    exponents = jnp.concatenate([exponent for exponent, _ in parts], 1)
-    scales = [jnp.broadcast_to(inverse, (HD, LANES)) for _, inverse in parts]
-    return bround(diagonal(nn(values, exponents)) * jnp.concatenate(scales, 0))
+    mixed = [
+        nn(values[i * HD : (i + 1) * HD], exponent) * inverse
+        for i, (exponent, inverse) in enumerate(parts)
+    ]
+    return bround(jnp.concatenate(mixed, 0))
 
 
 def attend_back(query, key, upstream, parts, grad_probs):

time: 98.3 us -> 98.3 us (level)
  transfers between devices with their start and end apart: 8 -> 8, of which waited for: 4 -> 4; matrix products, arithmetic and copies ran while one was open for 0% -> 0% of each run, Pallas kernels for 11% -> 10%
where the time goes in v9:
time: 98.3 us; the launch traced here: 97.9 us
  blocking collectives  43.3 us (44%)
  starting transfers between devices  22.4 us (23%)
  Pallas kernels  18.8 us (19%)
  waiting for transfers between devices  10.2 us (10%)
  local copies, waits for them, and re-layouts  1.98 us (2%)
  between operations  0.99 us (1%)
    all_to_all x1, blocking collectives, sum_over_chips(): slab = float_sum(lax.all_to_all(parts, NEAR, 0, 0, tiled=True))  28.4 us
    pallas_call x10, Pallas kernels, call(): pl.pallas_call(kernel, out_shape=[jax.ShapeDtypeStruct(shape, dtype) for...  18.8 us
    all_to_all x1, blocking collectives, sum_over_chips(): slab = float_sum(lax.all_to_all(copies, 'zh', 0, 0, tiled=True))  14.9 us
    ppermute x2, starting transfers between devices, passed_along(): return lax.ppermute(shard, AXES, pairs)  11.3 us
    ppermute x5, starting transfers between devices, swap_cores(): return lax.ppermute(shard, 'sub', [(0, 1), (1, 0)])  6.38 us
    all_to_all x1, waiting for transfers between devices, sum_over_chips(): total = lax.all_to_all(copies, NEAR, 0, 0, tiled=True)  5.91 us
    all_to_all x1, starting transfers between devices, sum_over_chips(): total = lax.all_to_all(copies, NEAR, 0, 0, tiled=True)  4.77 us
    ppermute x2, waiting for transfers between devices, passed_along(): return lax.ppermute(shard, AXES, pairs)  3.15 us
  transfers between devices with their start and end apart: 8, of which 4 were waited for; matrix products, arithmetic and copies ran while one was open for 0% of the time, Pallas kernels for 10%

profile of v9, /device:TPU:1, one launch (start us, length us, event | category | flops | bytes accessed | tf_op | source)
XLA Modules:
  0.0 97.9 jit_solution(6043016595830424121)
XLA Ops:
  0.7 0.0 copy-start.3
  0.7 0.0 copy-start.2
  0.7 1.2 %shard_map.144 = (bf16[192,512]{1,0:T(8,128)(2,1)S(1)}, bf16[192,576]{1,0:T(8,128)(2,1)S(1)}, bf16[192,192]{1,0:T(8,128)(2,1)S(1)}, s32[1,512]{1,0:T(1,128)S(1)}...) custom-call(s32[1]{0:T(128)} %bitcast.1.first_parent, bf16[192,512]{1,0:T(8,128)(2,1)} %bitcast.18, ...), custom_call_target="tpu_custom_call" | custom-call | flops 1000000000 | bytes 1000000 | tf_op jit(solution)/shard_map/pallas_call | solution.py:644
  1.9 5.1 %collective-permute-start = (bf16[208,128]{1,0:T(8,128)(2,1)S(1)}, bf16[208,128]{1,0:T(8,128)(2,1)S(1)}, u32[]{:S(2)}, u32[]{:S(2)}) collective-permute-start(bf16[208,128]{1,0:T(8,128)(2,1)S(1)} %get-tuple-element.64), channel_id=1, source_target_pairs={{1,0},{2,1},{3,2},{4,3},{5,4},{6,5},{7,6},{8,7},{9,8},{10,9},{11,1... | collective-permute-start | bytes 159752 | tf_op jit(solution)/shard_map/ppermute | solution.py:28
  7.0 0.0 copy-done.3
  7.1 0.1 collective-permute-start.1
  7.2 0.0 copy-done.2
  7.2 0.5 collective-permute-start.2
  7.7 3.0 %shard_map.145 = (bf16[1536,384]{1,0:T(8,128)(2,1)S(1)}, bf16[576,384]{1,0:T(8,128)(2,1)S(1)}, bf16[192,384]{1,0:T(8,128)(2,1)S(1)}, bf16[128,384]{1,0:T(8,128)(...) custom-call(bf16[1536,384]{1,0:T(8,128)(2,1)} %refs_0_.1, ...), custom_call_target="tpu_custom_call" | custom-call | flops 4000000000 | bytes 4000000 | tf_op jit(solution)/shard_map/pallas_call | solution.py:644
  10.7 0.0 collective-permute-done.1.other_out
  10.7 1.0 shard_map.146
  11.7 0.0 collective-permute-done.packed
  11.7 0.0 collective-permute-done.2.other_qkv
  11.7 5.0 %shard_map.147 = (bf16[128,384]{1,0:T(8,128)(2,1)S(1)}, bf16[16,192]{1,0:T(8,128)(2,1)S(1)}, bf16[192,128]{1,0:T(8,128)(2,1)S(1)}, bf16[128,384]{1,0:T(8,128)(2,...) custom-call(bf16[208,128]{1,0:T(8,128)(2,1)S(1)} %collective-permute, ...), custom_call_target="tpu_custom_call" | custom-call | flops 8000000000 | bytes 8000000 | tf_op jit(solution)/shard_map/pallas_call | solution.py:644
  16.7 0.9 shard_map.148
  17.6 0.2 collective-permute-start.3
  17.8 3.8 %shard_map.149 = (bf16[192,640]{1,0:T(8,128)(2,1)S(1)}, bf16[576,640]{1,0:T(8,128)(2,1)S(1)}, bf16[576,128]{1,0:T(8,128)(2,1)S(1)}, bf16[576,128]{1,0:T(8,128)(2,1)S(1)}) custom-call(s32[1]{0:T(128)} %bitcast.core_ref, s32[1]{0:T(128)} %bitcast.1.first_parent, bf16[192,512]{1,0:T(8,128)(2,1)S(1)} %get-tuple-element.67.refs_4_.rows, ...), custom_call_target="tpu_custom_call" | custom-call | flops 6000000000 | bytes 6000000 | tf_op jit(solution)/shard_map/pallas_call | solution.py:644
  21.6 0.7 collective-permute-start.4
  22.3 1.0 %collective-permute-done.4.fine_got = bf16[576,128]{1,0:T(8,128)(2,1)S(1)} collective-permute-done((bf16[576,128]{1,0:T(8,128)(2,1)S(1)}, bf16[576,128]{1,0:T(8,128)(2,1)S(1)}, u32[]{:S(2)}, u32[]{:S(2)}) %collective-permute-start.4) | collective-permute-done | bytes 147488 | tf_op jit(solution)/shard_map/ppermute | solution.py:32
  23.3 0.0 collective-permute-done.3.got
  23.3 0.3 shard_map.150
  23.6 28.4 %all_to_all.15 = bf16[32,168,128]{2,1,0:T(8,128)(2,1)S(1)} all-to-all(bf16[32,168,128]{2,1,0:T(8,128)(2,1)S(1)} %bitcast.12), channel_id=1, replica_groups=mesh['zh'=4,'zl'=2,'y'=4,'x'=4,'sub'=2] {'zl','y','x'}, dimensions={0} | all-to-all | bytes 2752512 | tf_op jit(solution)/shard_map/all_to_all | solution.py:665
  52.0 0.2 reduce_sum.24
  52.2 14.9 %all_to_all.16 = bf16[4,168,128]{2,1,0:T(8,128)(2,1)S(1)} all-to-all(bf16[4,168,128]{2,1,0:T(8,128)(2,1)S(1)} %broadcast_in_dim.6), channel_id=1, replica_groups=mesh['zh'=4,'zl'=2,'y'=4,'x'=4,'sub'=2] {'zh'}, dimensions={0} | all-to-all | bytes 344064 | tf_op jit(solution)/shard_map/all_to_all | solution.py:667
  67.2 1.3 %broadcast_in_dim.7 = bf16[32,168,128]{2,1,0:T(8,128)(2,1)} broadcast(bf16[168,128]{1,0:T(8,128)(2,1)S(1)} %reduce_sum.25), dimensions={1,2} | broadcast | bytes 1419264 | tf_op jit(solution)/shard_map/broadcast_in_dim | solution.py:669
  68.4 4.8 %all-to-all-start.2 = ((bf16[32,168,128]{2,1,0:T(8,128)(2,1)}), bf16[32,168,128]{2,1,0:T(8,128)(2,1)S(1)}, u32[]{:S(2)}, u32[]{:S(2)}) async-start(bf16[32,168,128]{2,1,0:T(8,128)(2,1)} %broadcast_in_dim.7), calls=%async_computation.2 | async-start | bytes 2752512 | tf_op jit(solution)/shard_map/all_to_all | solution.py:670
  73.2 0.6 shard_map.151
  73.8 0.0 copy-start
  73.8 0.6 copy-done
  74.4 0.0 copy-start.1
  74.4 6.1 %collective-permute-start.5 = (bf16[192,128]{1,0:T(8,128)(2,1)S(1)}, bf16[192,128]{1,0:T(8,128)(2,1)S(1)}, u32[]{:S(2)}, u32[]{:S(2)}) collective-permute-start(bf16[192,128]{1,0:T(8,128)(2,1)S(1)} %get-tuple-element.105), channel_id=1, source_target_pairs={{0,1},{1,2},{2,3},{3,4},{4,5},{5,6},{6,7},{7,8},{8,9},{9,10},{10,1... | collective-permute-start | bytes 147464 | tf_op jit(solution)/shard_map/ppermute | solution.py:28
  80.5 3.2 %collective-permute-done.5.row_late = bf16[192,128]{1,0:T(8,128)(2,1)S(1)} collective-permute-done((bf16[192,128]{1,0:T(8,128)(2,1)S(1)}, bf16[192,128]{1,0:T(8,128)(2,1)S(1)}, u32[]{:S(2)}, u32[]{:S(2)}) %collective-permute-start.5) | collective-permute-done | bytes 49184 | tf_op jit(solution)/shard_map/ppermute | solution.py:28
  83.7 5.9 %all-to-all-done.2 = bf16[32,168,128]{2,1,0:T(8,128)(2,1)S(1)} async-done(((bf16[32,168,128]{2,1,0:T(8,128)(2,1)}), bf16[32,168,128]{2,1,0:T(8,128)(2,1)S(1)}, u32[]{:S(2)}, u32[]{:S(2)}) %all-to-all-start.2) | async-done | bytes 1376288 | tf_op jit(solution)/shard_map/all_to_all | solution.py:670
  89.7 4.9 %collective-permute-start.6 = (bf16[2880,128]{1,0:T(8,128)(2,1)S(1)}, bf16[2880,128]{1,0:T(8,128)(2,1)S(1)}, u32[]{:S(2)}, u32[]{:S(2)}) collective-permute-start(bf16[2880,128]{1,0:T(8,128)(2,1)S(1)} %slice.4), channel_id=1, source_target_pairs={{0,1},{1,0},{2,3},{3,2},{4,5},{5,4},{6,7},{7,6},{8,9},{9,8},{10,11... | collective-permute-start | bytes 2211848 | tf_op jit(solution)/shard_map/ppermute | solution.py:32
  94.6 0.0 copy-done.1
  94.6 1.7 %shard_map.152 = (f32[3,192,384]{2,1,0:T(8,128)}, f32[192,384]{1,0:T(8,128)}, f32[1536,384]{1,0:T(8,128)}, bf16[192,512]{1,0:T(8,128)(2,1)}, bf16[128,384]{1,0:T(8,128)(2,1)}) custom-call(s32[1]{0:T(128)} %bitcast.core_ref, bf16[5376,128]{1,0:T(8,128)(2,1)S(1)} %bitcast.14, f32[192,128]{1,0:T(8,128)S(1)} %copy-done.1, ...), custom_call_target="tpu_custom_call" | custom-call | flops 3000000000 | bytes 3000000 | tf_op jit(solution)/shard_map/pallas_call | solution.py:644
  96.3 0.1 collective-permute-done.6.other
  96.4 1.3 %shard_map.153 = (f32[1536,384]{1,0:T(8,128)}, f32[192,576]{1,0:T(8,128)}, f32[192,192]{1,0:T(8,128)}) custom-call(s32[1]{0:T(128)} %bitcast.core_ref, f32[1536,384]{1,0:T(8,128)} %get-tuple-element.113.pool_in, bf16[5376,128]{1,0:T(8,128)(2,1)S(1)} %bitcast.15, bf16[2880,128]{1,0:T(8,128)(2,1)S(1)} %collective-permute-done.6.other), custom_call_target="tpu_custom_call", output_to_operand_aliasing={{0}: (1, {})} | custom-call | flops 2000000000 | bytes 2000000 | tf_op jit(solution)/shard_map/pallas_call | solution.py:644
  (3 shorter events, 0.1 us)
Async XLA Ops:
  0.7 6.4 %copy-start.3 = (bf16[192,384]{1,0:T(8,128)(2,1)S(1)}, bf16[192,384]{1,0:T(8,128)(2,1)}, u32[]{:S(2)}) copy-start(bf16[192,384]{1,0:T(8,128)(2,1)} %refs_2_.3) | copy-start | bytes 442372
  0.7 6.5 %copy-start.2 = (bf16[3,384,192]{1,2,0:T(8,128)(2,1)S(1)}, bf16[3,384,192]{1,2,0:T(8,128)(2,1)}, u32[]{:S(2)}) copy-start(bf16[3,384,192]{1,2,0:T(8,128)(2,1)} %param.13) | copy-start | bytes 1327108
  1.9 9.8 %collective-permute-start = (bf16[208,128]{1,0:T(8,128)(2,1)S(1)}, bf16[208,128]{1,0:T(8,128)(2,1)S(1)}, u32[]{:S(2)}, u32[]{:S(2)}) collective-permute-start(bf16[208,128]{1,0:T(8,128)(2,1)S(1)} %get-tuple-element.64), channel_id=1, source_target_pairs={{1,0},{2,1},{3,2},{4,3},{5,4},{6,5},{7,6},{8,7},{9,8},{10,9},{11,1... | collective-permute-start | bytes 159752 | tf_op jit(solution)/shard_map/ppermute | solution.py:28
  7.1 3.6 %collective-permute-start.1 = (bf16[192,384]{1,0:T(8,128)(2,1)S(1)}, bf16[192,384]{1,0:T(8,128)(2,1)S(1)}, u32[]{:S(2)}, u32[]{:S(2)}) collective-permute-start(bf16[192,384]{1,0:T(8,128)(2,1)S(1)} %copy-done.3), channel_id=1, source_target_pairs={{0,1},{1,0},{2,3},{3,2},{4,5},{5,4},{6,7},{7,6},{8,9},{9,8},{10,11... | collective-permute-start | bytes 442376 | tf_op jit(solution)/shard_map/ppermute | solution.py:32
  7.2 4.5 %collective-permute-start.2 = (bf16[576,384]{1,0:T(8,128)(2,1)S(1)}, bf16[576,384]{1,0:T(8,128)(2,1)S(1)}, u32[]{:S(2)}, u32[]{:S(2)}) collective-permute-start(bf16[576,384]{1,0:T(8,128)(2,1)S(1)} %bitcast.17), channel_id=1, source_target_pairs={{0,1},{1,0},{2,3},{3,2},{4,5},{5,4},{6,7},{7,6},{8,9},{9,8},{10,11... | collective-permute-start | bytes 1327112 | tf_op jit(solution)/shard_map/ppermute | solution.py:32
  17.6 5.7 %collective-permute-start.3 = (bf16[4608,128]{1,0:T(8,128)(2,1)S(1)}, bf16[4608,128]{1,0:T(8,128)(2,1)S(1)}, u32[]{:S(2)}, u32[]{:S(2)}) collective-permute-start(bf16[4608,128]{1,0:T(8,128)(2,1)S(1)} %get-tuple-element.86), channel_id=1, source_target_pairs={{0,1},{1,0},{2,3},{3,2},{4,5},{5,4},{6,7},{7,6},{8,9},{9,8},{10,11... | collective-permute-start | bytes 3538952 | tf_op jit(solution)/shard_map/ppermute | solution.py:32
  21.6 1.7 %collective-permute-start.4 = (bf16[576,128]{1,0:T(8,128)(2,1)S(1)}, bf16[576,128]{1,0:T(8,128)(2,1)S(1)}, u32[]{:S(2)}, u32[]{:S(2)}) collective-permute-start(bf16[576,128]{1,0:T(8,128)(2,1)S(1)} %get-tuple-element.98), channel_id=1, source_target_pairs={{0,1},{1,0},{2,3},{3,2},{4,5},{5,4},{6,7},{7,6},{8,9},{9,8},{10,11... | collective-permute-start | bytes 442376 | tf_op jit(solution)/shard_map/ppermute | solution.py:32
  68.4 21.2 %all-to-all-start.2 = ((bf16[32,168,128]{2,1,0:T(8,128)(2,1)}), bf16[32,168,128]{2,1,0:T(8,128)(2,1)S(1)}, u32[]{:S(2)}, u32[]{:S(2)}) async-start(bf16[32,168,128]{2,1,0:T(8,128)(2,1)} %broadcast_in_dim.7), calls=%async_computation.2 | async-start | bytes 2752512 | tf_op jit(solution)/shard_map/all_to_all | solution.py:670
  73.8 0.6 copy-start
  74.4 20.2 %copy-start.1 = (f32[192,128]{1,0:T(8,128)S(1)}, f32[192,128]{1,0:T(8,128)}, u32[]{:S(2)}) copy-start(f32[192,128]{1,0:T(8,128)} %copy-done) | copy-start | bytes 294916
  74.4 9.3 %collective-permute-start.5 = (bf16[192,128]{1,0:T(8,128)(2,1)S(1)}, bf16[192,128]{1,0:T(8,128)(2,1)S(1)}, u32[]{:S(2)}, u32[]{:S(2)}) collective-permute-start(bf16[192,128]{1,0:T(8,128)(2,1)S(1)} %get-tuple-element.105), channel_id=1, source_target_pairs={{0,1},{1,2},{2,3},{3,4},{4,5},{5,6},{6,7},{7,8},{8,9},{9,10},{10,1... | collective-permute-start | bytes 147464 | tf_op jit(solution)/shard_map/ppermute | solution.py:28
  89.7 6.8 %collective-permute-start.6 = (bf16[2880,128]{1,0:T(8,128)(2,1)S(1)}, bf16[2880,128]{1,0:T(8,128)(2,1)S(1)}, u32[]{:S(2)}, u32[]{:S(2)}) collective-permute-start(bf16[2880,128]{1,0:T(8,128)(2,1)S(1)} %slice.4), channel_id=1, source_target_pairs={{0,1},{1,0},{2,3},{3,2},{4,5},{5,4},{6,7},{7,6},{8,9},{9,8},{10,11... | collective-permute-start | bytes 2211848 | tf_op jit(solution)/shard_map/ppermute | solution.py:32

commit v10 on v9

--- a/solution.py
+++ b/solution.py
@@ -193,6 +193,23 @@
             store,
         )
     hidden[...] = bround(rows_float + tn(out_weight[...], mixed[...]))
+
+
+def sum_and_spread(parts, spread_out, staged, arrived):
+    total = jnp.zeros(parts.shape[1:], jnp.float32)
+    for i in range(parts.shape[0]):
+        total += parts[i].astype(jnp.float32)
+    step = staged.shape[0]
+    for i in range(step):
+        staged[i] = bround(total)
+    copies = [
+        pltpu.make_async_copy(staged, spread_out.at[pl.ds(i * step, step)], arrived.at[i])
+        for i in range(spread_out.shape[0] // step)
+    ]
+    for copy in copies:
+        copy.start()
+    for copy in copies:
+        copy.wait()
 
 
 def bring(first_parent, *refs):
@@ -664,9 +681,19 @@
 def sum_over_chips(parts, rows_after):
     slab = float_sum(lax.all_to_all(parts, NEAR, 0, 0, tiled=True))
     copies = jnp.broadcast_to(slab, (lax.axis_size("zh"),) + slab.shape)
-    slab = float_sum(lax.all_to_all(copies, "zh", 0, 0, tiled=True))
-    slab, *row_parts = rows_after(slab)
-    copies = jnp.broadcast_to(slab, parts.shape)
+    slabs = lax.all_to_all(copies, "zh", 0, 0, tiled=True)
+    slabs, *row_parts = rows_after(slabs)
+    step = parts.shape[0] // 4
+    (copies,) = call(
+        sum_and_spread,
+        [(parts.shape, parts.dtype)],
+        [(step,) + slab.shape],
+        slabs,
+        scalars=0,
+        copies=4,
+        to_hbm=True,
+        micros=0.5,
+    )
     total = lax.all_to_all(copies, NEAR, 0, 0, tiled=True)
     return lax.optimization_barrier((total, *row_parts))
 

time: 98.3 us -> 98.2 us (level)
  local copies, waits for them, and re-layouts: 1.98 us -> 0.72 us
  Pallas kernels: 18.8 us -> 20 us
    broadcast_in_dim x1 -> x0, local copies, waits for them, and re-layouts: 1.26 us -> none  [sum_over_chips(): copies = jnp.broadcast_to(slab, parts.shape)]
    pallas_call x10 -> x11, Pallas kernels: 18.8 us -> 20 us  [call(): pl.pallas_call(kernel, out_shape=[jax.ShapeDtypeStruct(shape, dtype) for...]
where the time goes in v10:
time: 98.2 us; the launch traced here: 97.8 us
  blocking collectives  43.3 us (44%)
  starting transfers between devices  22.4 us (23%)
  Pallas kernels  20 us (20%)
  waiting for transfers between devices  10.2 us (10%)
  between operations  0.99 us (1%)
    all_to_all x1, blocking collectives, sum_over_chips(): slab = float_sum(lax.all_to_all(parts, NEAR, 0, 0, tiled=True))  28.4 us
    pallas_call x11, Pallas kernels, call(): pl.pallas_call(kernel, out_shape=[jax.ShapeDtypeStruct(shape, dtype) for...  20 us
    all_to_all x1, blocking collectives, sum_over_chips(): slabs = lax.all_to_all(copies, 'zh', 0, 0, tiled=True)  14.9 us
    ppermute x2, starting transfers between devices, passed_along(): return lax.ppermute(shard, AXES, pairs)  11.3 us
    ppermute x5, starting transfers between devices, swap_cores(): return lax.ppermute(shard, 'sub', [(0, 1), (1, 0)])  6.37 us
    all_to_all x1, waiting for transfers between devices, sum_over_chips(): total = lax.all_to_all(copies, NEAR, 0, 0, tiled=True)  5.91 us
    all_to_all x1, starting transfers between devices, sum_over_chips(): total = lax.all_to_all(copies, NEAR, 0, 0, tiled=True)  4.78 us
    ppermute x2, waiting for transfers between devices, passed_along(): return lax.ppermute(shard, AXES, pairs)  3.16 us
  transfers between devices with their start and end apart: 8, of which 4 were waited for; matrix products, arithmetic and copies ran while one was open for 0% of the time, Pallas kernels for 10%

profile of v10, /device:TPU:1, one launch (start us, length us, event | category | flops | bytes accessed | tf_op | source)
XLA Modules:
  0.0 97.8 jit_solution(5632755935826681372)
XLA Ops:
  0.7 0.0 copy-start.3
  0.7 0.0 copy-start.2
  0.7 1.2 %shard_map.144 = (bf16[192,512]{1,0:T(8,128)(2,1)S(1)}, bf16[192,576]{1,0:T(8,128)(2,1)S(1)}, bf16[192,192]{1,0:T(8,128)(2,1)S(1)}, s32[1,512]{1,0:T(1,128)S(1)}...) custom-call(s32[1]{0:T(128)} %bitcast.1.first_parent, bf16[192,512]{1,0:T(8,128)(2,1)} %bitcast.18, ...), custom_call_target="tpu_custom_call" | custom-call | flops 1000000000 | bytes 1000000 | tf_op jit(solution)/shard_map/pallas_call | solution.py:661
  1.9 5.1 %collective-permute-start = (bf16[208,128]{1,0:T(8,128)(2,1)S(1)}, bf16[208,128]{1,0:T(8,128)(2,1)S(1)}, u32[]{:S(2)}, u32[]{:S(2)}) collective-permute-start(bf16[208,128]{1,0:T(8,128)(2,1)S(1)} %get-tuple-element.64), channel_id=1, source_target_pairs={{1,0},{2,1},{3,2},{4,3},{5,4},{6,5},{7,6},{8,7},{9,8},{10,9},{11,1... | collective-permute-start | bytes 159752 | tf_op jit(solution)/shard_map/ppermute | solution.py:28
  7.0 0.0 copy-done.3
  7.1 0.1 collective-permute-start.1
  7.2 0.0 copy-done.2
  7.2 0.5 collective-permute-start.2
  7.7 3.0 %shard_map.145 = (bf16[1536,384]{1,0:T(8,128)(2,1)S(1)}, bf16[576,384]{1,0:T(8,128)(2,1)S(1)}, bf16[192,384]{1,0:T(8,128)(2,1)S(1)}, bf16[128,384]{1,0:T(8,128)(...) custom-call(bf16[1536,384]{1,0:T(8,128)(2,1)} %refs_0_.1, ...), custom_call_target="tpu_custom_call" | custom-call | flops 4000000000 | bytes 4000000 | tf_op jit(solution)/shard_map/pallas_call | solution.py:661
  10.7 0.0 collective-permute-done.1.other_out
  10.7 1.0 shard_map.146
  11.7 0.0 collective-permute-done.packed
  11.7 0.0 collective-permute-done.2.other_qkv
  11.7 5.0 %shard_map.147 = (bf16[128,384]{1,0:T(8,128)(2,1)S(1)}, bf16[16,192]{1,0:T(8,128)(2,1)S(1)}, bf16[192,128]{1,0:T(8,128)(2,1)S(1)}, bf16[128,384]{1,0:T(8,128)(2,...) custom-call(bf16[208,128]{1,0:T(8,128)(2,1)S(1)} %collective-permute, ...), custom_call_target="tpu_custom_call" | custom-call | flops 8000000000 | bytes 8000000 | tf_op jit(solution)/shard_map/pallas_call | solution.py:661
  16.7 0.9 shard_map.148
  17.6 0.2 collective-permute-start.3
  17.8 3.8 %shard_map.149 = (bf16[192,640]{1,0:T(8,128)(2,1)S(1)}, bf16[576,640]{1,0:T(8,128)(2,1)S(1)}, bf16[576,128]{1,0:T(8,128)(2,1)S(1)}, bf16[576,128]{1,0:T(8,128)(2,1)S(1)}) custom-call(s32[1]{0:T(128)} %bitcast.core_ref, s32[1]{0:T(128)} %bitcast.1.first_parent, bf16[192,512]{1,0:T(8,128)(2,1)S(1)} %get-tuple-element.67.refs_4_.rows, ...), custom_call_target="tpu_custom_call" | custom-call | flops 6000000000 | bytes 6000000 | tf_op jit(solution)/shard_map/pallas_call | solution.py:661
  21.6 0.7 collective-permute-start.4
  22.3 1.0 %collective-permute-done.4.fine_got = bf16[576,128]{1,0:T(8,128)(2,1)S(1)} collective-permute-done((bf16[576,128]{1,0:T(8,128)(2,1)S(1)}, bf16[576,128]{1,0:T(8,128)(2,1)S(1)}, u32[]{:S(2)}, u32[]{:S(2)}) %collective-permute-start.4) | collective-permute-done | bytes 147488 | tf_op jit(solution)/shard_map/ppermute | solution.py:32
  23.3 0.0 collective-permute-done.3.got
  23.3 0.3 shard_map.150
  23.6 28.4 %all_to_all.15 = bf16[32,168,128]{2,1,0:T(8,128)(2,1)S(1)} all-to-all(bf16[32,168,128]{2,1,0:T(8,128)(2,1)S(1)} %bitcast.12), channel_id=1, replica_groups=mesh['zh'=4,'zl'=2,'y'=4,'x'=4,'sub'=2] {'zl','y','x'}, dimensions={0} | all-to-all | bytes 2752512 | tf_op jit(solution)/shard_map/all_to_all | solution.py:682
  52.0 0.2 reduce_sum.12
  52.2 14.9 %all_to_all.16.parts = bf16[4,168,128]{2,1,0:T(8,128)(2,1)S(1)} all-to-all(bf16[4,168,128]{2,1,0:T(8,128)(2,1)S(1)} %broadcast_in_dim.3), channel_id=1, replica_groups=mesh['zh'=4,'zl'=2,'y'=4,'x'=4,'sub'=2] {'zh'}, dimensions={0} | all-to-all | bytes 344064 | tf_op jit(solution)/shard_map/all_to_all | solution.py:684
  67.1 1.1 %shard_map.151 = bf16[32,168,128]{2,1,0:T(8,128)(2,1)} custom-call(bf16[4,168,128]{2,1,0:T(8,128)(2,1)S(1)} %all_to_all.16.parts), custom_call_target="tpu_custom_call" | custom-call | flops 500000000 | bytes 500000 | tf_op jit(solution)/shard_map/pallas_call | solution.py:661
  68.3 4.8 %all-to-all-start.2 = ((bf16[32,168,128]{2,1,0:T(8,128)(2,1)}), bf16[32,168,128]{2,1,0:T(8,128)(2,1)S(1)}, u32[]{:S(2)}, u32[]{:S(2)}) async-start(bf16[32,168,128]{2,1,0:T(8,128)(2,1)} %shard_map.151), calls=%async_computation.2 | async-start | bytes 2752512 | tf_op jit(solution)/shard_map/all_to_all | solution.py:697
  73.1 0.6 shard_map.152
  73.6 0.0 copy-start
  73.7 0.6 copy-done
  74.3 0.0 copy-start.1
  74.3 6.1 %collective-permute-start.5 = (bf16[192,128]{1,0:T(8,128)(2,1)S(1)}, bf16[192,128]{1,0:T(8,128)(2,1)S(1)}, u32[]{:S(2)}, u32[]{:S(2)}) collective-permute-start(bf16[192,128]{1,0:T(8,128)(2,1)S(1)} %get-tuple-element.105), channel_id=1, source_target_pairs={{0,1},{1,2},{2,3},{3,4},{4,5},{5,6},{6,7},{7,8},{8,9},{9,10},{10,1... | collective-permute-start | bytes 147464 | tf_op jit(solution)/shard_map/ppermute | solution.py:28
  80.4 3.2 %collective-permute-done.5.row_late = bf16[192,128]{1,0:T(8,128)(2,1)S(1)} collective-permute-done((bf16[192,128]{1,0:T(8,128)(2,1)S(1)}, bf16[192,128]{1,0:T(8,128)(2,1)S(1)}, u32[]{:S(2)}, u32[]{:S(2)}) %collective-permute-start.5) | collective-permute-done | bytes 49184 | tf_op jit(solution)/shard_map/ppermute | solution.py:28
  83.6 5.9 %all-to-all-done.2 = bf16[32,168,128]{2,1,0:T(8,128)(2,1)S(1)} async-done(((bf16[32,168,128]{2,1,0:T(8,128)(2,1)}), bf16[32,168,128]{2,1,0:T(8,128)(2,1)S(1)}, u32[]{:S(2)}, u32[]{:S(2)}) %all-to-all-start.2) | async-done | bytes 1376288 | tf_op jit(solution)/shard_map/all_to_all | solution.py:697
  89.5 4.9 %collective-permute-start.6 = (bf16[2880,128]{1,0:T(8,128)(2,1)S(1)}, bf16[2880,128]{1,0:T(8,128)(2,1)S(1)}, u32[]{:S(2)}, u32[]{:S(2)}) collective-permute-start(bf16[2880,128]{1,0:T(8,128)(2,1)S(1)} %slice.4), channel_id=1, source_target_pairs={{0,1},{1,0},{2,3},{3,2},{4,5},{5,4},{6,7},{7,6},{8,9},{9,8},{10,11... | collective-permute-start | bytes 2211848 | tf_op jit(solution)/shard_map/ppermute | solution.py:32
  94.5 0.0 copy-done.1
  94.5 1.7 %shard_map.153 = (f32[3,192,384]{2,1,0:T(8,128)}, f32[192,384]{1,0:T(8,128)}, f32[1536,384]{1,0:T(8,128)}, bf16[192,512]{1,0:T(8,128)(2,1)}, bf16[128,384]{1,0:T(8,128)(2,1)}) custom-call(s32[1]{0:T(128)} %bitcast.core_ref, bf16[5376,128]{1,0:T(8,128)(2,1)S(1)} %bitcast.14, f32[192,128]{1,0:T(8,128)S(1)} %copy-done.1, ...), custom_call_target="tpu_custom_call" | custom-call | flops 3000000000 | bytes 3000000 | tf_op jit(solution)/shard_map/pallas_call | solution.py:661
  96.2 0.1 collective-permute-done.6.other
  96.3 1.3 %shard_map.154 = (f32[1536,384]{1,0:T(8,128)}, f32[192,576]{1,0:T(8,128)}, f32[192,192]{1,0:T(8,128)}) custom-call(s32[1]{0:T(128)} %bitcast.core_ref, f32[1536,384]{1,0:T(8,128)} %get-tuple-element.113.pool_in, bf16[5376,128]{1,0:T(8,128)(2,1)S(1)} %bitcast.15, bf16[2880,128]{1,0:T(8,128)(2,1)S(1)} %collective-permute-done.6.other), custom_call_target="tpu_custom_call", output_to_operand_aliasing={{0}: (1, {})} | custom-call | flops 2000000000 | bytes 2000000 | tf_op jit(solution)/shard_map/pallas_call | solution.py:661
  (2 shorter events, 0.1 us)
Async XLA Ops:
  0.7 6.4 %copy-start.3 = (bf16[192,384]{1,0:T(8,128)(2,1)S(1)}, bf16[192,384]{1,0:T(8,128)(2,1)}, u32[]{:S(2)}) copy-start(bf16[192,384]{1,0:T(8,128)(2,1)} %refs_2_.3) | copy-start | bytes 442372
  0.7 6.5 %copy-start.2 = (bf16[3,384,192]{1,2,0:T(8,128)(2,1)S(1)}, bf16[3,384,192]{1,2,0:T(8,128)(2,1)}, u32[]{:S(2)}) copy-start(bf16[3,384,192]{1,2,0:T(8,128)(2,1)} %param.13) | copy-start | bytes 1327108
  1.9 9.8 %collective-permute-start = (bf16[208,128]{1,0:T(8,128)(2,1)S(1)}, bf16[208,128]{1,0:T(8,128)(2,1)S(1)}, u32[]{:S(2)}, u32[]{:S(2)}) collective-permute-start(bf16[208,128]{1,0:T(8,128)(2,1)S(1)} %get-tuple-element.64), channel_id=1, source_target_pairs={{1,0},{2,1},{3,2},{4,3},{5,4},{6,5},{7,6},{8,7},{9,8},{10,9},{11,1... | collective-permute-start | bytes 159752 | tf_op jit(solution)/shard_map/ppermute | solution.py:28
  7.1 3.6 %collective-permute-start.1 = (bf16[192,384]{1,0:T(8,128)(2,1)S(1)}, bf16[192,384]{1,0:T(8,128)(2,1)S(1)}, u32[]{:S(2)}, u32[]{:S(2)}) collective-permute-start(bf16[192,384]{1,0:T(8,128)(2,1)S(1)} %copy-done.3), channel_id=1, source_target_pairs={{0,1},{1,0},{2,3},{3,2},{4,5},{5,4},{6,7},{7,6},{8,9},{9,8},{10,11... | collective-permute-start | bytes 442376 | tf_op jit(solution)/shard_map/ppermute | solution.py:32
  7.2 4.5 %collective-permute-start.2 = (bf16[576,384]{1,0:T(8,128)(2,1)S(1)}, bf16[576,384]{1,0:T(8,128)(2,1)S(1)}, u32[]{:S(2)}, u32[]{:S(2)}) collective-permute-start(bf16[576,384]{1,0:T(8,128)(2,1)S(1)} %bitcast.17), channel_id=1, source_target_pairs={{0,1},{1,0},{2,3},{3,2},{4,5},{5,4},{6,7},{7,6},{8,9},{9,8},{10,11... | collective-permute-start | bytes 1327112 | tf_op jit(solution)/shard_map/ppermute | solution.py:32
  17.6 5.7 %collective-permute-start.3 = (bf16[4608,128]{1,0:T(8,128)(2,1)S(1)}, bf16[4608,128]{1,0:T(8,128)(2,1)S(1)}, u32[]{:S(2)}, u32[]{:S(2)}) collective-permute-start(bf16[4608,128]{1,0:T(8,128)(2,1)S(1)} %get-tuple-element.86), channel_id=1, source_target_pairs={{0,1},{1,0},{2,3},{3,2},{4,5},{5,4},{6,7},{7,6},{8,9},{9,8},{10,11... | collective-permute-start | bytes 3538952 | tf_op jit(solution)/shard_map/ppermute | solution.py:32
  21.6 1.7 %collective-permute-start.4 = (bf16[576,128]{1,0:T(8,128)(2,1)S(1)}, bf16[576,128]{1,0:T(8,128)(2,1)S(1)}, u32[]{:S(2)}, u32[]{:S(2)}) collective-permute-start(bf16[576,128]{1,0:T(8,128)(2,1)S(1)} %get-tuple-element.98), channel_id=1, source_target_pairs={{0,1},{1,0},{2,3},{3,2},{4,5},{5,4},{6,7},{7,6},{8,9},{9,8},{10,11... | collective-permute-start | bytes 442376 | tf_op jit(solution)/shard_map/ppermute | solution.py:32
  68.3 21.2 %all-to-all-start.2 = ((bf16[32,168,128]{2,1,0:T(8,128)(2,1)}), bf16[32,168,128]{2,1,0:T(8,128)(2,1)S(1)}, u32[]{:S(2)}, u32[]{:S(2)}) async-start(bf16[32,168,128]{2,1,0:T(8,128)(2,1)} %shard_map.151), calls=%async_computation.2 | async-start | bytes 2752512 | tf_op jit(solution)/shard_map/all_to_all | solution.py:697
  73.6 0.6 copy-start
  74.3 20.2 %copy-start.1 = (f32[192,128]{1,0:T(8,128)S(1)}, f32[192,128]{1,0:T(8,128)}, u32[]{:S(2)}) copy-start(f32[192,128]{1,0:T(8,128)} %copy-done) | copy-start | bytes 294916
  74.3 9.3 %collective-permute-start.5 = (bf16[192,128]{1,0:T(8,128)(2,1)S(1)}, bf16[192,128]{1,0:T(8,128)(2,1)S(1)}, u32[]{:S(2)}, u32[]{:S(2)}) collective-permute-start(bf16[192,128]{1,0:T(8,128)(2,1)S(1)} %get-tuple-element.105), channel_id=1, source_target_pairs={{0,1},{1,2},{2,3},{3,4},{4,5},{5,6},{6,7},{7,8},{8,9},{9,10},{10,1... | collective-permute-start | bytes 147464 | tf_op jit(solution)/shard_map/ppermute | solution.py:28
  89.5 6.8 %collective-permute-start.6 = (bf16[2880,128]{1,0:T(8,128)(2,1)S(1)}, bf16[2880,128]{1,0:T(8,128)(2,1)S(1)}, u32[]{:S(2)}, u32[]{:S(2)}) collective-permute-start(bf16[2880,128]{1,0:T(8,128)(2,1)S(1)} %slice.4), channel_id=1, source_target_pairs={{0,1},{1,0},{2,3},{3,2},{4,5},{5,4},{6,7},{7,6},{8,9},{9,8},{10,11... | collective-permute-start | bytes 2211848 | tf_op jit(solution)/shard_map/ppermute | solution.py:32

commit v11 on v10

--- a/solution.py
+++ b/solution.py
@@ -116,15 +116,16 @@
     return bround(jnp.concatenate(mixed, 0))
 
 
-def attend_back(query, key, upstream, parts, grad_probs):
-    scores, scales = [], []
-    for i, (exponent, inverse) in enumerate(parts):
+def attend_back(query, key, upstream, mixed, parts, grad_probs):
+    scales = [jnp.broadcast_to(inverse, (HD, LANES)) for _, inverse in parts]
+    upward = upstream.astype(jnp.float32) * jnp.concatenate(scales, 0)
+    overlap = upward * mixed.astype(jnp.float32) * HD**-0.5
+    scores = []
+    for i, (exponent, _) in enumerate(parts):
         grad_prob = grad_probs[:, i * LANES : (i + 1) * LANES]
-        weighted = exponent.astype(jnp.float32)
-        mean = inverse * jnp.sum(weighted * grad_prob, 0, keepdims=True)
-        scores.append(bround(weighted * (grad_prob - mean)))
-        scales.append(jnp.broadcast_to(inverse, (HD, LANES)))
-    spread_up = bround(upstream.astype(jnp.float32) * jnp.concatenate(scales, 0))
+        mean = jnp.sum(overlap[i * HD : (i + 1) * HD], 0, keepdims=True)
+        scores.append(bround(exponent.astype(jnp.float32) * (grad_prob - mean)))
+    spread_up = bround(upward)
     grad_value = nt(spread_up, jnp.concatenate([exponent for exponent, _ in parts], 0))
     grad_query = nn(key, jnp.concatenate(scores, 1))
     grad_key = nt(query, jnp.concatenate(scores, 0))
@@ -368,6 +369,7 @@
                 qkvs[half][at[0]],
                 qkvs[half][at[1]],
                 upward[half, at[0]],
+                mixed[half, at[0]],
                 parts[half, head],
                 grad_probs[half][:, head * LANES : (head + 2) * LANES],
             )
@@ -486,6 +488,7 @@
                 qkv[at[0], inner],
                 qkv[at[1], inner],
                 upward[at[0], lanes],
+                mixed[at[0], lanes],
                 parts,
                 grad_probs[:, head * LANES : (head + 2) * LANES],
             )

time: 98.2 us -> 97.8 us (level)
  no operation moved by 1% of the time
where the time goes in v11:
time: 97.8 us; the launch traced here: 97.5 us
  blocking collectives  43.3 us (44%)
  starting transfers between devices  22.4 us (23%)
  Pallas kernels  19.6 us (20%)
  waiting for transfers between devices  10.2 us (10%)
  between operations  0.99 us (1%)
    all_to_all x1, blocking collectives, sum_over_chips(): slab = float_sum(lax.all_to_all(parts, NEAR, 0, 0, tiled=True))  28.4 us
    pallas_call x11, Pallas kernels, call(): pl.pallas_call(kernel, out_shape=[jax.ShapeDtypeStruct(shape, dtype) for...  19.6 us
    all_to_all x1, blocking collectives, sum_over_chips(): slabs = lax.all_to_all(copies, 'zh', 0, 0, tiled=True)  14.9 us
    ppermute x2, starting transfers between devices, passed_along(): return lax.ppermute(shard, AXES, pairs)  11.3 us
    ppermute x5, starting transfers between devices, swap_cores(): return lax.ppermute(shard, 'sub', [(0, 1), (1, 0)])  6.39 us
    all_to_all x1, waiting for transfers between devices, sum_over_chips(): total = lax.all_to_all(copies, NEAR, 0, 0, tiled=True)  5.91 us
    all_to_all x1, starting transfers between devices, sum_over_chips(): total = lax.all_to_all(copies, NEAR, 0, 0, tiled=True)  4.78 us
    ppermute x2, waiting for transfers between devices, passed_along(): return lax.ppermute(shard, AXES, pairs)  3.16 us
  transfers between devices with their start and end apart: 8, of which 4 were waited for; matrix products, arithmetic and copies ran while one was open for 0% of the time, Pallas kernels for 10%

profile of v11, /device:TPU:1, one launch (start us, length us, event | category | flops | bytes accessed | tf_op | source)
XLA Modules:
  0.0 97.5 jit_solution(17895769215334588230)
XLA Ops:
  0.7 0.0 copy-start.3
  0.7 0.0 copy-start.2
  0.7 1.2 %shard_map.144 = (bf16[192,512]{1,0:T(8,128)(2,1)S(1)}, bf16[192,576]{1,0:T(8,128)(2,1)S(1)}, bf16[192,192]{1,0:T(8,128)(2,1)S(1)}, s32[1,512]{1,0:T(1,128)S(1)}...) custom-call(s32[1]{0:T(128)} %bitcast.1.first_parent, bf16[192,512]{1,0:T(8,128)(2,1)} %bitcast.18, ...), custom_call_target="tpu_custom_call" | custom-call | flops 1000000000 | bytes 1000000 | tf_op jit(solution)/shard_map/pallas_call | solution.py:664
  1.9 5.1 %collective-permute-start = (bf16[208,128]{1,0:T(8,128)(2,1)S(1)}, bf16[208,128]{1,0:T(8,128)(2,1)S(1)}, u32[]{:S(2)}, u32[]{:S(2)}) collective-permute-start(bf16[208,128]{1,0:T(8,128)(2,1)S(1)} %get-tuple-element.64), channel_id=1, source_target_pairs={{1,0},{2,1},{3,2},{4,3},{5,4},{6,5},{7,6},{8,7},{9,8},{10,9},{11,1... | collective-permute-start | bytes 159752 | tf_op jit(solution)/shard_map/ppermute | solution.py:28
  7.0 0.0 copy-done.3
  7.1 0.1 collective-permute-start.1
  7.2 0.0 copy-done.2
  7.2 0.5 collective-permute-start.2
  7.7 3.0 %shard_map.145 = (bf16[1536,384]{1,0:T(8,128)(2,1)S(1)}, bf16[576,384]{1,0:T(8,128)(2,1)S(1)}, bf16[192,384]{1,0:T(8,128)(2,1)S(1)}, bf16[128,384]{1,0:T(8,128)(...) custom-call(bf16[1536,384]{1,0:T(8,128)(2,1)} %refs_0_.1, ...), custom_call_target="tpu_custom_call" | custom-call | flops 4000000000 | bytes 4000000 | tf_op jit(solution)/shard_map/pallas_call | solution.py:664
  10.7 0.0 collective-permute-done.1.other_out
  10.7 1.0 shard_map.146
  11.7 0.0 collective-permute-done.packed
  11.7 0.0 collective-permute-done.2.other_qkv
  11.7 4.9 %shard_map.147 = (bf16[128,384]{1,0:T(8,128)(2,1)S(1)}, bf16[16,192]{1,0:T(8,128)(2,1)S(1)}, bf16[192,128]{1,0:T(8,128)(2,1)S(1)}, bf16[128,384]{1,0:T(8,128)(2,...) custom-call(bf16[208,128]{1,0:T(8,128)(2,1)S(1)} %collective-permute, ...), custom_call_target="tpu_custom_call" | custom-call | flops 8000000000 | bytes 8000000 | tf_op jit(solution)/shard_map/pallas_call | solution.py:664
  16.6 0.9 shard_map.148
  17.5 0.2 collective-permute-start.3
  17.7 3.5 %shard_map.149 = (bf16[192,640]{1,0:T(8,128)(2,1)S(1)}, bf16[576,640]{1,0:T(8,128)(2,1)S(1)}, bf16[576,128]{1,0:T(8,128)(2,1)S(1)}, bf16[576,128]{1,0:T(8,128)(2,1)S(1)}) custom-call(s32[1]{0:T(128)} %bitcast.core_ref, s32[1]{0:T(128)} %bitcast.1.first_parent, bf16[192,512]{1,0:T(8,128)(2,1)S(1)} %get-tuple-element.67.refs_4_.rows, ...), custom_call_target="tpu_custom_call" | custom-call | flops 6000000000 | bytes 6000000 | tf_op jit(solution)/shard_map/pallas_call | solution.py:664
  21.3 0.7 collective-permute-start.4
  21.9 1.0 %collective-permute-done.4.fine_got = bf16[576,128]{1,0:T(8,128)(2,1)S(1)} collective-permute-done((bf16[576,128]{1,0:T(8,128)(2,1)S(1)}, bf16[576,128]{1,0:T(8,128)(2,1)S(1)}, u32[]{:S(2)}, u32[]{:S(2)}) %collective-permute-start.4) | collective-permute-done | bytes 147488 | tf_op jit(solution)/shard_map/ppermute | solution.py:32
  22.9 0.0 collective-permute-done.3.got
  23.0 0.3 shard_map.150
  23.2 28.4 %all_to_all.15 = bf16[32,168,128]{2,1,0:T(8,128)(2,1)S(1)} all-to-all(bf16[32,168,128]{2,1,0:T(8,128)(2,1)S(1)} %bitcast.12), channel_id=1, replica_groups=mesh['zh'=4,'zl'=2,'y'=4,'x'=4,'sub'=2] {'zl','y','x'}, dimensions={0} | all-to-all | bytes 2752512 | tf_op jit(solution)/shard_map/all_to_all | solution.py:685
  51.7 0.2 reduce_sum.12
  51.9 14.9 %all_to_all.16.parts = bf16[4,168,128]{2,1,0:T(8,128)(2,1)S(1)} all-to-all(bf16[4,168,128]{2,1,0:T(8,128)(2,1)S(1)} %broadcast_in_dim.3), channel_id=1, replica_groups=mesh['zh'=4,'zl'=2,'y'=4,'x'=4,'sub'=2] {'zh'}, dimensions={0} | all-to-all | bytes 344064 | tf_op jit(solution)/shard_map/all_to_all | solution.py:687
  66.8 1.1 %shard_map.151 = bf16[32,168,128]{2,1,0:T(8,128)(2,1)} custom-call(bf16[4,168,128]{2,1,0:T(8,128)(2,1)S(1)} %all_to_all.16.parts), custom_call_target="tpu_custom_call" | custom-call | flops 500000000 | bytes 500000 | tf_op jit(solution)/shard_map/pallas_call | solution.py:664
  68.0 4.8 %all-to-all-start.2 = ((bf16[32,168,128]{2,1,0:T(8,128)(2,1)}), bf16[32,168,128]{2,1,0:T(8,128)(2,1)S(1)}, u32[]{:S(2)}, u32[]{:S(2)}) async-start(bf16[32,168,128]{2,1,0:T(8,128)(2,1)} %shard_map.151), calls=%async_computation.2 | async-start | bytes 2752512 | tf_op jit(solution)/shard_map/all_to_all | solution.py:700
  72.7 0.6 shard_map.152
  73.3 0.0 copy-start
  73.3 0.6 copy-done
  74.0 0.0 copy-start.1
  74.0 6.1 %collective-permute-start.5 = (bf16[192,128]{1,0:T(8,128)(2,1)S(1)}, bf16[192,128]{1,0:T(8,128)(2,1)S(1)}, u32[]{:S(2)}, u32[]{:S(2)}) collective-permute-start(bf16[192,128]{1,0:T(8,128)(2,1)S(1)} %get-tuple-element.105), channel_id=1, source_target_pairs={{0,1},{1,2},{2,3},{3,4},{4,5},{5,6},{6,7},{7,8},{8,9},{9,10},{10,1... | collective-permute-start | bytes 147464 | tf_op jit(solution)/shard_map/ppermute | solution.py:28
  80.1 3.2 %collective-permute-done.5.row_late = bf16[192,128]{1,0:T(8,128)(2,1)S(1)} collective-permute-done((bf16[192,128]{1,0:T(8,128)(2,1)S(1)}, bf16[192,128]{1,0:T(8,128)(2,1)S(1)}, u32[]{:S(2)}, u32[]{:S(2)}) %collective-permute-start.5) | collective-permute-done | bytes 49184 | tf_op jit(solution)/shard_map/ppermute | solution.py:28
  83.2 5.9 %all-to-all-done.2 = bf16[32,168,128]{2,1,0:T(8,128)(2,1)S(1)} async-done(((bf16[32,168,128]{2,1,0:T(8,128)(2,1)}), bf16[32,168,128]{2,1,0:T(8,128)(2,1)S(1)}, u32[]{:S(2)}, u32[]{:S(2)}) %all-to-all-start.2) | async-done | bytes 1376288 | tf_op jit(solution)/shard_map/all_to_all | solution.py:700
  89.2 4.9 %collective-permute-start.6 = (bf16[2880,128]{1,0:T(8,128)(2,1)S(1)}, bf16[2880,128]{1,0:T(8,128)(2,1)S(1)}, u32[]{:S(2)}, u32[]{:S(2)}) collective-permute-start(bf16[2880,128]{1,0:T(8,128)(2,1)S(1)} %slice.4), channel_id=1, source_target_pairs={{0,1},{1,0},{2,3},{3,2},{4,5},{5,4},{6,7},{7,6},{8,9},{9,8},{10,11... | collective-permute-start | bytes 2211848 | tf_op jit(solution)/shard_map/ppermute | solution.py:32
  94.1 0.0 copy-done.1
  94.1 1.7 %shard_map.153 = (f32[3,192,384]{2,1,0:T(8,128)}, f32[192,384]{1,0:T(8,128)}, f32[1536,384]{1,0:T(8,128)}, bf16[192,512]{1,0:T(8,128)(2,1)}, bf16[128,384]{1,0:T(8,128)(2,1)}) custom-call(s32[1]{0:T(128)} %bitcast.core_ref, bf16[5376,128]{1,0:T(8,128)(2,1)S(1)} %bitcast.14, f32[192,128]{1,0:T(8,128)S(1)} %copy-done.1, ...), custom_call_target="tpu_custom_call" | custom-call | flops 3000000000 | bytes 3000000 | tf_op jit(solution)/shard_map/pallas_call | solution.py:664
  95.9 0.1 collective-permute-done.6.other
  96.0 1.3 %shard_map.154 = (f32[1536,384]{1,0:T(8,128)}, f32[192,576]{1,0:T(8,128)}, f32[192,192]{1,0:T(8,128)}) custom-call(s32[1]{0:T(128)} %bitcast.core_ref, f32[1536,384]{1,0:T(8,128)} %get-tuple-element.113.pool_in, bf16[5376,128]{1,0:T(8,128)(2,1)S(1)} %bitcast.15, bf16[2880,128]{1,0:T(8,128)(2,1)S(1)} %collective-permute-done.6.other), custom_call_target="tpu_custom_call", output_to_operand_aliasing={{0}: (1, {})} | custom-call | flops 2000000000 | bytes 2000000 | tf_op jit(solution)/shard_map/pallas_call | solution.py:664
  (2 shorter events, 0.1 us)
Async XLA Ops:
  0.7 6.4 %copy-start.3 = (bf16[192,384]{1,0:T(8,128)(2,1)S(1)}, bf16[192,384]{1,0:T(8,128)(2,1)}, u32[]{:S(2)}) copy-start(bf16[192,384]{1,0:T(8,128)(2,1)} %refs_2_.3) | copy-start | bytes 442372
  0.7 6.5 %copy-start.2 = (bf16[3,384,192]{1,2,0:T(8,128)(2,1)S(1)}, bf16[3,384,192]{1,2,0:T(8,128)(2,1)}, u32[]{:S(2)}) copy-start(bf16[3,384,192]{1,2,0:T(8,128)(2,1)} %param.13) | copy-start | bytes 1327108
  1.9 9.8 %collective-permute-start = (bf16[208,128]{1,0:T(8,128)(2,1)S(1)}, bf16[208,128]{1,0:T(8,128)(2,1)S(1)}, u32[]{:S(2)}, u32[]{:S(2)}) collective-permute-start(bf16[208,128]{1,0:T(8,128)(2,1)S(1)} %get-tuple-element.64), channel_id=1, source_target_pairs={{1,0},{2,1},{3,2},{4,3},{5,4},{6,5},{7,6},{8,7},{9,8},{10,9},{11,1... | collective-permute-start | bytes 159752 | tf_op jit(solution)/shard_map/ppermute | solution.py:28
  7.1 3.6 %collective-permute-start.1 = (bf16[192,384]{1,0:T(8,128)(2,1)S(1)}, bf16[192,384]{1,0:T(8,128)(2,1)S(1)}, u32[]{:S(2)}, u32[]{:S(2)}) collective-permute-start(bf16[192,384]{1,0:T(8,128)(2,1)S(1)} %copy-done.3), channel_id=1, source_target_pairs={{0,1},{1,0},{2,3},{3,2},{4,5},{5,4},{6,7},{7,6},{8,9},{9,8},{10,11... | collective-permute-start | bytes 442376 | tf_op jit(solution)/shard_map/ppermute | solution.py:32
  7.2 4.5 %collective-permute-start.2 = (bf16[576,384]{1,0:T(8,128)(2,1)S(1)}, bf16[576,384]{1,0:T(8,128)(2,1)S(1)}, u32[]{:S(2)}, u32[]{:S(2)}) collective-permute-start(bf16[576,384]{1,0:T(8,128)(2,1)S(1)} %bitcast.17), channel_id=1, source_target_pairs={{0,1},{1,0},{2,3},{3,2},{4,5},{5,4},{6,7},{7,6},{8,9},{9,8},{10,11... | collective-permute-start | bytes 1327112 | tf_op jit(solution)/shard_map/ppermute | solution.py:32
  17.5 5.4 %collective-permute-start.3 = (bf16[4608,128]{1,0:T(8,128)(2,1)S(1)}, bf16[4608,128]{1,0:T(8,128)(2,1)S(1)}, u32[]{:S(2)}, u32[]{:S(2)}) collective-permute-start(bf16[4608,128]{1,0:T(8,128)(2,1)S(1)} %get-tuple-element.86), channel_id=1, source_target_pairs={{0,1},{1,0},{2,3},{3,2},{4,5},{5,4},{6,7},{7,6},{8,9},{9,8},{10,11... | collective-permute-start | bytes 3538952 | tf_op jit(solution)/shard_map/ppermute | solution.py:32
  21.3 1.7 %collective-permute-start.4 = (bf16[576,128]{1,0:T(8,128)(2,1)S(1)}, bf16[576,128]{1,0:T(8,128)(2,1)S(1)}, u32[]{:S(2)}, u32[]{:S(2)}) collective-permute-start(bf16[576,128]{1,0:T(8,128)(2,1)S(1)} %get-tuple-element.98), channel_id=1, source_target_pairs={{0,1},{1,0},{2,3},{3,2},{4,5},{5,4},{6,7},{7,6},{8,9},{9,8},{10,11... | collective-permute-start | bytes 442376 | tf_op jit(solution)/shard_map/ppermute | solution.py:32
  68.0 21.2 %all-to-all-start.2 = ((bf16[32,168,128]{2,1,0:T(8,128)(2,1)}), bf16[32,168,128]{2,1,0:T(8,128)(2,1)S(1)}, u32[]{:S(2)}, u32[]{:S(2)}) async-start(bf16[32,168,128]{2,1,0:T(8,128)(2,1)} %shard_map.151), calls=%async_computation.2 | async-start | bytes 2752512 | tf_op jit(solution)/shard_map/all_to_all | solution.py:700
  73.3 0.6 copy-start
  74.0 20.2 %copy-start.1 = (f32[192,128]{1,0:T(8,128)S(1)}, f32[192,128]{1,0:T(8,128)}, u32[]{:S(2)}) copy-start(f32[192,128]{1,0:T(8,128)} %copy-done) | copy-start | bytes 294916
  74.0 9.3 %collective-permute-start.5 = (bf16[192,128]{1,0:T(8,128)(2,1)S(1)}, bf16[192,128]{1,0:T(8,128)(2,1)S(1)}, u32[]{:S(2)}, u32[]{:S(2)}) collective-permute-start(bf16[192,128]{1,0:T(8,128)(2,1)S(1)} %get-tuple-element.105), channel_id=1, source_target_pairs={{0,1},{1,2},{2,3},{3,4},{4,5},{5,6},{6,7},{7,8},{8,9},{9,10},{10,1... | collective-permute-start | bytes 147464 | tf_op jit(solution)/shard_map/ppermute | solution.py:28
  89.2 6.8 %collective-permute-start.6 = (bf16[2880,128]{1,0:T(8,128)(2,1)S(1)}, bf16[2880,128]{1,0:T(8,128)(2,1)S(1)}, u32[]{:S(2)}, u32[]{:S(2)}) collective-permute-start(bf16[2880,128]{1,0:T(8,128)(2,1)S(1)} %slice.4), channel_id=1, source_target_pairs={{0,1},{1,0},{2,3},{3,2},{4,5},{5,4},{6,7},{7,6},{8,9},{9,8},{10,11... | collective-permute-start | bytes 2211848 | tf_op jit(solution)/shard_map/ppermute | solution.py:32
